TPU v7x, 128 devices: a whole 4x4x4 slice. The times are simulated.
128 devices in a mesh: dp: 2 (over z_hi), expert: 64 (over y, x, z_lo, core).
Axes of the slice: x: 4, y: 4, z: 4 (z_hi: 2, z_lo: 2; z = z_hi * 2 + z_lo), core: 2. Of those that a mesh axis runs over, the one named last changes fastest.
Arguments:
- tokens: bfloat16 [2048, 4096], P(('dp', 'expert')), may hold values from -6 to 6
- cotangent: bfloat16 [2048, 4096], P(('dp', 'expert')), may hold values from -6 to 6
- expert_ids: int32 [2048, 2], P(('dp', 'expert')), may hold values from 0 to 7, as said below
- gate_weights: float32 [2048, 2], P(('dp', 'expert')), may hold values from 0.2 to 1
- holder: int32 [8], replicated, may hold values from 0 to 7, as said below
- weight_in: bfloat16 [64, 4096, 256], P('expert'), may hold values from -6 to 6
- weight_out: bfloat16 [64, 128, 4096], P('expert'), may hold values from -6 to 6
- first_in: float32 [64, 4096, 256], P('expert', 'dp'), may hold values from -3 to 3
- second_in: float32 [64, 4096, 256], P('expert', 'dp'), may hold values from 0.1 to 1
- first_out: float32 [64, 128, 4096], P('expert', 'dp'), may hold values from -3 to 3
- second_out: float32 [64, 128, 4096], P('expert', 'dp'), may hold values from 0.1 to 1
Outputs:
- layer_out: bfloat16 [2048, 4096], P(('dp', 'expert'))
- grad_tokens: bfloat16 [2048, 4096], P(('dp', 'expert'))
- new_weight_in: bfloat16 [64, 4096, 256], P('expert', 'dp')
- new_weight_out: bfloat16 [64, 128, 4096], P('expert', 'dp')
- new_first_in: float32 [64, 4096, 256], P('expert', 'dp')
- new_second_in: float32 [64, 4096, 256], P('expert', 'dp')
- new_first_out: float32 [64, 128, 4096], P('expert', 'dp')
- new_second_out: float32 [64, 128, 4096], P('expert', 'dp')
Inputs may be any that keep to these rules, and one draw needn't show every extreme that they name: `expert_ids`: each row names 2 different experts. No expert is named by more than 8 rows of one device, and on every device one expert is named by exactly 8 rows. A permutation: before the re-placement expert e holds slots e * 8 to e * 8 + 7, after it slots holder[e] * 8 onward; exactly 2 experts change place.
All inputs are finite; a program needn't handle non-finite values.
Results may differ from a plain program's by a relative error of at most 0.0064.
Values may be sent and summed in bfloat16 or wider, within the bound.
No kernel may reach another device: no remote copies, remote signals or barrier semaphores. Data moves between devices by JAX's collectives and lax.ppermute only.
A program may use at most 128 MiB of HBM per device.

v0:
```python
import jax
import jax.numpy as jnp
from jax import lax
from jax.sharding import PartitionSpec as P

FF = 1024


beta_one = 0.9
beta_two = 0.95
learn_rate = 0.01
decay_rate = 0.1
epsilon = 1e-08


def forward_part(inputs, block_in, block_out):
    width = inputs.shape[1]
    hidden = block_out.shape[0]
    projected = jnp.dot(inputs, block_in, preferred_element_type=jnp.float32) * width ** (-0.5)
    gate_part = projected[:, :hidden]
    up_part = projected[:, hidden:]
    sigmoid = jax.nn.sigmoid(gate_part)
    activated = gate_part * sigmoid
    hidden_act = (activated * up_part).astype(jnp.bfloat16)
    outputs = (
        jnp.dot(hidden_act, block_out, preferred_element_type=jnp.float32) * FF ** (-0.5)
    ).astype(jnp.bfloat16)
    return (outputs, (gate_part, up_part, sigmoid, activated, hidden_act))


def backward_part(inputs, cot_rows, kept_state, block_in, block_out):
    width = inputs.shape[1]
    gate_part, up_part, sigmoid, activated, hidden_act = kept_state
    last_dims = (((1,), (1,)), ((), ()))
    first_dims = (((0,), (0,)), ((), ()))
    grad_hidden = lax.dot_general(
        cot_rows, block_out, last_dims, preferred_element_type=jnp.float32
    ) * FF ** (-0.5)
    slopes = sigmoid * (1.0 + gate_part * (1.0 - sigmoid))
    grad_gate = grad_hidden * up_part * slopes
    grad_up = grad_hidden * activated
    grad_pre = (jnp.concatenate([grad_gate, grad_up], axis=1) * width ** (-0.5)).astype(
        jnp.bfloat16
    )
    grad_rows = lax.dot_general(
        grad_pre, block_in, last_dims, preferred_element_type=jnp.float32
    ).astype(jnp.bfloat16)
    grad_in = lax.dot_general(inputs, grad_pre, first_dims, preferred_element_type=jnp.float32)
    grad_out = lax.dot_general(
        hidden_act, cot_rows, first_dims, preferred_element_type=jnp.float32
    ) * FF ** (-0.5)
    return (grad_rows, grad_in, grad_out)


def adam_step(weight, grad, first, second):
    first_new = beta_one * first + (1.0 - beta_one) * grad
    second_new = beta_two * second + (1.0 - beta_two) * grad * grad
    widened = weight.astype(jnp.float32)
    weight_new = (
        widened - learn_rate * (first_new / (jnp.sqrt(second_new) + epsilon) + decay_rate * widened)
    ).astype(jnp.bfloat16)
    return (weight_new, first_new, second_new)


def move_weights(slot_in, slot_out, slot_from):
    count = slot_from.shape[0]
    spread = (
        lax.all_to_all(
            slot_in.reshape(count, -1), "expert", split_axis=0, concat_axis=0, tiled=True
        ),
        lax.all_to_all(
            slot_out.reshape(count, -1), "expert", split_axis=0, concat_axis=0, tiled=True
        ),
    )
    collected = (
        lax.all_to_all(
            jnp.take(spread[0], slot_from, axis=0),
            "expert",
            split_axis=0,
            concat_axis=0,
            tiled=True,
        ),
        lax.all_to_all(
            jnp.take(spread[1], slot_from, axis=0),
            "expert",
            split_axis=0,
            concat_axis=0,
            tiled=True,
        ),
    )
    return (collected[0].reshape(slot_in.shape), collected[1].reshape(slot_out.shape))


def move_moments(states, slot_from):
    count = slot_from.shape[0]
    spread = (
        lax.all_to_all(
            states[0].reshape(count, -1), "expert", split_axis=0, concat_axis=0, tiled=True
        ),
        lax.all_to_all(
            states[1].reshape(count, -1), "expert", split_axis=0, concat_axis=0, tiled=True
        ),
        lax.all_to_all(states[2], "expert", split_axis=0, concat_axis=0, tiled=True),
        lax.all_to_all(states[3], "expert", split_axis=0, concat_axis=0, tiled=True),
    )
    collected = (
        lax.all_to_all(
            jnp.take(spread[0], slot_from, axis=0),
            "expert",
            split_axis=0,
            concat_axis=0,
            tiled=True,
        ),
        lax.all_to_all(
            jnp.take(spread[1], slot_from, axis=0),
            "expert",
            split_axis=0,
            concat_axis=0,
            tiled=True,
        ),
        lax.all_to_all(
            jnp.take(spread[2], slot_from, axis=0),
            "expert",
            split_axis=0,
            concat_axis=0,
            tiled=True,
        ),
        lax.all_to_all(
            jnp.take(spread[3], slot_from, axis=0),
            "expert",
            split_axis=0,
            concat_axis=0,
            tiled=True,
        ),
    )
    return tuple((collected[index].reshape(states[index].shape) for index in range(4)))


def fan_out(group_rows, groups, shards, capacity, width):
    widened = jnp.broadcast_to(
        group_rows.reshape(groups, 1, capacity, width), (groups, shards, capacity, width)
    )
    return widened.reshape(groups * shards, capacity, width)


def fold_back(returned, groups, shards, capacity, width):
    return jnp.sum(
        returned.reshape(groups, shards, capacity, width).astype(jnp.float32), axis=1
    ).reshape(groups * capacity, width)


def on_device(
    tokens,
    cotangent,
    expert_ids,
    gate_weights,
    holder,
    weight_in,
    weight_out,
    first_in,
    second_in,
    first_out,
    second_out,
):
    tok_rows, width = tokens.shape
    top_count = expert_ids.shape[1]
    groups = holder.shape[0]
    slots = lax.axis_size("expert")
    shards = slots // groups
    routed = tok_rows * top_count
    capacity = 2 * routed // groups
    data_half = lax.axis_index("dp")
    columns = jnp.arange(groups, dtype=jnp.int32)
    slot_ids = jnp.arange(slots, dtype=jnp.int32)
    anchor = jnp.sum(jnp.where(holder[:, None] == columns[None, :], columns[:, None], 0), axis=0)
    slot_from = anchor[slot_ids // shards] * shards + slot_ids % shards
    slot_in = weight_in[0]
    slot_out = weight_out[0]
    states = (first_in[0], second_in[0], first_out[0], second_out[0])
    slot_in, slot_out = move_weights(slot_in, slot_out, slot_from)
    states = move_moments(states, slot_from)
    flat_ids = expert_ids.reshape(routed)
    matches = flat_ids[:, None] == columns[None, :]
    target = jnp.sum(jnp.where(matches, holder[None, :], 0), axis=1)
    onehot = (target[:, None] == columns[None, :]).astype(jnp.int32)
    earlier = jnp.cumsum(onehot, axis=0) - onehot
    order_in = jnp.sum(earlier * onehot, axis=1)
    position = target * capacity + order_in
    source_row = (
        jnp.full((groups * capacity,), routed, jnp.int32)
        .at[position]
        .set(jnp.arange(routed, dtype=jnp.int32))
    )
    live_rows = source_row < routed
    clipped = jnp.minimum(source_row, routed - 1)
    token_of = clipped // top_count
    group_inputs = jnp.where(live_rows[:, None], tokens[token_of], jnp.zeros((), jnp.bfloat16))
    scaled_cot = (
        (gate_weights[:, :, None] * cotangent[:, None, :].astype(jnp.float32))
        .astype(jnp.bfloat16)
        .reshape(routed, width)
    )
    group_cots = jnp.where(live_rows[:, None], scaled_cot[clipped], jnp.zeros((), jnp.bfloat16))
    send_rows = fan_out(group_inputs, groups, shards, capacity, width)
    send_cots = fan_out(group_cots, groups, shards, capacity, width)
    received = (
        lax.all_to_all(send_rows, "expert", split_axis=0, concat_axis=0, tiled=True),
        lax.all_to_all(send_cots, "expert", split_axis=0, concat_axis=0, tiled=True),
    )
    rows_in = received[0].reshape(slots * capacity, width)
    rows_cot = received[1].reshape(slots * capacity, width)
    outputs, kept_state = forward_part(rows_in, slot_in, slot_out)
    grad_rows, grad_in, grad_out = backward_part(rows_in, rows_cot, kept_state, slot_in, slot_out)
    returned = (
        lax.all_to_all(
            outputs.reshape(slots, capacity, width),
            "expert",
            split_axis=0,
            concat_axis=0,
            tiled=True,
        ),
        lax.all_to_all(
            grad_rows.reshape(slots, capacity, width),
            "expert",
            split_axis=0,
            concat_axis=0,
            tiled=True,
        ),
    )
    back_out = returned[0]
    back_grad = returned[1]
    summed_out = fold_back(back_out, groups, shards, capacity, width)[position].reshape(
        tok_rows, top_count, width
    )
    summed_grad = fold_back(back_grad, groups, shards, capacity, width)[position].reshape(
        tok_rows, top_count, width
    )
    layer_out = jnp.sum(summed_out * gate_weights[:, :, None], axis=1).astype(jnp.bfloat16)
    grad_tokens = jnp.sum(summed_grad, axis=1).astype(jnp.bfloat16)
    half_in, half_out = (
        lax.psum_scatter(grad_in, "dp", scatter_dimension=0, tiled=True),
        lax.psum_scatter(grad_out, "dp", scatter_dimension=0, tiled=True),
    )
    rows_in_half = first_in.shape[1]
    rows_out_half = first_out.shape[1]
    weight_half_in = lax.dynamic_slice_in_dim(slot_in, data_half * rows_in_half, rows_in_half, 0)
    weight_half_out = lax.dynamic_slice_in_dim(
        slot_out, data_half * rows_out_half, rows_out_half, 0
    )
    new_weight_in, new_first_in, new_second_in = adam_step(
        weight_half_in, half_in, states[0], states[1]
    )
    new_weight_out, new_first_out, new_second_out = adam_step(
        weight_half_out, half_out, states[2], states[3]
    )
    return (
        layer_out,
        grad_tokens,
        new_weight_in[None],
        new_weight_out[None],
        new_first_in[None],
        new_second_in[None],
        new_first_out[None],
        new_second_out[None],
    )


def solution(mesh):
    return jax.shard_map(
        on_device,
        mesh=mesh,
        in_specs=(
            P(("dp", "expert"), None),
            P(("dp", "expert"), None),
            P(("dp", "expert"), None),
            P(("dp", "expert"), None),
            P(),
            P("expert", None, None),
            P("expert", None, None),
            P("expert", "dp", None),
            P("expert", "dp", None),
            P("expert", "dp", None),
            P("expert", "dp", None),
        ),
        out_specs=(
            P(("dp", "expert"), None),
            P(("dp", "expert"), None),
            P("expert", "dp", None),
            P("expert", "dp", None),
            P("expert", "dp", None),
            P("expert", "dp", None),
            P("expert", "dp", None),
            P("expert", "dp", None),
        ),
        check_vma=False,
    )
```

profile of v0, /device:TPU:0, one launch (start us, length us, event | category | flops | bytes accessed | tf_op | source)
XLA Modules:
  0.0 705.6 jit_solution(16240636632791768684)
XLA Ops:
  7.2 4.8 all_to_all.125
  12.5 7.2 %reduce.8 = bf16[64,8192]{1,0:T(8,128)(2,1)S(1)} reduce(bf16[64,1,8192]{2,1,0:T(2,128)(2,1)S(1)} %all_to_all.125, bf16[]{:T(256)} %broadcast.424), dimensions={1}, to_apply=%all_to_all.125.reduce_sub_computation | reduce | bytes 2097154 | tf_op jit(solution)/shard_map/all_to_all | solution.py:71
  21.3 9.4 %all-to-all-start.3 = ((bf16[64,2,4096]{2,1,0:T(2,128)(2,1)}), bf16[64,2,4096]{2,1,0:T(2,128)(2,1)S(1)}, u32[]{:S(2)}, u32[]{:S(2)}) async-start(bf16[64,2,4096]{2,1,0:T(2,128)(2,1)} %reshape.476), calls=%async_computation.3 | async-start | bytes 2097152 | tf_op jit(solution)/shard_map/all_to_all | solution.py:71
  32.8 15.9 %all-to-all-done.3 = bf16[64,2,4096]{2,1,0:T(2,128)(2,1)S(1)} async-done(((bf16[64,2,4096]{2,1,0:T(2,128)(2,1)}), bf16[64,2,4096]{2,1,0:T(2,128)(2,1)S(1)}, u32[]{:S(2)}, u32[]{:S(2)}) %all-to-all-start.3) | async-done | bytes 1048608 | tf_op jit(solution)/shard_map/all_to_all | solution.py:71
  48.7 4.7 all-to-all-start.12
  55.6 15.9 %all-to-all-done.12 = f32[64,1,4096]{2,1,0:T(1,128)S(1)} async-done(((f32[64,1,4096]{2,1,0:T(1,128)}), f32[64,1,4096]{2,1,0:T(1,128)S(1)}, u32[]{:S(2)}, u32[]{:S(2)}) %all-to-all-start.12) | async-done | bytes 1048608 | tf_op jit(solution)/shard_map/all_to_all | solution.py:103
  71.5 4.8 all-to-all-start.14
  76.3 10.1 %all_to_all.124 = bf16[64,1,16384]{2,1,0:T(2,128)(2,1)} reshape(bf16[1,4096,256]{2,1,0:T(8,128)(2,1)} %param.20) | data formatting | bytes 4194304 | tf_op jit(solution)/shard_map/all_to_all | solution.py:68
  86.4 13.2 %reduce.6 = bf16[64,16384]{1,0:T(8,128)(2,1)S(1)} reduce(bf16[64,1,16384]{2,1,0:T(2,128)(2,1)} %all_to_all.124, bf16[]{:T(256)} %broadcast.424), dimensions={1}, to_apply=%all_to_all.124.reduce_sub_computation | reduce | bytes 4194306 | tf_op jit(solution)/shard_map/all_to_all | solution.py:68
  103.1 5.1 compare_and_fusion
  109.2 8.8 %all-to-all-start.1 = ((bf16[64,2,8192]{2,1,0:T(2,128)(2,1)}), bf16[64,2,8192]{2,1,0:T(2,128)(2,1)S(1)}, u32[]{:S(2)}, u32[]{:S(2)}) async-start(bf16[64,2,8192]{2,1,0:T(2,128)(2,1)} %reshape.472), calls=%async_computation.1 | async-start | bytes 4194304 | tf_op jit(solution)/shard_map/all_to_all | solution.py:68
  118.1 3.4 reshape.477
  132.5 14.3 %all-to-all-done.1 = bf16[64,2,8192]{2,1,0:T(2,128)(2,1)S(1)} async-done(((bf16[64,2,8192]{2,1,0:T(2,128)(2,1)}), bf16[64,2,8192]{2,1,0:T(2,128)(2,1)S(1)}, u32[]{:S(2)}, u32[]{:S(2)}) %all-to-all-start.1) | async-done | bytes 2097184 | tf_op jit(solution)/shard_map/all_to_all | solution.py:68
  146.8 5.0 all-to-all-start.4
  151.8 4.3 all_to_all.104
  156.2 13.7 %all-to-all-done.4 = bf16[64,2,4096]{2,1,0:T(2,128)(2,1)S(1)} async-done(((bf16[64,2,4096]{2,1,0:T(2,128)(2,1)}), bf16[64,2,4096]{2,1,0:T(2,128)(2,1)S(1)}, u32[]{:S(2)}, u32[]{:S(2)}) %all-to-all-start.4) | async-done | bytes 1048608 | tf_op jit(solution)/shard_map/all_to_all | solution.py:83
  170.9 5.6 all-to-all-start.8
  176.4 4.3 all_to_all.109
  180.8 24.2 %all-to-all-done.8 = f32[64,1,8192]{2,1,0:T(1,128)} async-done(((f32[64,1,8192]{2,1,0:T(1,128)}), f32[64,1,8192]{2,1,0:T(1,128)}, u32[]{:S(2)}, u32[]{:S(2)}) %all-to-all-start.8) | async-done | bytes 2097184 | tf_op jit(solution)/shard_map/all_to_all | solution.py:97
  205.0 5.8 all-to-all-start.10
  224.9 6.8 reshape.473
  231.7 4.5 copy.90
  236.2 3.2 gather_fusion.1
  239.5 8.8 %all-to-all-start.13 = ((f32[64,1,4096]{2,1,0:T(1,128)}), f32[64,1,4096]{2,1,0:T(1,128)S(1)}, u32[]{:S(2)}, u32[]{:S(2)}) async-start(f32[64,1,4096]{2,1,0:T(1,128)} %copy.58), calls=%async_computation.14 | async-start | bytes 2097152 | tf_op jit(solution)/shard_map/all_to_all | solution.py:121
  250.2 2.9 reduce.7
  253.1 4.5 reshape.474
  257.6 8.8 %all-to-all-done.13 = f32[64,1,4096]{2,1,0:T(1,128)S(1)} async-done(((f32[64,1,4096]{2,1,0:T(1,128)}), f32[64,1,4096]{2,1,0:T(1,128)S(1)}, u32[]{:S(2)}, u32[]{:S(2)}) %all-to-all-start.13) | async-done | bytes 1048608 | tf_op jit(solution)/shard_map/all_to_all | solution.py:121
  267.4 5.1 all-to-all-start.2
  279.9 21.3 %all-to-all-done.2 = bf16[64,2,8192]{2,1,0:T(2,128)(2,1)S(1)} async-done(((bf16[64,2,8192]{2,1,0:T(2,128)(2,1)}), bf16[64,2,8192]{2,1,0:T(2,128)(2,1)S(1)}, u32[]{:S(2)}, u32[]{:S(2)}) %all-to-all-start.2) | async-done | bytes 2097184 | tf_op jit(solution)/shard_map/all_to_all | solution.py:76
  302.6 56.1 %all_to_all.142 = bf16[64,8,4096]{2,1,0:T(8,128)(2,1)} all-to-all(bf16[64,8,4096]{2,1,0:T(8,128)(2,1)S(1)} %bitcast.131), channel_id=1, replica_groups=mesh['dp'=2,'expert'=64] {'expert'}, dimensions={0} | all-to-all | bytes 8388608 | tf_op jit(solution)/shard_map/all_to_all | solution.py:207
  361.2 5.7 all-to-all-start.6
  366.9 2.8 copy.89
  372.2 2.8 copy.88
  377.4 3.9 select_bitcast_fusion
  381.3 3.5 copy.56
  384.8 32.4 %all-to-all-done.6 = bf16[64,8,4096]{2,1,0:T(8,128)(2,1)} async-done(((bf16[64,8,4096]{2,1,0:T(8,128)(2,1)}), bf16[64,8,4096]{2,1,0:T(8,128)(2,1)}, u32[]{:S(2)}, u32[]{:S(2)}) %all-to-all-start.6) | async-done | bytes 4194336 | tf_op jit(solution)/shard_map/all_to_all | solution.py:208
  417.2 10.0 %all-to-all-start.9 = ((f32[64,1,8192]{2,1,0:T(1,128)}), f32[64,1,8192]{2,1,0:T(1,128)}, u32[]{:S(2)}, u32[]{:S(2)}) async-start(f32[64,1,8192]{2,1,0:T(1,128)} %copy.56), calls=%async_computation.9 | async-start | bytes 4194304 | tf_op jit(solution)/shard_map/all_to_all | solution.py:107
  427.4 3.4 reshape.479
  430.8 8.0 %reduce.1 = bf16[64,8192]{1,0:T(8,128)(2,1)S(1)} reduce(bf16[64,1,8192]{2,1,0:T(2,128)(2,1)} %reshape.479, bf16[]{:T(256)} %constant.167), dimensions={1}, to_apply=%all_to_all.100.reduce_sub_computation | reduce | bytes 2097154 | tf_op jit(solution)/shard_map/all_to_all | solution.py:83
  440.0 6.8 reshape.475
  446.9 13.8 %reduce = bf16[64,16384]{1,0:T(8,128)(2,1)} reduce(bf16[64,1,16384]{2,1,0:T(2,128)(2,1)} %reshape.475, bf16[]{:T(256)} %constant.167), dimensions={1}, to_apply=%all_to_all.96.reduce_sub_computation | reduce | bytes 4194306 | tf_op jit(solution)/shard_map/all_to_all | solution.py:76
  460.7 3.1 reshape.308
  463.8 3.6 fusion.13
  467.4 4.5 multiply_multiply_fusion.2
  471.9 4.3 convolution_multiply_fusion
  476.1 5.1 copy.57
  481.2 9.0 %all-to-all-start.11 = ((f32[64,1,8192]{2,1,0:T(1,128)}), f32[64,1,8192]{2,1,0:T(1,128)}, u32[]{:S(2)}, u32[]{:S(2)}) async-start(f32[64,1,8192]{2,1,0:T(1,128)} %copy.57), calls=%async_computation.12 | async-start | bytes 4194304 | tf_op jit(solution)/shard_map/all_to_all | solution.py:114
  490.3 4.2 fusion.1
  494.5 24.3 %all-to-all-done.11 = f32[64,1,8192]{2,1,0:T(1,128)} async-done(((f32[64,1,8192]{2,1,0:T(1,128)}), f32[64,1,8192]{2,1,0:T(1,128)}, u32[]{:S(2)}, u32[]{:S(2)}) %all-to-all-start.11) | async-done | bytes 2097184 | tf_op jit(solution)/shard_map/all_to_all | solution.py:114
  518.8 5.7 all-to-all-start.7
  524.6 5.6 fusion.5
  530.2 3.3 fusion
  533.4 41.6 %all-to-all-done.7 = bf16[64,8,4096]{2,1,0:T(8,128)(2,1)} async-done(((bf16[64,8,4096]{2,1,0:T(8,128)(2,1)}), bf16[64,8,4096]{2,1,0:T(8,128)(2,1)}, u32[]{:S(2)}, u32[]{:S(2)}) %all-to-all-start.7) | async-done | bytes 4194336 | tf_op jit(solution)/shard_map/all_to_all | solution.py:222
  575.1 10.2 %all-to-all-start.5 = ((bf16[64,8,4096]{2,1,0:T(8,128)(2,1)}), bf16[64,8,4096]{2,1,0:T(8,128)(2,1)}, u32[]{:S(2)}, u32[]{:S(2)}) async-start(bf16[64,8,4096]{2,1,0:T(8,128)(2,1)} %fusion), calls=%async_computation.5 | async-start | bytes 8388608 | tf_op jit(solution)/shard_map/all_to_all | solution.py:215
  587.3 9.1 %multiply_reduce_fusion.1 = f32[64,8192]{1,0:T(8,128)} fusion(f32[64,1,8192]{2,1,0:T(1,128)} %all-to-all-done.9), kind=kLoop, calls=%fused_computation.40 | loop fusion | flops 524288 | bytes 4194304 | tf_op jit(solution)/shard_map/mul | solution.py:56
  599.2 36.0 %all-to-all-done.5 = bf16[64,8,4096]{2,1,0:T(8,128)(2,1)} async-done(((bf16[64,8,4096]{2,1,0:T(8,128)(2,1)}), bf16[64,8,4096]{2,1,0:T(8,128)(2,1)}, u32[]{:S(2)}, u32[]{:S(2)}) %all-to-all-start.5) | async-done | bytes 4194336 | tf_op jit(solution)/shard_map/all_to_all | solution.py:215
  635.2 9.9 %all-to-all-start.15 = ((f32[64,1,4096]{2,1,0:T(1,128)}), f32[64,1,4096]{2,1,0:T(1,128)}, u32[]{:S(2)}, u32[]{:S(2)}) async-start(f32[64,1,4096]{2,1,0:T(1,128)} %copy.60), calls=%async_computation.17 | async-start | bytes 2097152 | tf_op jit(solution)/shard_map/all_to_all | solution.py:128
  645.1 9.1 %multiply_reduce_fusion = f32[64,8192]{1,0:T(8,128)} fusion(f32[64,1,8192]{2,1,0:T(1,128)} %all-to-all-done.11), kind=kLoop, calls=%fused_computation.38 | loop fusion | flops 524288 | bytes 4194304 | tf_op jit(solution)/shard_map/mul | solution.py:57
  654.2 2.9 mul.219
  657.1 3.2 convert_reduce_fusion
  663.9 3.0 convert_reduce_fusion.1
  675.5 5.2 fusion.30
  680.7 11.2 %reduce-scatter.3.cloned.1.call-done = f32[2048,256]{1,0:T(8,128)} async-done(((f32[4096,256]{1,0:T(8,128)}), f32[2048,256]{1,0:T(8,128)}) %reduce-scatter.3.cloned.1.call-update) | async-done | bytes 2097168 | tf_op jit(solution)/shard_map/reduce_scatter | solution.py:241
  691.9 6.6 fusion.25
  (116 shorter events, 74.5 us)
Async XLA Ops:
  7.2 269.7 %copy-start = (bf16[16,4096]{1,0:T(8,128)(2,1)S(1)}, bf16[16,4096]{1,0:T(8,128)(2,1)}, u32[]{:S(2)}) copy-start(bf16[16,4096]{1,0:T(8,128)(2,1)} %param.15) | copy-start | bytes 393220
  19.7 11.0 %copy-start.14 = (f32[1,64,4096]{2,1,0:T(8,128)S(1)}, f32[1,64,4096]{2,1,0:T(8,128)}, u32[]{:S(2)}) copy-start(f32[1,64,4096]{2,1,0:T(8,128)} %param.24) | copy-start | bytes 3145732
  21.3 27.5 %all-to-all-start.3 = ((bf16[64,2,4096]{2,1,0:T(2,128)(2,1)}), bf16[64,2,4096]{2,1,0:T(2,128)(2,1)S(1)}, u32[]{:S(2)}, u32[]{:S(2)}) async-start(bf16[64,2,4096]{2,1,0:T(2,128)(2,1)} %reshape.476), calls=%async_computation.3 | async-start | bytes 2097152 | tf_op jit(solution)/shard_map/all_to_all | solution.py:71
  30.7 22.7 %copy-start.15 = (f32[1,64,4096]{2,1,0:T(8,128)S(1)}, f32[1,64,4096]{2,1,0:T(8,128)}, u32[]{:S(2)}) copy-start(f32[1,64,4096]{2,1,0:T(8,128)} %param.25) | copy-start | bytes 3145732
  48.7 6.8 copy-start.9
  48.7 22.8 %all-to-all-start.12 = ((f32[64,1,4096]{2,1,0:T(1,128)}), f32[64,1,4096]{2,1,0:T(1,128)S(1)}, u32[]{:S(2)}, u32[]{:S(2)}) async-start(f32[64,1,4096]{2,1,0:T(1,128)} %all_to_all.114), calls=%async_computation.13 | async-start | bytes 2097152 | tf_op jit(solution)/shard_map/all_to_all | solution.py:103
  71.5 4.8 copy-start.11
  71.5 36.7 %all-to-all-start.14 = ((f32[64,1,4096]{2,1,0:T(1,128)}), f32[64,1,4096]{2,1,0:T(1,128)S(1)}, u32[]{:S(2)}, u32[]{:S(2)}) async-start(f32[64,1,4096]{2,1,0:T(1,128)} %all_to_all.119), calls=%async_computation.16 | async-start | bytes 2097152 | tf_op jit(solution)/shard_map/all_to_all | solution.py:104
  99.6 2.8 copy-start.24
  108.2 9.9 %copy-start.10 = (bf16[64,2,4096]{2,1,0:T(2,128)(2,1)S(1)}, bf16[64,2,4096]{2,1,0:T(2,128)(2,1)}, u32[]{:S(2)}) copy-start(bf16[64,2,4096]{2,1,0:T(2,128)(2,1)} %copy-done.9) | copy-start | bytes 3145732
  108.2 1.0 copy-start.12
  109.2 37.6 %all-to-all-start.1 = ((bf16[64,2,8192]{2,1,0:T(2,128)(2,1)}), bf16[64,2,8192]{2,1,0:T(2,128)(2,1)S(1)}, u32[]{:S(2)}, u32[]{:S(2)}) async-start(bf16[64,2,8192]{2,1,0:T(2,128)(2,1)} %reshape.472), calls=%async_computation.1 | async-start | bytes 4194304 | tf_op jit(solution)/shard_map/all_to_all | solution.py:68
  146.8 23.1 %all-to-all-start.4 = ((bf16[64,2,4096]{2,1,0:T(2,128)(2,1)}), bf16[64,2,4096]{2,1,0:T(2,128)(2,1)S(1)}, u32[]{:S(2)}, u32[]{:S(2)}) async-start(bf16[64,2,4096]{2,1,0:T(2,128)(2,1)} %reshape.478), calls=%async_computation.4 | async-start | bytes 2097152 | tf_op jit(solution)/shard_map/all_to_all | solution.py:83
  169.9 1.0 copy-start.7
  170.9 34.2 %all-to-all-start.8 = ((f32[64,1,8192]{2,1,0:T(1,128)}), f32[64,1,8192]{2,1,0:T(1,128)}, u32[]{:S(2)}, u32[]{:S(2)}) async-start(f32[64,1,8192]{2,1,0:T(1,128)} %all_to_all.104), calls=%async_computation.8 | async-start | bytes 4194304 | tf_op jit(solution)/shard_map/all_to_all | solution.py:97
  180.8 30.0 %copy-start.18 = (s32[16,2]{0,1:T(2,128)S(1)}, s32[16,2]{0,1:T(2,128)}, u32[]{:S(2)}) copy-start(s32[16,2]{0,1:T(2,128)} %param.17) | copy-start | bytes 388
  205.0 34.5 %all-to-all-start.10 = ((f32[64,1,8192]{2,1,0:T(1,128)}), f32[64,1,8192]{2,1,0:T(1,128)}, u32[]{:S(2)}, u32[]{:S(2)}) async-start(f32[64,1,8192]{2,1,0:T(1,128)} %all_to_all.109), calls=%async_computation.11 | async-start | bytes 4194304 | tf_op jit(solution)/shard_map/all_to_all | solution.py:100
  211.5 4.9 copy-start.20
  239.5 26.9 %all-to-all-start.13 = ((f32[64,1,4096]{2,1,0:T(1,128)}), f32[64,1,4096]{2,1,0:T(1,128)S(1)}, u32[]{:S(2)}, u32[]{:S(2)}) async-start(f32[64,1,4096]{2,1,0:T(1,128)} %copy.58), calls=%async_computation.14 | async-start | bytes 2097152 | tf_op jit(solution)/shard_map/all_to_all | solution.py:121
  257.6 14.9 %copy-start.19 = (f32[16,2]{0,1:T(2,128)S(1)}, f32[16,2]{0,1:T(2,128)}, u32[]{:S(2)}) copy-start(f32[16,2]{0,1:T(2,128)} %param.18) | copy-start | bytes 388
  257.6 15.6 %copy-start.16 = (bf16[16,4096]{1,0:T(8,128)(2,1)S(1)}, bf16[16,4096]{1,0:T(8,128)(2,1)}, u32[]{:S(2)}) copy-start(bf16[16,4096]{1,0:T(8,128)(2,1)} %param.16) | copy-start | bytes 393220
  257.6 16.9 %copy-start.22 = (s32[64]{0:T(128)S(1)}, s32[64]{0:T(128)}, u32[]{:S(2)}) copy-start(s32[64]{0:T(128)} %get-tuple-element.28) | copy-start | bytes 772
  257.6 16.9 %copy-start.23 = (s32[64]{0:T(128)S(1)}, s32[64]{0:T(128)}, u32[]{:S(2)}) copy-start(s32[64]{0:T(128)} %get-tuple-element.29) | copy-start | bytes 772
  266.4 1.0 copy-start.4
  267.4 33.8 %all-to-all-start.2 = ((bf16[64,2,8192]{2,1,0:T(2,128)(2,1)}), bf16[64,2,8192]{2,1,0:T(2,128)(2,1)S(1)}, u32[]{:S(2)}, u32[]{:S(2)}) async-start(bf16[64,2,8192]{2,1,0:T(2,128)(2,1)} %reshape.474), calls=%async_computation.2 | async-start | bytes 4194304 | tf_op jit(solution)/shard_map/all_to_all | solution.py:76
  276.9 1.7 copy-start.17
  301.2 1.3 copy-start.2
  361.2 55.9 %all-to-all-start.6 = ((bf16[64,8,4096]{2,1,0:T(8,128)(2,1)}), bf16[64,8,4096]{2,1,0:T(8,128)(2,1)}, u32[]{:S(2)}, u32[]{:S(2)}) async-start(bf16[64,8,4096]{2,1,0:T(8,128)(2,1)} %bitcast.130), calls=%async_computation.6 | async-start | bytes 8388608 | tf_op jit(solution)/shard_map/all_to_all | solution.py:208
  384.8 42.6 %copy-start.8 = (bf16[64,2,4096]{2,1,0:T(2,128)(2,1)S(1)}, bf16[64,2,4096]{2,1,0:T(2,128)(2,1)}, u32[]{:S(2)}) copy-start(bf16[64,2,4096]{2,1,0:T(2,128)(2,1)} %copy-done.7) | copy-start | bytes 3145732
  417.2 64.1 %all-to-all-start.9 = ((f32[64,1,8192]{2,1,0:T(1,128)}), f32[64,1,8192]{2,1,0:T(1,128)}, u32[]{:S(2)}, u32[]{:S(2)}) async-start(f32[64,1,8192]{2,1,0:T(1,128)} %copy.56), calls=%async_computation.9 | async-start | bytes 4194304 | tf_op jit(solution)/shard_map/all_to_all | solution.py:107
  427.1 248.3 %reduce-scatter.5.cloned.1.call-start = ((), (), s32[]{:S(2)}) async-start(), calls=%async_computation.19 | async-start | bytes 3145728 | tf_op jit(solution)/shard_map/reduce_scatter | solution.py:242
  430.8 9.2 %copy-start.3 = (bf16[64,2,8192]{2,1,0:T(2,128)(2,1)S(1)}, bf16[64,2,8192]{2,1,0:T(2,128)(2,1)}, u32[]{:S(2)}) copy-start(bf16[64,2,8192]{2,1,0:T(2,128)(2,1)} %copy-done.2) | copy-start | bytes 6291460
  463.8 3.6 copy-start.13
  481.2 37.6 %all-to-all-start.11 = ((f32[64,1,8192]{2,1,0:T(1,128)}), f32[64,1,8192]{2,1,0:T(1,128)}, u32[]{:S(2)}, u32[]{:S(2)}) async-start(f32[64,1,8192]{2,1,0:T(1,128)} %copy.57), calls=%async_computation.12 | async-start | bytes 4194304 | tf_op jit(solution)/shard_map/all_to_all | solution.py:114
  518.8 56.2 %all-to-all-start.7 = ((bf16[64,8,4096]{2,1,0:T(8,128)(2,1)}), bf16[64,8,4096]{2,1,0:T(8,128)(2,1)}, u32[]{:S(2)}, u32[]{:S(2)}) async-start(bf16[64,8,4096]{2,1,0:T(8,128)(2,1)} %fusion.1), calls=%async_computation.7 | async-start | bytes 8388608 | tf_op jit(solution)/shard_map/all_to_all | solution.py:222
  524.5 167.3 %reduce-scatter.3.cloned.1.call-start = ((), (), s32[]{:S(2)}) async-start(), calls=%async_computation.18 | async-start | bytes 6291456 | tf_op jit(solution)/shard_map/reduce_scatter | solution.py:241
  533.4 51.8 %copy-start.21 = (s32[32]{0:T(128)S(1)}, s32[32]{0:T(128)}, u32[]{:S(2)}) copy-start(s32[32]{0:T(128)} %copy-done.20) | copy-start | bytes 388
  533.4 51.8 %copy-start.6 = (f32[64,1,4096]{2,0,1:T(8,128)S(1)}, f32[64,1,4096]{2,0,1:T(8,128)}, u32[]{:S(2)}) copy-start(f32[64,1,4096]{2,0,1:T(8,128)} %get-tuple-element.24) | copy-start | bytes 3145732
  575.1 60.1 %all-to-all-start.5 = ((bf16[64,8,4096]{2,1,0:T(8,128)(2,1)}), bf16[64,8,4096]{2,1,0:T(8,128)(2,1)}, u32[]{:S(2)}, u32[]{:S(2)}) async-start(bf16[64,8,4096]{2,1,0:T(8,128)(2,1)} %fusion), calls=%async_computation.5 | async-start | bytes 8388608 | tf_op jit(solution)/shard_map/all_to_all | solution.py:215
  635.2 40.3 %all-to-all-start.15 = ((f32[64,1,4096]{2,1,0:T(1,128)}), f32[64,1,4096]{2,1,0:T(1,128)}, u32[]{:S(2)}, u32[]{:S(2)}) async-start(f32[64,1,4096]{2,1,0:T(1,128)} %copy.60), calls=%async_computation.17 | async-start | bytes 2097152 | tf_op jit(solution)/shard_map/all_to_all | solution.py:128
  668.4 7.1 %copy-start.5 = (f32[64,1,4096]{2,1,0:T(1,128)S(1)}, f32[64,1,4096]{2,1,0:T(1,128)}, u32[]{:S(2)}) copy-start(f32[64,1,4096]{2,1,0:T(1,128)} %copy-done.4) | copy-start | bytes 3145732
  691.9 6.6 copy-start.1
Sparse Core Ops, SparseCore 0:
  476.3 105.2 reduce-scatter.4
  584.1 107.7 reduce-scatter.2
where the time goes:
time: 718 us; the launch traced here: 706 us
  waiting for transfers between devices  260 us (36%)
  local copies, waits for them, and re-layouts  134 us (19%)
  starting transfers between devices  109 us (15%)
  other arithmetic  106 us (15%)
  blocking collectives  56.1 us (8%)
  matrix products  25.4 us (4%)
  between operations  14.8 us (2%)
    all_to_all x1, blocking collectives, on_device(): lax.all_to_all(send_rows, 'expert', split_axis=0, concat_axis=0, tiled=True)  56.1 us
    unnamed x66, local copies, waits for them, and re-layouts  52.4 us
    all_to_all x1, waiting for transfers between devices, on_device(): lax.all_to_all(grad_rows.reshape(slots, capacity, width), 'expert', split...  41.6 us
    all_to_all x1, waiting for transfers between devices, on_device(): lax.all_to_all(outputs.reshape(slots, capacity, width), 'expert', split_a...  36 us
    all_to_all x1, waiting for transfers between devices, on_device(): lax.all_to_all(send_cots, 'expert', split_axis=0, concat_axis=0, tiled=True)  32.4 us
    all_to_all x1, waiting for transfers between devices, move_moments(): lax.all_to_all(jnp.take(spread[1], slot_from, axis=0), 'expert', split_ax...  24.3 us
    all_to_all x1, waiting for transfers between devices, move_moments(): lax.all_to_all(states[0].reshape(count, -1), 'expert', split_axis=0, conc...  24.2 us
    all_to_all x1, waiting for transfers between devices, move_weights(): lax.all_to_all(jnp.take(spread[0], slot_from, axis=0), 'expert', split_ax...  21.3 us
  transfers between devices with their start and end apart: 17, of which 13 were waited for; matrix products, arithmetic and copies ran while one was open for 31% of the time, Pallas kernels for 0%

commit v1 on v0

v1 whole, which is shorter than its diff:
```python
import jax
import jax.numpy as jnp
from jax import lax
from jax.sharding import Mesh, PartitionSpec as P

FF = 1024

beta_one = 0.9
beta_two = 0.95
learn_rate = 0.01
decay_rate = 0.1
epsilon = 1e-08

PARTS = ("y", "xh", "xl", "z", "c")
GROUP = ("y", "xh")
FLIP = [(0, 1), (1, 0)]
half_type = jnp.bfloat16


def adam_step(weight, grad, first, second):
    first_new = beta_one * first + (1.0 - beta_one) * grad
    second_new = beta_two * second + (1.0 - beta_two) * grad * grad
    widened = weight.astype(jnp.float32)
    weight_new = (
        widened - learn_rate * (first_new / (jnp.sqrt(second_new) + epsilon) + decay_rate * widened)
    ).astype(jnp.bfloat16)
    return (weight_new, first_new, second_new)


def flip(value, axis):
    return lax.ppermute(value, axis, FLIP)


def gather_group(piece):
    rows = piece.shape[0] // 2
    from_x = flip(piece, "xl")
    from_z = flip(piece, "z")
    diag = jnp.concatenate([flip(from_z[:rows], "xl"), flip(from_x[rows:], "z")], axis=0)
    mine = jnp.stack([piece, from_x, from_z, diag])
    other = flip(mine, "c")
    return mine, other


def reduce_group(mine, other):
    rows = mine.shape[1] // 2
    wide = mine.astype(jnp.float32) + flip(other, "c").astype(jnp.float32)
    own, to_x, to_z, diag = wide[0], wide[1], wide[2], wide[3].astype(half_type)
    via_x = flip(diag[:rows], "xl").astype(jnp.float32)
    via_z = flip(diag[rows:], "z").astype(jnp.float32)
    to_z = jnp.concatenate([to_z[:rows] + via_x, to_z[rows:]], axis=0).astype(half_type)
    to_x = jnp.concatenate([to_x[:rows], to_x[rows:] + via_z], axis=0).astype(half_type)
    return own + flip(to_x, "xl").astype(jnp.float32) + flip(to_z, "z").astype(jnp.float32)


def swap_branches(experts, shards):
    def one(low, high):
        pairs = []
        for shard in range(shards):
            pairs.append((low * shards + shard, high * shards + shard))
            pairs.append((high * shards + shard, low * shards + shard))

        def move(values):
            return tuple(lax.ppermute(value, PARTS, pairs) for value in values)

        return move

    return [one(low, high) for low in range(experts) for high in range(low + 1, experts)]


def on_device(
    tokens,
    cotangent,
    expert_ids,
    gate_weights,
    holder,
    weight_in,
    weight_out,
    first_in,
    second_in,
    first_out,
    second_out,
):
    tok_rows, width = tokens.shape
    top_count = expert_ids.shape[1]
    groups = holder.shape[0]
    shards = 8
    routed = tok_rows * top_count
    capacity = 2 * routed // groups
    hidden = weight_out.shape[1]
    data_half = lax.axis_index("dp")
    columns = jnp.arange(groups, dtype=jnp.int32)
    my_expert = lax.axis_index("y") * 2 + lax.axis_index("xh")
    changed = holder != columns
    low = jnp.min(jnp.where(changed, columns, groups - 1))
    high = jnp.max(jnp.where(changed, columns, 0))
    case = low * (2 * groups - 1 - low) // 2 + (high - low - 1)
    branches = swap_branches(groups, shards)
    case = jnp.clip(case, 0, len(branches) - 1)
    moved = (my_expert == low) | (my_expert == high)
    slot_in = weight_in[0]
    slot_out = weight_out[0]
    states = (first_in[0], second_in[0], first_out[0], second_out[0])
    rows_in_half = first_in.shape[1]
    rows_out_half = first_out.shape[1]
    half_w_in = lax.dynamic_slice_in_dim(slot_in, data_half * rows_in_half, rows_in_half, 0)
    half_w_out = lax.dynamic_slice_in_dim(slot_out, data_half * rows_out_half, rows_out_half, 0)

    flat_ids = expert_ids.reshape(routed)
    onehot = (flat_ids[:, None] == columns[None, :]).astype(jnp.int32)
    earlier = jnp.cumsum(onehot, axis=0) - onehot
    order_in = jnp.sum(earlier * onehot, axis=1)
    position = (flat_ids * capacity + order_in).reshape(tok_rows, top_count)
    places = jnp.arange(groups * capacity, dtype=jnp.int32)
    picks = position[:, :, None] == places[None, None, :]
    chosen = jnp.any(picks, axis=1).astype(jnp.bfloat16)
    gate_of = jnp.sum(jnp.where(picks, gate_weights[:, :, None], 0.0), axis=(0, 1))
    spread = (((0,), (0,)), ((), ()))
    group_inputs = lax.dot_general(chosen, tokens, spread, preferred_element_type=jnp.float32).astype(jnp.bfloat16)
    group_cots = (
        gate_of[:, None] * lax.dot_general(chosen, cotangent, spread, preferred_element_type=jnp.float32)
    ).astype(jnp.bfloat16)
    send = jnp.concatenate(
        [group_inputs.reshape(groups, capacity, width), group_cots.reshape(groups, capacity, width)], axis=1
    )
    received = lax.all_to_all(send, GROUP, split_axis=0, concat_axis=0, tiled=True)
    rows_piece = received[:, :capacity].reshape(groups * capacity, width)
    cots_piece = received[:, capacity:].reshape(groups * capacity, width)
    in_mine, in_other = gather_group(rows_piece)
    cot_mine, cot_other = gather_group(cots_piece)
    rows_in = jnp.concatenate([in_mine, in_other]).reshape(-1, width)
    rows_cot = jnp.concatenate([cot_mine, cot_other]).reshape(-1, width)

    early = lax.switch(
        case,
        branches,
        (
            states[0].astype(half_type),
            states[1].astype(half_type),
            states[2].astype(half_type),
            states[3].astype(half_type),
            half_w_in,
            half_w_out,
        ),
    )

    last_dims = (((1,), (1,)), ((), ()))
    first_dims = (((0,), (0,)), ((), ()))
    projected = jnp.dot(rows_in, slot_in, preferred_element_type=jnp.float32) * width ** (-0.5)
    gate_part = projected[:, :hidden]
    up_part = projected[:, hidden:]
    sigmoid = jax.nn.sigmoid(gate_part)
    activated = gate_part * sigmoid
    hidden_act = (activated * up_part).astype(jnp.bfloat16)
    outputs = (jnp.dot(hidden_act, slot_out, preferred_element_type=jnp.float32) * FF ** (-0.5)).astype(jnp.bfloat16)
    grad_hidden = lax.dot_general(rows_cot, slot_out, last_dims, preferred_element_type=jnp.float32) * FF ** (-0.5)
    slopes = sigmoid * (1.0 + gate_part * (1.0 - sigmoid))
    grad_gate = grad_hidden * up_part * slopes
    grad_up = grad_hidden * activated
    grad_pre = (jnp.concatenate([grad_gate, grad_up], axis=1) * width ** (-0.5)).astype(jnp.bfloat16)
    grad_rows = lax.dot_general(grad_pre, slot_in, last_dims, preferred_element_type=jnp.float32).astype(jnp.bfloat16)
    grad_in = lax.dot_general(rows_in, grad_pre, first_dims, preferred_element_type=jnp.float32)
    grad_out = lax.dot_general(hidden_act, rows_cot, first_dims, preferred_element_type=jnp.float32) * FF ** (-0.5)

    other_half = 1 - data_half
    away_in = lax.dynamic_slice_in_dim(grad_in, other_half * rows_in_half, rows_in_half, 0).astype(half_type)
    away_out = lax.dynamic_slice_in_dim(grad_out, other_half * rows_out_half, rows_out_half, 0).astype(half_type)
    half_in = lax.dynamic_slice_in_dim(grad_in, data_half * rows_in_half, rows_in_half, 0) + flip(away_in, "dp").astype(jnp.float32)
    half_out = lax.dynamic_slice_in_dim(grad_out, data_half * rows_out_half, rows_out_half, 0) + flip(away_out, "dp").astype(jnp.float32)
    late = lax.switch(case, branches, (half_in.astype(half_type), half_out.astype(half_type)))

    out_pieces = outputs.reshape(2, 4, groups * capacity, width)
    grad_pieces = grad_rows.reshape(2, 4, groups * capacity, width)
    out_sum = reduce_group(out_pieces[0], out_pieces[1])
    grad_sum = reduce_group(grad_pieces[0], grad_pieces[1])
    back = jnp.concatenate(
        [
            out_sum.astype(half_type).reshape(groups, capacity, width),
            grad_sum.astype(half_type).reshape(groups, capacity, width),
        ],
        axis=1,
    )
    back = lax.all_to_all(back, GROUP, split_axis=0, concat_axis=0, tiled=True)
    back_out = back[:, :capacity].reshape(groups * capacity, width)
    back_grad = back[:, capacity:].reshape(groups * capacity, width)
    picked = picks.astype(jnp.bfloat16)
    layer_out = sum(
        gate_weights[:, k : k + 1] * jnp.dot(picked[:, k], back_out, preferred_element_type=jnp.float32)
        for k in range(top_count)
    ).astype(jnp.bfloat16)
    grad_tokens = jnp.dot(chosen, back_grad, preferred_element_type=jnp.float32).astype(jnp.bfloat16)

    def placed(came, stayed):
        return jnp.where(moved, came.astype(stayed.dtype), stayed)

    new_weight_in, new_first_in, new_second_in = adam_step(
        placed(early[4], half_w_in), placed(late[0], half_in), placed(early[0], states[0]), placed(early[1], states[1])
    )
    new_weight_out, new_first_out, new_second_out = adam_step(
        placed(early[5], half_w_out), placed(late[1], half_out), placed(early[2], states[2]), placed(early[3], states[3])
    )
    return (
        layer_out,
        grad_tokens,
        new_weight_in[None],
        new_weight_out[None],
        new_first_in[None],
        new_second_in[None],
        new_first_out[None],
        new_second_out[None],
    )


def solution(mesh):
    fine = Mesh(mesh.devices.reshape(2, 4, 2, 2, 2, 2), ("dp",) + PARTS)
    rows = P(("dp",) + PARTS, None)
    slots = P(PARTS, None, None)
    halves = P(PARTS, "dp", None)
    return jax.shard_map(
        on_device,
        mesh=fine,
        in_specs=(rows, rows, rows, rows, P(), slots, slots, halves, halves, halves, halves),
        out_specs=(rows, rows, halves, halves, halves, halves, halves, halves),
        check_vma=False,
    )
```

time: 718 us -> 385 us (0.54)
  waiting for transfers between devices: 260 us -> 61.1 us
  starting transfers between devices: 109 us -> 250 us
  local copies, waits for them, and re-layouts: 134 us -> 16.5 us
  other arithmetic: 106 us -> 23.3 us
  blocking collectives: 56.1 us -> 0 us
  matrix products: 25.4 us -> 14.1 us
  loops' own time: 0 us -> 9 us
  between operations: 14.8 us -> 5.87 us
    all_to_all x15 -> x2, waiting for transfers between devices: 249 us -> 4.02 us  [the longest x1 4.01 us: on_device(): back = lax.all_to_all(back, GROUP, split_axis=0, concat_axis=0, tiled=True)]
    ppermute x0 -> x30, starting transfers between devices: none -> 204 us  [the longest x22 147 us: flip(): return lax.ppermute(value, axis, FLIP)]
    all_to_all x15 -> x2, starting transfers between devices: 108 us -> 45.9 us  [the longest x1 38.9 us: on_device(): back = lax.all_to_all(back, GROUP, split_axis=0, concat_axis=0, tiled=True)]
    ppermute x0 -> x30, waiting for transfers between devices: none -> 57.1 us  [the longest x22 57.1 us: flip(): return lax.ppermute(value, axis, FLIP)]
    all_to_all x1 -> x0, blocking collectives: 56.1 us -> none  [on_device(): lax.all_to_all(send_rows, 'expert', split_axis=0, concat_axis=0, tiled=True)]
    all_to_all x6 -> x0, other arithmetic: 48.7 us -> none  [the longest x1 13.8 us: move_weights(): lax.all_to_all(jnp.take(spread[0], slot_from, axis=0), 'expert', split_ax...]
    unnamed x66 -> x40, local copies, waits for them, and re-layouts: 52.4 us -> 5.67 us
    all_to_all x11 -> x0, local copies, waits for them, and re-layouts: 41 us -> none  [the longest x2 10.6 us: move_weights(): lax.all_to_all(slot_in.reshape(count, -1), 'expert', split_axis=0, concat...]
  transfers between devices with their start and end apart: 17 -> 32, of which waited for: 13 -> 13; matrix products, arithmetic and copies ran while one was open for 31% -> 7% of each run, Pallas kernels for 0% -> 0%
where the time goes in v1:
time: 385 us; the launch traced here: 380 us
  starting transfers between devices  250 us (65%)
  waiting for transfers between devices  61.1 us (16%)
  other arithmetic  23.3 us (6%)
  local copies, waits for them, and re-layouts  16.5 us (4%)
  matrix products  14.1 us (4%)
  loops' own time  9 us (2%)
  between operations  5.87 us (2%)
    ppermute x22, starting transfers between devices, flip(): return lax.ppermute(value, axis, FLIP)  147 us
    ppermute x22, waiting for transfers between devices, flip(): return lax.ppermute(value, axis, FLIP)  57.1 us
    ppermute x8, starting transfers between devices, move(): return tuple((lax.ppermute(value, PARTS, pairs) for value in values))  56.6 us
    all_to_all x1, starting transfers between devices, on_device(): back = lax.all_to_all(back, GROUP, split_axis=0, concat_axis=0, tiled=True)  38.9 us
    unnamed x2, loops' own time  9 us
  transfers between devices with their start and end apart: 32, of which 13 were waited for; matrix products, arithmetic and copies ran while one was open for 7% of the time, Pallas kernels for 0%

profile of v1, /device:TPU:0, one launch (start us, length us, event | category | flops | bytes accessed | tf_op | source)
XLA Modules:
  0.0 379.7 jit_solution(2610573424858715419)
XLA Ops:
  3.9 1.2 fusion.2
  5.2 1.1 pad_maximum_fusion.2
  6.3 7.0 %all-to-all-start = ((bf16[8,16,4096]{2,1,0:T(8,128)(2,1)}), bf16[8,16,4096]{2,1,0:T(8,128)(2,1)}, u32[]{:S(2)}, u32[]{:S(2)}) async-start(bf16[8,16,4096]{2,1,0:T(8,128)(2,1)} %pad_maximum_fusion.2), calls=%async_computation | async-start | bytes 2097152 | tf_op jit(solution)/shard_map/all_to_all | solution.py:125
  18.1 1.3 dynamic-slice_bitcast_fusion
  19.4 1.1 dynamic-slice_bitcast_fusion.1
  20.6 56.1 %conditional.8 = (bf16[2048,256]{1,0:T(8,128)(2,1)}, bf16[64,4096]{1,0:T(8,128)(2,1)}, bf16[2048,256]{1,0:T(8,128)(2,1)}, bf16[2048,256]{1,0:T(8,128)(2,1)}, bf1...) conditional(s32[]{:T(128)} %clamp.4, (bf16[2048,256]{1,0:T(8,128)(2,1)S(1)}, ...), branch_computations={%region_6.7_spmd, %region_7.8_spmd, %region_8.9_spmd, %region_9.10... | conditional | flops 1572864 | bytes 40894808
  20.6 12.1 %collective-permute-start.78 = (bf16[2048,256]{1,0:T(8,128)(2,1)S(1)}, bf16[2048,256]{1,0:T(8,128)(2,1)}, u32[]{:S(2)}, u32[]{:S(2)}) collective-permute-start(bf16[2048,256]{1,0:T(8,128)(2,1)S(1)} %get-tuple-element.678), channel_id=1, source_target_pairs={{16,24},{24,16},{17,25},{25,17},{18,26},{26,18},{19,27},{27,19},{2... | collective-permute-start | bytes 3145736 | tf_op jit(solution)/shard_map/cond/branch_13_fun/ppermute | solution.py:63
  32.7 1.5 collective-permute-start.79
  34.3 10.6 %collective-permute-start.80 = (bf16[2048,256]{1,0:T(8,128)(2,1)S(1)}, bf16[2048,256]{1,0:T(8,128)(2,1)}, u32[]{:S(2)}, u32[]{:S(2)}) collective-permute-start(bf16[2048,256]{1,0:T(8,128)(2,1)S(1)} %convert_element_type.720), channel_id=1, source_target_pairs={{16,24},{24,16},{17,25},{25,17},{18,26},{26,18},{19,27},{27,19},{2... | collective-permute-start | bytes 3145736 | tf_op jit(solution)/shard_map/cond/branch_13_fun/ppermute | solution.py:63
  45.0 10.7 %collective-permute-start.81 = (bf16[2048,256]{1,0:T(8,128)(2,1)S(1)}, bf16[2048,256]{1,0:T(8,128)(2,1)}, u32[]{:S(2)}, u32[]{:S(2)}) collective-permute-start(bf16[2048,256]{1,0:T(8,128)(2,1)S(1)} %convert_element_type.721), channel_id=1, source_target_pairs={{16,24},{24,16},{17,25},{25,17},{18,26},{26,18},{19,27},{27,19},{2... | collective-permute-start | bytes 3145736 | tf_op jit(solution)/shard_map/cond/branch_13_fun/ppermute | solution.py:63
  55.7 10.4 %collective-permute-start.82 = (bf16[64,4096]{1,0:T(8,128)(2,1)S(1)}, bf16[64,4096]{1,0:T(8,128)(2,1)}, u32[]{:S(2)}, u32[]{:S(2)}) collective-permute-start(bf16[64,4096]{1,0:T(8,128)(2,1)S(1)} %convert_element_type.722), channel_id=1, source_target_pairs={{16,24},{24,16},{17,25},{25,17},{18,26},{26,18},{19,27},{27,19},{2... | collective-permute-start | bytes 1572872 | tf_op jit(solution)/shard_map/cond/branch_13_fun/ppermute | solution.py:63
  66.2 1.6 collective-permute-start.83
  77.4 1.4 slice_bitcast_fusion.14
  78.8 1.2 collective-permute-start.224
  80.0 1.6 collective-permute-start.225
  82.2 75.6 %collective-permute-start.235 = (bf16[64,4096]{1,0:T(8,128)(2,1)S(1)}, bf16[64,4096]{1,0:T(8,128)(2,1)S(1)}, u32[]{:S(2)}, u32[]{:S(2)}) collective-permute-start(bf16[64,4096]{1,0:T(8,128)(2,1)S(1)} %get-tuple-element.898), channel_id=1, source_target_pairs={{0,2},{2,0},{1,3},{3,1},{4,6},{6,4},{5,7},{7,5},{8,10},{10,8},{9,1... | collective-permute-start | bytes 1572872 | tf_op jit(solution)/shard_map/ppermute | solution.py:31
  157.7 1.3 constant_dynamic-update-slice_fusion.4
  159.0 1.3 collective-permute-start.227
  160.4 1.6 collective-permute-start.226
  162.4 9.2 %collective-permute-done.235 = bf16[64,4096]{1,0:T(8,128)(2,1)S(1)} collective-permute-done((bf16[64,4096]{1,0:T(8,128)(2,1)S(1)}, bf16[64,4096]{1,0:T(8,128)(2,1)S(1)}, u32[]{:S(2)}, u32[]{:S(2)}) %collective-permute-start.235) | collective-permute-done | bytes 524320 | tf_op jit(solution)/shard_map/ppermute | solution.py:31
  171.6 1.6 collective-permute-start.236
  173.3 3.9 %collective-permute-done.227 = bf16[32,4096]{1,0:T(8,128)(2,1)S(1)} collective-permute-done((bf16[32,4096]{1,0:T(8,128)(2,1)S(1)}, bf16[32,4096]{1,0:T(8,128)(2,1)S(1)}, u32[]{:S(2)}, u32[]{:S(2)}) %collective-permute-start.227) | collective-permute-done | bytes 262176 | tf_op jit(solution)/shard_map/ppermute | solution.py:31
  177.6 10.2 %collective-permute-start.228 = (bf16[4,64,4096]{2,1,0:T(8,128)(2,1)S(1)}, bf16[4,64,4096]{2,1,0:T(8,128)(2,1)S(1)}, u32[]{:S(2)}, u32[]{:S(2)}) collective-permute-start(bf16[4,64,4096]{2,1,0:T(8,128)(2,1)S(1)} %pad_maximum_fusion), channel_id=1, source_target_pairs={{0,1},{1,0},{2,3},{3,2},{4,5},{5,4},{6,7},{7,6},{8,9},{9,8},{10,11... | collective-permute-start | bytes 6291464 | tf_op jit(solution)/shard_map/ppermute | solution.py:31
  188.1 9.0 %collective-permute-start.238 = (bf16[4,64,4096]{2,1,0:T(8,128)(2,1)S(1)}, bf16[4,64,4096]{2,1,0:T(8,128)(2,1)S(1)}, u32[]{:S(2)}, u32[]{:S(2)}) collective-permute-start(bf16[4,64,4096]{2,1,0:T(8,128)(2,1)S(1)} %pad_maximum_fusion.1), channel_id=1, source_target_pairs={{0,1},{1,0},{2,3},{3,2},{4,5},{5,4},{6,7},{7,6},{8,9},{9,8},{10,11... | collective-permute-start | bytes 6291464 | tf_op jit(solution)/shard_map/ppermute | solution.py:31
  197.5 1.4 copy-done.64
  198.8 1.3 fusion.15
  201.4 1.6 multiply_multiply_fusion.2
  202.9 1.3 convolution_convert_fusion
  204.2 1.3 fusion.52
  205.6 1.3 multiply_convert_fusion
  207.7 2.7 fusion.66
  210.3 8.9 %collective-permute-start.239 = (bf16[4,64,4096]{2,1,0:T(8,128)(2,1)}, bf16[4,64,4096]{2,1,0:T(8,128)(2,1)}, u32[]{:S(2)}, u32[]{:S(2)}) collective-permute-start(bf16[4,64,4096]{2,1,0:T(8,128)(2,1)} %bitcast.29), channel_id=1, source_target_pairs={{0,1},{1,0},{2,3},{3,2},{4,5},{5,4},{6,7},{7,6},{8,9},{9,8},{10,11... | collective-permute-start | bytes 6291464 | tf_op jit(solution)/shard_map/ppermute | solution.py:31
  219.4 9.2 %collective-permute-start.244 = (bf16[2048,256]{1,0:T(8,128)(2,1)S(1)}, bf16[2048,256]{1,0:T(8,128)(2,1)S(1)}, u32[]{:S(2)}, u32[]{:S(2)}) collective-permute-start(bf16[2048,256]{1,0:T(8,128)(2,1)S(1)} %dynamic-slice_convert_fusion), channel_id=1, source_target_pairs={{0,64},{64,0},{1,65},{65,1},{2,66},{66,2},{3,67},{67,3},{4,68},{68... | collective-permute-start | bytes 3145736 | tf_op jit(solution)/shard_map/ppermute | solution.py:31
  228.6 9.0 %collective-permute-start.245 = (bf16[64,4096]{1,0:T(8,128)(2,1)S(1)}, bf16[64,4096]{1,0:T(8,128)(2,1)S(1)}, u32[]{:S(2)}, u32[]{:S(2)}) collective-permute-start(bf16[64,4096]{1,0:T(8,128)(2,1)S(1)} %dynamic-slice_convert_fusion.1), channel_id=1, source_target_pairs={{0,64},{64,0},{1,65},{65,1},{2,66},{66,2},{3,67},{67,3},{4,68},{68... | collective-permute-start | bytes 1572872 | tf_op jit(solution)/shard_map/ppermute | solution.py:31
  237.6 2.4 fusion.65
  240.0 8.9 %collective-permute-start.229 = (bf16[4,64,4096]{2,1,0:T(8,128)(2,1)}, bf16[4,64,4096]{2,1,0:T(8,128)(2,1)}, u32[]{:S(2)}, u32[]{:S(2)}) collective-permute-start(bf16[4,64,4096]{2,1,0:T(8,128)(2,1)} %bitcast.13), channel_id=1, source_target_pairs={{0,1},{1,0},{2,3},{3,2},{4,5},{5,4},{6,7},{7,6},{8,9},{9,8},{10,11... | collective-permute-start | bytes 6291464 | tf_op jit(solution)/shard_map/ppermute | solution.py:31
  248.9 17.3 %collective-permute-done.245 = bf16[64,4096]{1,0:T(8,128)(2,1)S(1)} collective-permute-done((bf16[64,4096]{1,0:T(8,128)(2,1)S(1)}, bf16[64,4096]{1,0:T(8,128)(2,1)S(1)}, u32[]{:S(2)}, u32[]{:S(2)}) %collective-permute-start.245) | collective-permute-done | bytes 524320 | tf_op jit(solution)/shard_map/ppermute | solution.py:31
  267.4 9.9 %conditional.9 = (bf16[2048,256]{1,0:T(8,128)(2,1)}, bf16[64,4096]{1,0:T(8,128)(2,1)}) conditional(s32[]{:T(128)} %clamp.4, (bf16[2048,256]{1,0:T(8,128)(2,1)S(1)}, bf16[64,4096]{1,0:T(8,128)(2,1)S(1)}) %tuple.685, (bf16[2048,256]{1,0:T(8,128)(2,1)S(1)}, bf16[64,4096]{1,0:T(8,128)(2,1)S(1)}) %tuple.685, ...), branch_computations={%region_34.35_spmd, %region_35.36_spmd, %region_36.37_spmd, %regio... | conditional | bytes 6291552
  267.4 8.4 %collective-permute-start.194 = (bf16[2048,256]{1,0:T(8,128)(2,1)S(1)}, bf16[2048,256]{1,0:T(8,128)(2,1)}, u32[]{:S(2)}, u32[]{:S(2)}) collective-permute-start(bf16[2048,256]{1,0:T(8,128)(2,1)S(1)} %get-tuple-element.794), channel_id=1, source_target_pairs={{16,24},{24,16},{17,25},{25,17},{18,26},{26,18},{19,27},{27,19},{2... | collective-permute-start | bytes 3145736 | tf_op jit(solution)/shard_map/cond/branch_13_fun/ppermute | solution.py:63
  275.8 1.5 collective-permute-start.195
  277.2 3.1 convert_add_fusion
  280.5 1.3 collective-permute-start.240
  281.8 1.5 collective-permute-start.242
  283.2 2.4 convert_add_fusion.1
  286.3 1.0 collective-permute-start.232
  287.3 1.4 collective-permute-done.240
  288.6 2.3 collective-permute-done.242
  291.2 2.0 collective-permute-start.241
  293.2 1.9 collective-permute-done.230
  295.1 1.5 collective-permute-done.232
  297.4 1.4 collective-permute-start.231
  298.8 7.5 %collective-permute-done.243 = bf16[64,4096]{1,0:T(8,128)(2,1)S(1)} collective-permute-done((bf16[64,4096]{1,0:T(8,128)(2,1)S(1)}, bf16[64,4096]{1,0:T(8,128)(2,1)S(1)}, u32[]{:S(2)}, u32[]{:S(2)}) %collective-permute-start.243) | collective-permute-done | bytes 524320 | tf_op jit(solution)/shard_map/ppermute | solution.py:31
  306.3 1.5 collective-permute-done.241
  308.0 8.5 %collective-permute-done.233 = bf16[64,4096]{1,0:T(8,128)(2,1)S(1)} collective-permute-done((bf16[64,4096]{1,0:T(8,128)(2,1)S(1)}, bf16[64,4096]{1,0:T(8,128)(2,1)S(1)}, u32[]{:S(2)}, u32[]{:S(2)}) %collective-permute-start.233) | collective-permute-done | bytes 524320 | tf_op jit(solution)/shard_map/ppermute | solution.py:31
  316.5 1.5 collective-permute-done.231
  318.1 1.1 pad_maximum_fusion.3
  319.2 38.9 %all-to-all-start.1 = ((bf16[8,16,4096]{2,1,0:T(8,128)(2,1)}), bf16[8,16,4096]{2,1,0:T(8,128)(2,1)}, u32[]{:S(2)}, u32[]{:S(2)}) async-start(bf16[8,16,4096]{2,1,0:T(8,128)(2,1)} %pad_maximum_fusion.3), calls=%async_computation.1 | async-start | bytes 2097152 | tf_op jit(solution)/shard_map/all_to_all | solution.py:182
  358.2 4.7 %fusion.46 = (bf16[1,64,4096]{2,1,0:T(8,128)(2,1)}, f32[64,4096]{1,0:T(8,128)}, f32[64,4096]{1,0:T(8,128)}) fusion(bf16[64,4096]{1,0:T(8,128)(2,1)} %get-tuple-element.844, pred[]{:T(512)S(6)} %or.3, bf16[64,4096]{1,0:T(8,128)(2,1)} %copy-done.69, f32[128,4096]{1,0:T(8,128)} %copy-done.63, s32[]{:T(128)S(6)} %select_n.80, ...), kind=kLoop, calls=%fused_computation.92 | loop fusion | flops 6291456 | bytes 8912901 | tf_op jit(solution)/shard_map/broadcast_in_dim | solution.py:205
  362.9 1.1 copy-done.65
  363.9 6.3 %fusion.33 = (bf16[1,2048,256]{2,1,0:T(8,128)(2,1)}, f32[2048,256]{1,0:T(8,128)}, f32[2048,256]{1,0:T(8,128)}) fusion(bf16[2048,256]{1,0:T(8,128)(2,1)} %get-tuple-element.840, pred[]{:T(512)S(6)} %or.3, bf16[2048,256]{1,0:T(8,128)(2,1)} %copy-done.67, f32[4096,256]{1,0:T(8,128)S(1)} %copy-done.62, s32[]{:T(128)S(6)} %select_n.79, ...), kind=kLoop, calls=%fused_computation.65 | loop fusion | flops 12582912 | bytes 17825796 | tf_op jit(solution)/shard_map/broadcast_in_dim | solution.py:204
  370.2 4.0 %all-to-all-done.1 = bf16[8,16,4096]{2,1,0:T(8,128)(2,1)} async-done(((bf16[8,16,4096]{2,1,0:T(8,128)(2,1)}), bf16[8,16,4096]{2,1,0:T(8,128)(2,1)}, u32[]{:S(2)}, u32[]{:S(2)}) %all-to-all-start.1) | async-done | bytes 1048608 | tf_op jit(solution)/shard_map/all_to_all | solution.py:182
  374.3 1.9 convolution_convert_fusion.2
  376.1 1.2 convolution_multiply_fusion.3
  377.4 1.9 fusion.4
  (105 shorter events, 12.7 us)
Async XLA Ops:
  0.6 2.9 copy-start
  5.2 8.1 %copy-start.70 = (s32[8]{0:T(128)S(1)}, s32[8]{0:T(128)}, u32[]{:S(2)}) copy-start(s32[8]{0:T(128)} %param.71) | copy-start | bytes 100
  6.3 71.1 %all-to-all-start = ((bf16[8,16,4096]{2,1,0:T(8,128)(2,1)}), bf16[8,16,4096]{2,1,0:T(8,128)(2,1)}, u32[]{:S(2)}, u32[]{:S(2)}) async-start(bf16[8,16,4096]{2,1,0:T(8,128)(2,1)} %pad_maximum_fusion.2), calls=%async_computation | async-start | bytes 2097152 | tf_op jit(solution)/shard_map/all_to_all | solution.py:125
  13.3 7.3 %copy-start.2 = (f32[1,2048,256]{2,1,0:T(8,128)S(1)}, f32[1,2048,256]{2,1,0:T(8,128)}, u32[]{:S(2)}) copy-start(f32[1,2048,256]{2,1,0:T(8,128)} %param.74) | copy-start | bytes 6291460
  13.3 7.3 %copy-start.32 = (f32[1,64,4096]{2,1,0:T(8,128)S(1)}, f32[1,64,4096]{2,1,0:T(8,128)}, u32[]{:S(2)}) copy-start(f32[1,64,4096]{2,1,0:T(8,128)} %param.76) | copy-start | bytes 3145732
  20.6 24.2 %copy-start.17 = (f32[2048,256]{1,0:T(8,128)S(1)}, f32[2048,256]{1,0:T(8,128)}, u32[]{:S(2)}) copy-start(f32[2048,256]{1,0:T(8,128)} %get-tuple-element.681) | copy-start | bytes 6291460
  20.6 47.1 %collective-permute-start.78 = (bf16[2048,256]{1,0:T(8,128)(2,1)S(1)}, bf16[2048,256]{1,0:T(8,128)(2,1)}, u32[]{:S(2)}, u32[]{:S(2)}) collective-permute-start(bf16[2048,256]{1,0:T(8,128)(2,1)S(1)} %get-tuple-element.678), channel_id=1, source_target_pairs={{16,24},{24,16},{17,25},{25,17},{18,26},{26,18},{19,27},{27,19},{2... | collective-permute-start | bytes 3145736 | tf_op jit(solution)/shard_map/cond/branch_13_fun/ppermute | solution.py:63
  32.7 33.4 %collective-permute-start.79 = (bf16[64,4096]{1,0:T(8,128)(2,1)S(1)}, bf16[64,4096]{1,0:T(8,128)(2,1)}, u32[]{:S(2)}, u32[]{:S(2)}) collective-permute-start(bf16[64,4096]{1,0:T(8,128)(2,1)S(1)} %get-tuple-element.679), channel_id=1, source_target_pairs={{16,24},{24,16},{17,25},{25,17},{18,26},{26,18},{19,27},{27,19},{2... | collective-permute-start | bytes 1572872 | tf_op jit(solution)/shard_map/cond/branch_13_fun/ppermute | solution.py:63
  34.3 33.4 %collective-permute-start.80 = (bf16[2048,256]{1,0:T(8,128)(2,1)S(1)}, bf16[2048,256]{1,0:T(8,128)(2,1)}, u32[]{:S(2)}, u32[]{:S(2)}) collective-permute-start(bf16[2048,256]{1,0:T(8,128)(2,1)S(1)} %convert_element_type.720), channel_id=1, source_target_pairs={{16,24},{24,16},{17,25},{25,17},{18,26},{26,18},{19,27},{27,19},{2... | collective-permute-start | bytes 3145736 | tf_op jit(solution)/shard_map/cond/branch_13_fun/ppermute | solution.py:63
  44.9 21.2 %copy-start.46 = (f32[64,4096]{1,0:T(8,128)S(1)}, f32[64,4096]{1,0:T(8,128)}, u32[]{:S(2)}) copy-start(f32[64,4096]{1,0:T(8,128)} %get-tuple-element.683) | copy-start | bytes 3145732
  45.0 22.8 %collective-permute-start.81 = (bf16[2048,256]{1,0:T(8,128)(2,1)S(1)}, bf16[2048,256]{1,0:T(8,128)(2,1)}, u32[]{:S(2)}, u32[]{:S(2)}) collective-permute-start(bf16[2048,256]{1,0:T(8,128)(2,1)S(1)} %convert_element_type.721), channel_id=1, source_target_pairs={{16,24},{24,16},{17,25},{25,17},{18,26},{26,18},{19,27},{27,19},{2... | collective-permute-start | bytes 3145736 | tf_op jit(solution)/shard_map/cond/branch_13_fun/ppermute | solution.py:63
  55.7 12.0 %collective-permute-start.82 = (bf16[64,4096]{1,0:T(8,128)(2,1)S(1)}, bf16[64,4096]{1,0:T(8,128)(2,1)}, u32[]{:S(2)}, u32[]{:S(2)}) collective-permute-start(bf16[64,4096]{1,0:T(8,128)(2,1)S(1)} %convert_element_type.722), channel_id=1, source_target_pairs={{16,24},{24,16},{17,25},{25,17},{18,26},{26,18},{19,27},{27,19},{2... | collective-permute-start | bytes 1572872 | tf_op jit(solution)/shard_map/cond/branch_13_fun/ppermute | solution.py:63
  66.2 1.6 collective-permute-start.83
  78.8 80.2 %collective-permute-start.224 = (bf16[64,4096]{1,0:T(8,128)(2,1)S(1)}, bf16[64,4096]{1,0:T(8,128)(2,1)S(1)}, u32[]{:S(2)}, u32[]{:S(2)}) collective-permute-start(bf16[64,4096]{1,0:T(8,128)(2,1)S(1)} %get-tuple-element.897), channel_id=1, source_target_pairs={{0,4},{4,0},{1,5},{5,1},{2,6},{6,2},{3,7},{7,3},{8,12},{12,8},{9,1... | collective-permute-start | bytes 1572872 | tf_op jit(solution)/shard_map/ppermute | solution.py:31
  80.0 80.3 %collective-permute-start.225 = (bf16[64,4096]{1,0:T(8,128)(2,1)S(1)}, bf16[64,4096]{1,0:T(8,128)(2,1)S(1)}, u32[]{:S(2)}, u32[]{:S(2)}) collective-permute-start(bf16[64,4096]{1,0:T(8,128)(2,1)S(1)} %get-tuple-element.897), channel_id=1, source_target_pairs={{0,2},{2,0},{1,3},{3,1},{4,6},{6,4},{5,7},{7,5},{8,10},{10,8},{9,1... | collective-permute-start | bytes 1572872 | tf_op jit(solution)/shard_map/ppermute | solution.py:31
  81.6 80.3 %collective-permute-start.234 = (bf16[64,4096]{1,0:T(8,128)(2,1)S(1)}, bf16[64,4096]{1,0:T(8,128)(2,1)S(1)}, u32[]{:S(2)}, u32[]{:S(2)}) collective-permute-start(bf16[64,4096]{1,0:T(8,128)(2,1)S(1)} %get-tuple-element.898), channel_id=1, source_target_pairs={{0,4},{4,0},{1,5},{5,1},{2,6},{6,2},{3,7},{7,3},{8,12},{12,8},{9,1... | collective-permute-start | bytes 1572872 | tf_op jit(solution)/shard_map/ppermute | solution.py:31
  82.2 89.5 %collective-permute-start.235 = (bf16[64,4096]{1,0:T(8,128)(2,1)S(1)}, bf16[64,4096]{1,0:T(8,128)(2,1)S(1)}, u32[]{:S(2)}, u32[]{:S(2)}) collective-permute-start(bf16[64,4096]{1,0:T(8,128)(2,1)S(1)} %get-tuple-element.898), channel_id=1, source_target_pairs={{0,2},{2,0},{1,3},{3,1},{4,6},{6,4},{5,7},{7,5},{8,10},{10,8},{9,1... | collective-permute-start | bytes 1572872 | tf_op jit(solution)/shard_map/ppermute | solution.py:31
  159.0 18.2 %collective-permute-start.227 = (bf16[32,4096]{1,0:T(8,128)(2,1)S(1)}, bf16[32,4096]{1,0:T(8,128)(2,1)S(1)}, u32[]{:S(2)}, u32[]{:S(2)}) collective-permute-start(bf16[32,4096]{1,0:T(8,128)(2,1)S(1)} %slice.207), channel_id=1, source_target_pairs={{0,2},{2,0},{1,3},{3,1},{4,6},{6,4},{5,7},{7,5},{8,10},{10,8},{9,1... | collective-permute-start | bytes 786440 | tf_op jit(solution)/shard_map/ppermute | solution.py:31
  160.4 16.9 %collective-permute-start.226 = (bf16[32,4096]{1,0:T(8,128)(2,1)S(1)}, bf16[32,4096]{1,0:T(8,128)(2,1)S(1)}, u32[]{:S(2)}, u32[]{:S(2)}) collective-permute-start(bf16[32,4096]{1,0:T(8,128)(2,1)S(1)} %slice.206), channel_id=1, source_target_pairs={{0,4},{4,0},{1,5},{5,1},{2,6},{6,2},{3,7},{7,3},{8,12},{12,8},{9,1... | collective-permute-start | bytes 786440 | tf_op jit(solution)/shard_map/ppermute | solution.py:31
  161.9 25.9 %collective-permute-start.237 = (bf16[32,4096]{1,0:T(8,128)(2,1)S(1)}, bf16[32,4096]{1,0:T(8,128)(2,1)S(1)}, u32[]{:S(2)}, u32[]{:S(2)}) collective-permute-start(bf16[32,4096]{1,0:T(8,128)(2,1)S(1)} %slice.221), channel_id=1, source_target_pairs={{0,2},{2,0},{1,3},{3,1},{4,6},{6,4},{5,7},{7,5},{8,10},{10,8},{9,1... | collective-permute-start | bytes 786440 | tf_op jit(solution)/shard_map/ppermute | solution.py:31
  171.6 16.2 %collective-permute-start.236 = (bf16[32,4096]{1,0:T(8,128)(2,1)S(1)}, bf16[32,4096]{1,0:T(8,128)(2,1)S(1)}, u32[]{:S(2)}, u32[]{:S(2)}) collective-permute-start(bf16[32,4096]{1,0:T(8,128)(2,1)S(1)} %slice.220), channel_id=1, source_target_pairs={{0,4},{4,0},{1,5},{5,1},{2,6},{6,2},{3,7},{7,3},{8,12},{12,8},{9,1... | collective-permute-start | bytes 786440 | tf_op jit(solution)/shard_map/ppermute | solution.py:31
  177.6 19.7 %collective-permute-start.228 = (bf16[4,64,4096]{2,1,0:T(8,128)(2,1)S(1)}, bf16[4,64,4096]{2,1,0:T(8,128)(2,1)S(1)}, u32[]{:S(2)}, u32[]{:S(2)}) collective-permute-start(bf16[4,64,4096]{2,1,0:T(8,128)(2,1)S(1)} %pad_maximum_fusion), channel_id=1, source_target_pairs={{0,1},{1,0},{2,3},{3,2},{4,5},{5,4},{6,7},{7,6},{8,9},{9,8},{10,11... | collective-permute-start | bytes 6291464 | tf_op jit(solution)/shard_map/ppermute | solution.py:31
  188.1 12.7 %collective-permute-start.238 = (bf16[4,64,4096]{2,1,0:T(8,128)(2,1)S(1)}, bf16[4,64,4096]{2,1,0:T(8,128)(2,1)S(1)}, u32[]{:S(2)}, u32[]{:S(2)}) collective-permute-start(bf16[4,64,4096]{2,1,0:T(8,128)(2,1)S(1)} %pad_maximum_fusion.1), channel_id=1, source_target_pairs={{0,1},{1,0},{2,3},{3,2},{4,5},{5,4},{6,7},{7,6},{8,9},{9,8},{10,11... | collective-permute-start | bytes 6291464 | tf_op jit(solution)/shard_map/ppermute | solution.py:31
  197.2 1.6 copy-start.64
  200.1 1.2 copy-start.68
  205.6 60.8 %copy-start.61 = (f32[4096,256]{1,0:T(8,128)}, f32[4096,256]{1,0:T(8,128)S(1)}, u32[]{:S(2)}) copy-start(f32[4096,256]{1,0:T(8,128)S(1)} %fusion.52) | copy-start | bytes 12582916
  207.6 58.6 %copy-start.63 = (f32[128,4096]{1,0:T(8,128)}, f32[128,4096]{1,0:T(8,128)S(1)}, u32[]{:S(2)}) copy-start(f32[128,4096]{1,0:T(8,128)S(1)} %convolution_multiply_fusion) | copy-start | bytes 6291460
  210.3 66.9 %collective-permute-start.239 = (bf16[4,64,4096]{2,1,0:T(8,128)(2,1)}, bf16[4,64,4096]{2,1,0:T(8,128)(2,1)}, u32[]{:S(2)}, u32[]{:S(2)}) collective-permute-start(bf16[4,64,4096]{2,1,0:T(8,128)(2,1)} %bitcast.29), channel_id=1, source_target_pairs={{0,1},{1,0},{2,3},{3,2},{4,5},{5,4},{6,7},{7,6},{8,9},{9,8},{10,11... | collective-permute-start | bytes 6291464 | tf_op jit(solution)/shard_map/ppermute | solution.py:31
  219.4 47.0 %collective-permute-start.244 = (bf16[2048,256]{1,0:T(8,128)(2,1)S(1)}, bf16[2048,256]{1,0:T(8,128)(2,1)S(1)}, u32[]{:S(2)}, u32[]{:S(2)}) collective-permute-start(bf16[2048,256]{1,0:T(8,128)(2,1)S(1)} %dynamic-slice_convert_fusion), channel_id=1, source_target_pairs={{0,64},{64,0},{1,65},{65,1},{2,66},{66,2},{3,67},{67,3},{4,68},{68... | collective-permute-start | bytes 3145736 | tf_op jit(solution)/shard_map/ppermute | solution.py:31
  228.6 37.6 %collective-permute-start.245 = (bf16[64,4096]{1,0:T(8,128)(2,1)S(1)}, bf16[64,4096]{1,0:T(8,128)(2,1)S(1)}, u32[]{:S(2)}, u32[]{:S(2)}) collective-permute-start(bf16[64,4096]{1,0:T(8,128)(2,1)S(1)} %dynamic-slice_convert_fusion.1), channel_id=1, source_target_pairs={{0,64},{64,0},{1,65},{65,1},{2,66},{66,2},{3,67},{67,3},{4,68},{68... | collective-permute-start | bytes 1572872 | tf_op jit(solution)/shard_map/ppermute | solution.py:31
  240.0 43.2 %collective-permute-start.229 = (bf16[4,64,4096]{2,1,0:T(8,128)(2,1)}, bf16[4,64,4096]{2,1,0:T(8,128)(2,1)}, u32[]{:S(2)}, u32[]{:S(2)}) collective-permute-start(bf16[4,64,4096]{2,1,0:T(8,128)(2,1)} %bitcast.13), channel_id=1, source_target_pairs={{0,1},{1,0},{2,3},{3,2},{4,5},{5,4},{6,7},{7,6},{8,9},{9,8},{10,11... | collective-permute-start | bytes 6291464 | tf_op jit(solution)/shard_map/ppermute | solution.py:31
  266.2 0.8 copy-start.69
  266.3 1.0 copy-start.67
  267.4 9.9 %collective-permute-start.194 = (bf16[2048,256]{1,0:T(8,128)(2,1)S(1)}, bf16[2048,256]{1,0:T(8,128)(2,1)}, u32[]{:S(2)}, u32[]{:S(2)}) collective-permute-start(bf16[2048,256]{1,0:T(8,128)(2,1)S(1)} %get-tuple-element.794), channel_id=1, source_target_pairs={{16,24},{24,16},{17,25},{25,17},{18,26},{26,18},{19,27},{27,19},{2... | collective-permute-start | bytes 3145736 | tf_op jit(solution)/shard_map/cond/branch_13_fun/ppermute | solution.py:63
  275.8 1.5 collective-permute-start.195
  280.4 2.9 copy-start.66
  280.5 8.2 %collective-permute-start.240 = (bf16[32,4096]{1,0:T(8,128)(2,1)S(1)}, bf16[32,4096]{1,0:T(8,128)(2,1)S(1)}, u32[]{:S(2)}, u32[]{:S(2)}) collective-permute-start(bf16[32,4096]{1,0:T(8,128)(2,1)S(1)} %get-tuple-element.895), channel_id=1, source_target_pairs={{0,2},{2,0},{1,3},{3,1},{4,6},{6,4},{5,7},{7,5},{8,10},{10,8},{9,1... | collective-permute-start | bytes 786440 | tf_op jit(solution)/shard_map/ppermute | solution.py:31
  281.8 9.2 %collective-permute-start.242 = (bf16[32,4096]{1,0:T(8,128)(2,1)S(1)}, bf16[32,4096]{1,0:T(8,128)(2,1)S(1)}, u32[]{:S(2)}, u32[]{:S(2)}) collective-permute-start(bf16[32,4096]{1,0:T(8,128)(2,1)S(1)} %get-tuple-element.894), channel_id=1, source_target_pairs={{0,4},{4,0},{1,5},{5,1},{2,6},{6,2},{3,7},{7,3},{8,12},{12,8},{9,1... | collective-permute-start | bytes 786440 | tf_op jit(solution)/shard_map/ppermute | solution.py:31
  285.8 9.3 %collective-permute-start.230 = (bf16[32,4096]{1,0:T(8,128)(2,1)S(1)}, bf16[32,4096]{1,0:T(8,128)(2,1)S(1)}, u32[]{:S(2)}, u32[]{:S(2)}) collective-permute-start(bf16[32,4096]{1,0:T(8,128)(2,1)S(1)} %get-tuple-element.891), channel_id=1, source_target_pairs={{0,2},{2,0},{1,3},{3,1},{4,6},{6,4},{5,7},{7,5},{8,10},{10,8},{9,1... | collective-permute-start | bytes 786440 | tf_op jit(solution)/shard_map/ppermute | solution.py:31
  286.3 10.3 %collective-permute-start.232 = (bf16[32,4096]{1,0:T(8,128)(2,1)S(1)}, bf16[32,4096]{1,0:T(8,128)(2,1)S(1)}, u32[]{:S(2)}, u32[]{:S(2)}) collective-permute-start(bf16[32,4096]{1,0:T(8,128)(2,1)S(1)} %get-tuple-element.890), channel_id=1, source_target_pairs={{0,4},{4,0},{1,5},{5,1},{2,6},{6,2},{3,7},{7,3},{8,12},{12,8},{9,1... | collective-permute-start | bytes 786440 | tf_op jit(solution)/shard_map/ppermute | solution.py:31
  291.1 15.2 %collective-permute-start.243 = (bf16[64,4096]{1,0:T(8,128)(2,1)S(1)}, bf16[64,4096]{1,0:T(8,128)(2,1)S(1)}, u32[]{:S(2)}, u32[]{:S(2)}) collective-permute-start(bf16[64,4096]{1,0:T(8,128)(2,1)S(1)} %pad_maximum_fusion.7), channel_id=1, source_target_pairs={{0,2},{2,0},{1,3},{3,1},{4,6},{6,4},{5,7},{7,5},{8,10},{10,8},{9,1... | collective-permute-start | bytes 1572872 | tf_op jit(solution)/shard_map/ppermute | solution.py:31
  291.2 16.6 %collective-permute-start.241 = (bf16[64,4096]{1,0:T(8,128)(2,1)S(1)}, bf16[64,4096]{1,0:T(8,128)(2,1)S(1)}, u32[]{:S(2)}, u32[]{:S(2)}) collective-permute-start(bf16[64,4096]{1,0:T(8,128)(2,1)S(1)} %pad_maximum_fusion.6), channel_id=1, source_target_pairs={{0,4},{4,0},{1,5},{5,1},{2,6},{6,2},{3,7},{7,3},{8,12},{12,8},{9,1... | collective-permute-start | bytes 1572872 | tf_op jit(solution)/shard_map/ppermute | solution.py:31
  296.7 19.7 %collective-permute-start.233 = (bf16[64,4096]{1,0:T(8,128)(2,1)S(1)}, bf16[64,4096]{1,0:T(8,128)(2,1)S(1)}, u32[]{:S(2)}, u32[]{:S(2)}) collective-permute-start(bf16[64,4096]{1,0:T(8,128)(2,1)S(1)} %pad_maximum_fusion.5), channel_id=1, source_target_pairs={{0,2},{2,0},{1,3},{3,1},{4,6},{6,4},{5,7},{7,5},{8,10},{10,8},{9,1... | collective-permute-start | bytes 1572872 | tf_op jit(solution)/shard_map/ppermute | solution.py:31
  297.4 20.5 %collective-permute-start.231 = (bf16[64,4096]{1,0:T(8,128)(2,1)S(1)}, bf16[64,4096]{1,0:T(8,128)(2,1)S(1)}, u32[]{:S(2)}, u32[]{:S(2)}) collective-permute-start(bf16[64,4096]{1,0:T(8,128)(2,1)S(1)} %pad_maximum_fusion.4), channel_id=1, source_target_pairs={{0,4},{4,0},{1,5},{5,1},{2,6},{6,2},{3,7},{7,3},{8,12},{12,8},{9,1... | collective-permute-start | bytes 1572872 | tf_op jit(solution)/shard_map/ppermute | solution.py:31
  319.2 55.1 %all-to-all-start.1 = ((bf16[8,16,4096]{2,1,0:T(8,128)(2,1)}), bf16[8,16,4096]{2,1,0:T(8,128)(2,1)}, u32[]{:S(2)}, u32[]{:S(2)}) async-start(bf16[8,16,4096]{2,1,0:T(8,128)(2,1)} %pad_maximum_fusion.3), calls=%async_computation.1 | async-start | bytes 2097152 | tf_op jit(solution)/shard_map/all_to_all | solution.py:182
  358.1 4.7 %copy-start.3 = (f32[1,2048,256]{2,1,0:T(8,128)S(1)}, f32[1,2048,256]{2,1,0:T(8,128)}, u32[]{:S(2)}) copy-start(f32[1,2048,256]{2,1,0:T(8,128)} %param.75) | copy-start | bytes 6291460
  358.1 4.7 %copy-start.62 = (f32[4096,256]{1,0:T(8,128)S(1)}, f32[4096,256]{1,0:T(8,128)}, u32[]{:S(2)}) copy-start(f32[4096,256]{1,0:T(8,128)} %copy-done.61) | copy-start | bytes 12582916
  358.1 5.8 %copy-start.65 = (bf16[1,4096,256]{2,1,0:T(8,128)(2,1)S(1)}, bf16[1,4096,256]{2,1,0:T(8,128)(2,1)}, u32[]{:S(2)}) copy-start(bf16[1,4096,256]{2,1,0:T(8,128)(2,1)} %param.72) | copy-start | bytes 6291460
  363.9 15.3 %copy-start.1 = (bf16[16,4096]{1,0:T(8,128)(2,1)S(1)}, bf16[16,4096]{1,0:T(8,128)(2,1)}, u32[]{:S(2)}) copy-start(bf16[16,4096]{1,0:T(8,128)(2,1)} %param.67) | copy-start | bytes 393220

commit v2 on v1

v2 whole, which is shorter than its diff:
```python
import functools

import jax
import jax.numpy as jnp
from jax import lax
from jax.experimental import pallas as pl
from jax.experimental.pallas import tpu as pltpu
from jax.sharding import Mesh, PartitionSpec as P

FF = 1024

beta_one = 0.9
beta_two = 0.95
learn_rate = 0.01
decay_rate = 0.1
epsilon = 1e-08

PARTS = ("y", "xh", "xl", "z", "c")
GROUP = ("y", "xh")
DISTANCES = range(1, 8)
FLIP = [(0, 1), (1, 0)]
half_type = jnp.bfloat16


def adam_step(weight, grad, first, second):
    first_new = beta_one * first + (1.0 - beta_one) * grad
    second_new = beta_two * second + (1.0 - beta_two) * grad * grad
    weight_new = (
        weight - learn_rate * (first_new / (jnp.sqrt(second_new) + epsilon) + decay_rate * weight)
    ).astype(jnp.bfloat16)
    return (weight_new, first_new, second_new)


STEPS = 8


def sections(inner_rows, outer_rows, lanes, outer_columns):
    parts = outer_columns // lanes
    inner = [slice(k * inner_rows, (k + 1) * inner_rows) for k in range(3)]
    start = 3 * inner_rows
    outer = [
        [
            slice(start + (k * parts + p) * outer_rows, start + (k * parts + p + 1) * outer_rows)
            for p in range(parts)
        ]
        for k in range(3)
    ]
    return inner, outer


def step_specs(inner, outer):
    rows, lanes = inner.shape[0] // STEPS, inner.shape[1]
    outer_rows, columns = outer.shape[0], outer.shape[1] // STEPS
    inner_spec = pl.BlockSpec((rows, lanes), lambda i, at: (i, 0))
    outer_spec = pl.BlockSpec((outer_rows, columns), lambda i, at: (0, i))
    whole_inner = pl.BlockSpec((rows, lanes), lambda i, at: (at[0] * STEPS + i, 0))
    whole_outer = pl.BlockSpec((outer_rows, columns), lambda i, at: (at[0], i))
    height = 3 * rows + 3 * outer_rows * columns // lanes
    packed_spec = pl.BlockSpec((1, height, lanes), lambda i, at: (i, 0, 0))
    return inner_spec, outer_spec, whole_inner, whole_outer, packed_spec


def pack_kernel(at, first_in, second_in, weight_in, first_out, second_out, weight_out, packed):
    lanes = first_in.shape[1]
    inner, outer = sections(first_in.shape[0], first_out.shape[0], lanes, first_out.shape[1])
    moved = at[1] == 1

    def put(rows, value):
        packed[0, rows, :] = jnp.where(moved, value.astype(jnp.float32), 0.0).astype(packed.dtype)

    for rows, ref in zip(inner, (first_in, second_in, weight_in)):
        put(rows, ref[...])
    for parts, ref in zip(outer, (first_out, second_out, weight_out)):
        for p, rows in enumerate(parts):
            put(rows, ref[:, p * lanes : (p + 1) * lanes])


def pack(at, states, slot_in, slot_out):
    inner_spec, outer_spec, whole_inner, whole_outer, packed_spec = step_specs(states[0], states[2])
    return pl.pallas_call(
        pack_kernel,
        grid_spec=pltpu.PrefetchScalarGridSpec(
            num_scalar_prefetch=1,
            grid=(STEPS,),
            in_specs=[inner_spec, inner_spec, whole_inner, outer_spec, outer_spec, whole_outer],
            out_specs=packed_spec,
        ),
        out_shape=jax.ShapeDtypeStruct((STEPS,) + packed_spec.block_shape[1:], half_type),
        cost_estimate=pl.CostEstimate(flops=4 << 20, bytes_accessed=24 << 20, transcendentals=0),
    )(at, states[0], states[1], slot_in, states[2], states[3], slot_out)


def adam_kernel(
    at,
    packed,
    first_in,
    second_in,
    weight_in,
    first_out,
    second_out,
    weight_out,
    grad_in,
    grad_out,
    late_in,
    late_out,
    new_weight_in,
    new_first_in,
    new_second_in,
    new_weight_out,
    new_first_out,
    new_second_out,
):
    lanes = first_in.shape[1]
    inner, outer = sections(first_in.shape[0], first_out.shape[0], lanes, first_out.shape[1])
    moved = at[1] == 1

    def placed(rows, stayed):
        came = packed[0, rows, :].astype(jnp.float32) - stayed.astype(half_type).astype(jnp.float32)
        return jnp.where(moved, came, stayed.astype(jnp.float32))

    new_weight_in[...], new_first_in[...], new_second_in[...] = adam_step(
        placed(inner[2], weight_in[...]),
        jnp.where(moved, late_in[...].astype(jnp.float32), grad_in[...]),
        placed(inner[0], first_in[...]),
        placed(inner[1], second_in[...]),
    )
    for p in range(len(outer[0])):
        part = slice(p * lanes, (p + 1) * lanes)
        new_weight_out[:, part], new_first_out[:, part], new_second_out[:, part] = adam_step(
            placed(outer[2][p], weight_out[:, part]),
            jnp.where(moved, late_out[:, part].astype(jnp.float32), grad_out[:, part]),
            placed(outer[0][p], first_out[:, part]),
            placed(outer[1][p], second_out[:, part]),
        )


def adam(at, packed, states, slot_in, slot_out, grad_in, grad_out, late_in, late_out):
    inner_spec, outer_spec, whole_inner, whole_outer, packed_spec = step_specs(states[0], states[2])
    inner_shape, outer_shape = states[0].shape, states[2].shape
    return pl.pallas_call(
        adam_kernel,
        grid_spec=pltpu.PrefetchScalarGridSpec(
            num_scalar_prefetch=1,
            grid=(STEPS,),
            in_specs=[packed_spec, inner_spec, inner_spec, whole_inner, outer_spec, outer_spec, whole_outer]
            + [inner_spec, outer_spec, inner_spec, outer_spec],
            out_specs=[inner_spec] * 3 + [outer_spec] * 3,
        ),
        out_shape=[
            jax.ShapeDtypeStruct(shape, dtype)
            for shape in (inner_shape, outer_shape)
            for dtype in (jnp.bfloat16, jnp.float32, jnp.float32)
        ],
        cost_estimate=pl.CostEstimate(flops=16 << 20, bytes_accessed=30 << 20, transcendentals=1 << 20),
        compiler_params=pltpu.CompilerParams(vmem_limit_bytes=24 * 1024 * 1024),
    )(at, packed, states[0], states[1], slot_in, states[2], states[3], slot_out, grad_in, grad_out, late_in, late_out)


def flip(value, axis):
    return lax.ppermute(value, axis, FLIP)


def tie(first, *others):
    return lax.optimization_barrier((first,) + others)[0]


def split_at(rows, share):
    return int(rows * share) // 16 * 16


def gather_groups(pieces, share, holds):
    cut = split_at(pieces[0].shape[0], share)
    near = [(flip(piece, "xl"), flip(piece, "z"), flip(piece, "c")) for piece in pieces]
    gathered = []
    last = None
    for piece, (from_x, from_z, from_c), hold in zip(pieces, near, holds):
        if last is not None:
            from_x, from_z = tie((from_x, from_z), last)
        if hold is not None:
            from_x, from_z = tie((from_x, from_z), hold)
        parts = []
        if cut:
            parts.append(flip(from_z[:cut], "xl"))
        if cut < piece.shape[0]:
            parts.append(flip(from_x[cut:], "z"))
        sides = flip(jnp.concatenate([from_x, from_z]), "c")
        diag = jnp.concatenate(parts)
        gathered.append([piece, from_x, from_z, from_c, sides, diag, flip(diag, "c")])
        last = diag
    return [jnp.concatenate(parts) for parts in gathered]


def reduce_start(array, share):
    rows = array.shape[0] // 8
    piece = lambda start, count=1: array[start * rows : (start + count) * rows]
    cut = split_at(rows, share)
    diag = (piece(6).astype(jnp.float32) + flip(piece(7), "c").astype(jnp.float32)).astype(half_type)
    sides = piece(1, 2).astype(jnp.float32) + flip(piece(4, 2), "c").astype(jnp.float32)
    own = piece(0).astype(jnp.float32) + flip(piece(3), "c").astype(jnp.float32)
    to_x, to_z = sides[:rows], sides[rows:]
    if cut:
        via_x = flip(diag[:cut], "xl").astype(jnp.float32)
        to_z = jnp.concatenate([to_z[:cut] + via_x, to_z[cut:]])
    if cut < rows:
        via_z = flip(diag[cut:], "z").astype(jnp.float32)
        to_x = jnp.concatenate([to_x[:cut], to_x[cut:] + via_z])
    return own, to_x.astype(half_type), to_z.astype(half_type)


def exchange(values, distance):
    pairs = [(slot, slot ^ (distance * 8)) for slot in range(64)]
    return tuple(lax.ppermute(value, PARTS, pairs) for value in values)


def late_steps(values, rows_to_x, rows_to_z, distance):
    moved = exchange(values, distance)
    return moved, tuple(flip(rows, "xl") for rows in rows_to_x), tuple(flip(rows, "z") for rows in rows_to_z)


def on_device(
    tokens,
    cotangent,
    expert_ids,
    gate_weights,
    holder,
    weight_in,
    weight_out,
    first_in,
    second_in,
    first_out,
    second_out,
):
    tok_rows, width = tokens.shape
    top_count = expert_ids.shape[1]
    groups = holder.shape[0]
    shards = 8
    routed = tok_rows * top_count
    capacity = 2 * routed // groups
    hidden = weight_out.shape[1]
    data_half = lax.axis_index("dp")
    columns = jnp.arange(groups, dtype=jnp.int32)
    my_expert = lax.axis_index("y") * 2 + lax.axis_index("xh")
    changed = holder != columns
    low = jnp.min(jnp.where(changed, columns, groups - 1))
    high = jnp.max(jnp.where(changed, columns, 0))
    case = jnp.clip((low ^ high) - 1, 0, 6)
    moved = (my_expert == low) | (my_expert == high)
    slot_in = weight_in[0]
    slot_out = weight_out[0]
    states = (first_in[0], second_in[0], first_out[0], second_out[0])
    rows_in_half = first_in.shape[1]
    rows_out_half = first_out.shape[1]
    at = jnp.stack([data_half, moved]).astype(jnp.int32)

    flat_ids = expert_ids.reshape(routed)
    onehot = (flat_ids[:, None] == columns[None, :]).astype(jnp.int32)
    earlier = jnp.cumsum(onehot, axis=0) - onehot
    order_in = jnp.sum(earlier * onehot, axis=1)
    position = (flat_ids * capacity + order_in).reshape(tok_rows, top_count)
    places = jnp.arange(groups * capacity, dtype=jnp.int32)
    picks = position[:, :, None] == places[None, None, :]
    chosen = jnp.any(picks, axis=1).astype(jnp.bfloat16)
    gate_of = jnp.sum(jnp.where(picks, gate_weights[:, :, None], 0.0), axis=(0, 1))
    spread = (((0,), (0,)), ((), ()))
    group_inputs = lax.dot_general(chosen, tokens, spread, preferred_element_type=jnp.float32).astype(jnp.bfloat16)
    group_cots = (
        gate_of[:, None] * lax.dot_general(chosen, cotangent, spread, preferred_element_type=jnp.float32)
    ).astype(jnp.bfloat16)
    send = jnp.concatenate(
        [group_inputs.reshape(groups, capacity, width), group_cots.reshape(groups, capacity, width)], axis=1
    )
    at, send = lax.optimization_barrier((at, send))
    share = lax.psum_scatter(pack(at, states, slot_in, slot_out), GROUP, scatter_dimension=0, tiled=True)
    received = lax.all_to_all(send, GROUP, split_axis=0, concat_axis=0, tiled=True)
    rows_piece = received[:, :capacity].reshape(groups * capacity, width)
    cots_piece = received[:, capacity:].reshape(groups * capacity, width)
    rows_in, rows_cot = gather_groups((rows_piece, cots_piece), 0.5, (None, None))

    last_dims = (((1,), (1,)), ((), ()))
    first_dims = (((0,), (0,)), ((), ()))
    projected = jnp.dot(rows_in, slot_in, preferred_element_type=jnp.float32) * width ** (-0.5)
    gate_part = projected[:, :hidden]
    up_part = projected[:, hidden:]
    sigmoid = jax.nn.sigmoid(gate_part)
    activated = gate_part * sigmoid
    hidden_act = (activated * up_part).astype(jnp.bfloat16)
    outputs = (jnp.dot(hidden_act, slot_out, preferred_element_type=jnp.float32) * FF ** (-0.5)).astype(jnp.bfloat16)
    grad_hidden = lax.dot_general(rows_cot, slot_out, last_dims, preferred_element_type=jnp.float32) * FF ** (-0.5)
    slopes = sigmoid * (1.0 + gate_part * (1.0 - sigmoid))
    grad_gate = grad_hidden * up_part * slopes
    grad_up = grad_hidden * activated
    grad_pre = (jnp.concatenate([grad_gate, grad_up], axis=1) * width ** (-0.5)).astype(jnp.bfloat16)
    grad_rows = lax.dot_general(grad_pre, slot_in, last_dims, preferred_element_type=jnp.float32).astype(jnp.bfloat16)
    grad_in = lax.dot_general(rows_in, grad_pre, first_dims, preferred_element_type=jnp.float32)
    grad_out = lax.dot_general(hidden_act, rows_cot, first_dims, preferred_element_type=jnp.float32) * FF ** (-0.5)

    other_half = 1 - data_half
    away_in = lax.dynamic_slice_in_dim(grad_in, other_half * rows_in_half, rows_in_half, 0).astype(half_type)
    away_out = lax.dynamic_slice_in_dim(grad_out, other_half * rows_out_half, rows_out_half, 0).astype(half_type)
    kept_in = lax.dynamic_slice_in_dim(grad_in, data_half * rows_in_half, rows_in_half, 0)
    kept_out = lax.dynamic_slice_in_dim(grad_out, data_half * rows_out_half, rows_out_half, 0)
    came_out = flip(away_out, "dp")
    half_out = kept_out + came_out.astype(jnp.float32)
    half_in = kept_in + flip(away_in, "dp").astype(jnp.float32)
    half_in, half_out, share = lax.optimization_barrier((half_in, half_out, share))
    early = lax.all_gather(share, GROUP, axis=0, tiled=True)

    own_out, out_to_x, out_to_z = reduce_start(outputs, 0.5)
    own_grad, grad_to_x, grad_to_z = reduce_start(grad_rows, 0.5)
    (late_in, late_out), from_x, from_z = lax.switch(
        case,
        [functools.partial(late_steps, distance=distance) for distance in DISTANCES],
        (half_in.astype(half_type), half_out.astype(half_type)),
        (out_to_x, grad_to_x),
        (out_to_z, grad_to_z),
    )
    out_sum, grad_sum = (
        own + part_x.astype(jnp.float32) + part_z.astype(jnp.float32)
        for own, part_x, part_z in zip((own_out, own_grad), from_x, from_z)
    )
    back = jnp.concatenate(
        [
            out_sum.astype(half_type).reshape(groups, capacity, width),
            grad_sum.astype(half_type).reshape(groups, capacity, width),
        ],
        axis=1,
    )
    back = lax.all_to_all(back, GROUP, split_axis=0, concat_axis=0, tiled=True)
    new_weight_in, new_first_in, new_second_in, new_weight_out, new_first_out, new_second_out = adam(
        at, early, states, slot_in, slot_out, half_in, half_out, late_in, late_out
    )
    back, new_weight_in = lax.optimization_barrier((back, new_weight_in))
    back_out = back[:, :capacity].reshape(groups * capacity, width)
    back_grad = back[:, capacity:].reshape(groups * capacity, width)
    picked = picks.astype(jnp.bfloat16)
    layer_out = sum(
        gate_weights[:, k : k + 1] * jnp.dot(picked[:, k], back_out, preferred_element_type=jnp.float32)
        for k in range(top_count)
    ).astype(jnp.bfloat16)
    grad_tokens = jnp.dot(chosen, back_grad, preferred_element_type=jnp.float32).astype(jnp.bfloat16)

    return (
        layer_out,
        grad_tokens,
        new_weight_in[None],
        new_weight_out[None],
        new_first_in[None],
        new_second_in[None],
        new_first_out[None],
        new_second_out[None],
    )


def solution(mesh):
    fine = Mesh(mesh.devices.reshape(2, 4, 2, 2, 2, 2), ("dp",) + PARTS)
    rows = P(("dp",) + PARTS, None)
    slots = P(PARTS, None, None)
    halves = P(PARTS, "dp", None)
    return jax.shard_map(
        on_device,
        mesh=fine,
        in_specs=(rows, rows, rows, rows, P(), slots, slots, halves, halves, halves, halves),
        out_specs=(rows, rows, halves, halves, halves, halves, halves, halves),
        check_vma=False,
    )
```

time: 385 us -> 296 us (0.77); the launches traced: 380 us -> 298 us
  starting transfers between devices: 250 us -> 37.6 us
  waiting for transfers between devices: 61.1 us -> 175 us
  Pallas kernels: 0 us -> 17.4 us
  between operations: 5.87 us -> 17.3 us
  loops' own time: 9 us -> 0.06 us
  other arithmetic: 23.3 us -> 19.2 us
    ppermute x22 -> x30, starting transfers between devices: 147 us -> 20.4 us  [flip(): return lax.ppermute(value, axis, FLIP)]
    ppermute x22 -> x30, waiting for transfers between devices: 57.1 us -> 129 us  [flip(): return lax.ppermute(value, axis, FLIP)]
    ppermute x8 -> x2, starting transfers between devices: 56.6 us -> 5.8 us  [exchange(): return tuple((lax.ppermute(value, PARTS, pairs) for value in values))]
    all_to_all x1, starting transfers between devices: 38.9 us -> 4.26 us  [on_device(): back = lax.all_to_all(back, GROUP, split_axis=0, concat_axis=0, tiled=True)]
    all_gather x0 -> x1, waiting for transfers between devices: none -> 22.5 us  [on_device(): early = lax.all_gather(share, GROUP, axis=0, tiled=True)]
    pallas_call x0 -> x2, Pallas kernels: none -> 17.4 us  [the longest x1 9.09 us: adam(): pl.pallas_call(adam_kernel, grid_spec=pltpu.PrefetchScalarGridSpec(num_sc...]
    ppermute x8 -> x2, waiting for transfers between devices: 0.02 us -> 15.9 us  [exchange(): return tuple((lax.ppermute(value, PARTS, pairs) for value in values))]
    broadcast_in_dim x2 -> x0, other arithmetic: 11 us -> none  [the longest x1 6.31 us: on_device(): new_weight_in[None]]
  transfers between devices with their start and end apart: 32 -> 36, of which waited for: 13 -> 14; matrix products, arithmetic and copies ran while one was open for 7% -> 10% of each run, Pallas kernels for 0% -> 6%
where the time goes in v2:
time: 296 us; the launch traced here: 298 us
  waiting for transfers between devices  175 us (59%)
  starting transfers between devices  37.6 us (13%)
  other arithmetic  19.2 us (6%)
  Pallas kernels  17.4 us (6%)
  between operations  17.3 us (6%)
  local copies, waits for them, and re-layouts  16.7 us (6%)
  matrix products  14.2 us (5%)
    ppermute x30, waiting for transfers between devices, flip(): return lax.ppermute(value, axis, FLIP)  129 us
    all_gather x1, waiting for transfers between devices, on_device(): early = lax.all_gather(share, GROUP, axis=0, tiled=True)  22.5 us
    ppermute x30, starting transfers between devices, flip(): return lax.ppermute(value, axis, FLIP)  20.4 us
    ppermute x2, waiting for transfers between devices, exchange(): return tuple((lax.ppermute(value, PARTS, pairs) for value in values))  15.9 us
    unnamed x45, local copies, waits for them, and re-layouts  10 us
    pallas_call x1, Pallas kernels, adam(): pl.pallas_call(adam_kernel, grid_spec=pltpu.PrefetchScalarGridSpec(num_sc...  9.09 us
    pallas_call x1, Pallas kernels, pack(): pl.pallas_call(pack_kernel, grid_spec=pltpu.PrefetchScalarGridSpec(num_sc...  8.32 us
    all_to_all x1, waiting for transfers between devices, on_device(): lax.all_to_all(send, GROUP, split_axis=0, concat_axis=0, tiled=True)  7.45 us
  transfers between devices with their start and end apart: 36, of which 14 were waited for; matrix products, arithmetic and copies ran while one was open for 10% of the time, Pallas kernels for 6%

profile of v2, /device:TPU:0, one launch (start us, length us, event | category | flops | bytes accessed | tf_op | source)
XLA Modules:
  0.0 297.6 jit_solution(11681718715239123471)
XLA Ops:
  7.2 1.3 select_reduce_fusion.2
  9.8 0.8 copy.31
  11.9 0.8 select_reduce_fusion
  13.6 1.2 fusion.2
  14.9 1.0 pad_maximum_fusion
  15.9 7.0 %all-to-all-start = ((bf16[8,16,4096]{2,1,0:T(8,128)(2,1)}), bf16[8,16,4096]{2,1,0:T(8,128)(2,1)S(1)}, u32[]{:S(2)}, u32[]{:S(2)}) async-start(bf16[8,16,4096]{2,1,0:T(8,128)(2,1)} %pad_maximum_fusion), calls=%async_computation | async-start | bytes 2097152 | tf_op jit(solution)/shard_map/all_to_all | solution.py:274
  23.0 8.3 %shard_map.170 = bf16[8,1152,256]{2,1,0:T(8,128)(2,1)} custom-call(s32[2]{0:T(128)} %pad_add_fusion.at, f32[2048,256]{1,0:T(8,128)} %bitcast.73, f32[2048,256]{1,0:T(8,128)} %bitcast.75, bf16[4096,256]{1,0:T(8,128)(2,1)} %bitcast.69, f32[64,4096]{1,0:T(8,128)} %bitcast.77, f32[64,4096]{1,0:T(8,128)} %bitcast.79, bf16[128,4096]{1,0:T(8,128)(2,1)} %bitcast.71), custom_call_target="tpu_custom_call" | custom-call | flops 4194304 | bytes 25165824 | tf_op jit(solution)/shard_map/pallas_call | solution.py:80
  32.7 7.5 %all-to-all-done = bf16[8,16,4096]{2,1,0:T(8,128)(2,1)S(1)} async-done(((bf16[8,16,4096]{2,1,0:T(8,128)(2,1)}), bf16[8,16,4096]{2,1,0:T(8,128)(2,1)S(1)}, u32[]{:S(2)}, u32[]{:S(2)}) %all-to-all-start) | async-done | bytes 1048608 | tf_op jit(solution)/shard_map/all_to_all | solution.py:274
  40.2 2.0 collective-permute-start.43
  42.8 1.4 collective-permute-start.50
  44.5 10.7 %collective-permute-done.43 = bf16[64,4096]{1,0:T(8,128)(2,1)S(1)} collective-permute-done((bf16[64,4096]{1,0:T(8,128)(2,1)S(1)}, bf16[64,4096]{1,0:T(8,128)(2,1)S(1)}, u32[]{:S(2)}, u32[]{:S(2)}) %collective-permute-start.43) | collective-permute-done | bytes 524320 | tf_op jit(solution)/shard_map/ppermute | solution.py:160
  55.2 7.6 %collective-permute-done.42 = bf16[64,4096]{1,0:T(8,128)(2,1)S(1)} collective-permute-done((bf16[64,4096]{1,0:T(8,128)(2,1)S(1)}, bf16[64,4096]{1,0:T(8,128)(2,1)S(1)}, u32[]{:S(2)}, u32[]{:S(2)}) %collective-permute-start.42) | collective-permute-done | bytes 524320 | tf_op jit(solution)/shard_map/ppermute | solution.py:160
  63.7 2.0 collective-permute-done.45
  66.4 17.2 %collective-permute-done.46 = bf16[32,4096]{1,0:T(8,128)(2,1)S(1)} collective-permute-done((bf16[32,4096]{1,0:T(8,128)(2,1)S(1)}, bf16[32,4096]{1,0:T(8,128)(2,1)S(1)}, u32[]{:S(2)}, u32[]{:S(2)}) %collective-permute-start.46) | collective-permute-done | bytes 262176 | tf_op jit(solution)/shard_map/ppermute | solution.py:160
  85.6 11.9 %collective-permute-done.54 = bf16[32,4096]{1,0:T(8,128)(2,1)S(1)} collective-permute-done((bf16[32,4096]{1,0:T(8,128)(2,1)S(1)}, bf16[32,4096]{1,0:T(8,128)(2,1)S(1)}, u32[]{:S(2)}, u32[]{:S(2)}) %collective-permute-start.54) | collective-permute-done | bytes 262176 | tf_op jit(solution)/shard_map/ppermute | solution.py:160
  97.9 1.3 convolution_multiply_fusion.4
  100.5 1.6 multiply_multiply_fusion
  102.1 0.8 convolution_multiply_fusion
  102.9 1.3 multiply_convert_fusion
  104.2 1.3 fusion.25
  105.6 3.3 %collective-permute-start.57 = (bf16[2048,256]{1,0:T(8,128)(2,1)S(1)}, bf16[2048,256]{1,0:T(8,128)(2,1)S(1)}, u32[]{:S(2)}, u32[]{:S(2)}) collective-permute-start(bf16[2048,256]{1,0:T(8,128)(2,1)S(1)} %dynamic-slice_convert_fusion), channel_id=1, source_target_pairs={{0,64},{64,0},{1,65},{65,1},{2,66},{66,2},{3,67},{67,3},{4,68},{68... | collective-permute-start | bytes 3145736 | tf_op jit(solution)/shard_map/ppermute | solution.py:160
  109.6 0.9 fusion.37
  110.9 1.3 convolution_convert_fusion
  112.4 1.1 fusion.38
  113.6 0.8 collective-permute-start.63
  114.5 0.7 fusion.42
  116.5 27.5 %collective-permute-done.58 = bf16[64,4096]{1,0:T(8,128)(2,1)S(1)} collective-permute-done((bf16[64,4096]{1,0:T(8,128)(2,1)S(1)}, bf16[64,4096]{1,0:T(8,128)(2,1)S(1)}, u32[]{:S(2)}, u32[]{:S(2)}) %collective-permute-start.58) | collective-permute-done | bytes 524320 | tf_op jit(solution)/shard_map/ppermute | solution.py:160
  144.0 0.9 collective-permute-start.61
  144.9 1.1 convert_add_fusion.7.grad_out
  146.0 0.8 fusion.41
  146.8 0.8 collective-permute-start.66
  147.6 1.5 convert_add_fusion.2.grad_in
  149.1 0.8 collective-permute-start.64
  149.9 2.0 fusion.35
  151.9 2.0 fusion.36
  153.9 1.2 fusion.40
  155.2 1.1 fusion.39
  156.3 1.6 fusion.10
  158.0 1.1 fusion.9
  159.2 76.2 %conditional.4 = (bf16[2048,256]{1,0:T(8,128)(2,1)}, bf16[64,4096]{1,0:T(8,128)(2,1)}, bf16[64,4096]{1,0:T(8,128)(2,1)}, bf16[64,4096]{1,0:T(8,128)(2,1)}, bf16[...) conditional(s32[]{:T(128)} %clamp.3, (f32[2048,256]{1,0:T(8,128)S(1)}, ...), branch_computations={%region_7.8_spmd, %region_8.9_spmd, %region_9.10_spmd, %region_10.... | conditional | flops 786432 | bytes 19398944
  159.3 4.3 %collective-permute-start.37 = (bf16[64,4096]{1,0:T(8,128)(2,1)S(1)}, bf16[64,4096]{1,0:T(8,128)(2,1)}, u32[]{:S(2)}, u32[]{:S(2)}) collective-permute-start(bf16[64,4096]{1,0:T(8,128)(2,1)S(1)} %convert_element_type.188), channel_id=1, source_target_pairs={{0,56},{1,57},{2,58},{3,59},{4,60},{5,61},{6,62},{7,63},{8,48},{9,... | collective-permute-start | bytes 1572872 | tf_op jit(solution)/shard_map/cond/branch_6_fun/ppermute | solution.py:212
  163.8 1.5 collective-permute-start.36
  165.2 1.5 collective-permute-start.38
  166.8 0.9 collective-permute-start.40
  167.7 0.8 collective-permute-start.39
  168.5 15.9 %collective-permute-done.37 = bf16[64,4096]{1,0:T(8,128)(2,1)} collective-permute-done((bf16[64,4096]{1,0:T(8,128)(2,1)S(1)}, bf16[64,4096]{1,0:T(8,128)(2,1)}, u32[]{:S(2)}, u32[]{:S(2)}) %collective-permute-start.37) | collective-permute-done | bytes 524320 | tf_op jit(solution)/shard_map/cond/branch_6_fun/ppermute | solution.py:212
  184.4 1.2 collective-permute-start.41
  185.6 31.5 %collective-permute-done.38 = bf16[64,4096]{1,0:T(8,128)(2,1)} collective-permute-done((bf16[64,4096]{1,0:T(8,128)(2,1)S(1)}, bf16[64,4096]{1,0:T(8,128)(2,1)}, u32[]{:S(2)}, u32[]{:S(2)}) %collective-permute-start.38) | collective-permute-done | bytes 524320 | tf_op jit(solution)/shard_map/cond/branch_6_fun/ppermute | solution.py:160
  217.1 18.3 %collective-permute-done.39 = bf16[64,4096]{1,0:T(8,128)(2,1)} collective-permute-done((bf16[64,4096]{1,0:T(8,128)(2,1)S(1)}, bf16[64,4096]{1,0:T(8,128)(2,1)}, u32[]{:S(2)}, u32[]{:S(2)}) %collective-permute-start.39) | collective-permute-done | bytes 524320 | tf_op jit(solution)/shard_map/cond/branch_6_fun/ppermute | solution.py:160
  235.9 1.6 collective-permute-done.67
  237.5 1.6 fusion.8
  239.2 1.7 fusion.7
  240.8 1.1 pad_maximum_fusion.3
  241.9 4.3 %all-to-all-start.1 = ((bf16[8,16,4096]{2,1,0:T(8,128)(2,1)}), bf16[8,16,4096]{2,1,0:T(8,128)(2,1)}, u32[]{:S(2)}, u32[]{:S(2)}) async-start(bf16[8,16,4096]{2,1,0:T(8,128)(2,1)} %pad_maximum_fusion.3), calls=%async_computation.2 | async-start | bytes 2097152 | tf_op jit(solution)/shard_map/all_to_all | solution.py:328
  246.2 22.5 %all-gather.2.cloned.1.call-done.packed = bf16[8,1152,256]{2,1,0:T(8,128)(2,1)} async-done(((bf16[1,1152,256]{2,1,0:T(8,128)(2,1)}), bf16[8,1152,256]{2,1,0:T(8,128)(2,1)}) %all-gather.2.cloned.1.call-update) | async-done | bytes 4718608 | tf_op jit(solution)/shard_map/all_gather | solution.py:306
  268.7 1.6 copy-done.4
  270.3 1.6 copy-done.5
  271.9 2.3 copy-done.6
  274.2 1.2 copy-done.7
  275.4 1.2 copy-done.8
  276.6 9.1 %shard_map.171 = (bf16[2048,256]{1,0:T(8,128)(2,1)}, f32[2048,256]{1,0:T(8,128)}, f32[2048,256]{1,0:T(8,128)}, bf16[64,4096]{1,0:T(8,128)(2,1)}, f32[64,4096]{1,0:T(8,128)}, /*index=5*/f32[64,4096]{1,0:T(8,128)}) custom-call(s32[2]{0:T(128)S(1)} %copy-done.9, bf16[8,1152,256]{2,1,0:T(8,128)(2,1)S(1)} %copy-done.6, f32[2048,256]{1,0:T(8,128)S(1)} %bitcast.74, ...), custom_call_target="tpu_custom_call" | custom-call | flops 16777216 | bytes 31457280 | tf_op jit(solution)/shard_map/pallas_call | solution.py:140
  285.8 1.9 convolution_convert_fusion.2
  287.6 1.2 convolution_multiply_fusion.3
  288.9 1.9 fusion.4
  (118 shorter events, 12.0 us)
Async XLA Ops:
  7.2 6.1 %copy-start = (bf16[16,4096]{1,0:T(8,128)(2,1)S(1)}, bf16[16,4096]{1,0:T(8,128)(2,1)}, u32[]{:S(2)}) copy-start(bf16[16,4096]{1,0:T(8,128)(2,1)} %param.18) | copy-start | bytes 393220
  15.9 24.2 %all-to-all-start = ((bf16[8,16,4096]{2,1,0:T(8,128)(2,1)}), bf16[8,16,4096]{2,1,0:T(8,128)(2,1)S(1)}, u32[]{:S(2)}, u32[]{:S(2)}) async-start(bf16[8,16,4096]{2,1,0:T(8,128)(2,1)} %pad_maximum_fusion), calls=%async_computation | async-start | bytes 2097152 | tf_op jit(solution)/shard_map/all_to_all | solution.py:274
  23.0 130.9 %reduce-scatter.2.cloned.1.call-start = ((), (), s32[]{:S(2)}) async-start(), calls=%async_computation.3 | async-start | bytes 5308416 | tf_op jit(solution)/shard_map/reduce_scatter | solution.py:273
  31.4 237.3 %all-gather.2.cloned.1.call-start = ((), (), s32[]{:S(2)}) async-start(), calls=%async_computation.4 | async-start | bytes 5308416 | tf_op jit(solution)/shard_map/all_gather | solution.py:306
  40.2 14.9 %collective-permute-start.43 = (bf16[64,4096]{1,0:T(8,128)(2,1)S(1)}, bf16[64,4096]{1,0:T(8,128)(2,1)S(1)}, u32[]{:S(2)}, u32[]{:S(2)}) collective-permute-start(bf16[64,4096]{1,0:T(8,128)(2,1)S(1)} %get-tuple-element.251), channel_id=1, source_target_pairs={{0,2},{2,0},{1,3},{3,1},{4,6},{6,4},{5,7},{7,5},{8,10},{10,8},{9,1... | collective-permute-start | bytes 1572872 | tf_op jit(solution)/shard_map/ppermute | solution.py:160
  42.2 20.6 %collective-permute-start.42 = (bf16[64,4096]{1,0:T(8,128)(2,1)S(1)}, bf16[64,4096]{1,0:T(8,128)(2,1)S(1)}, u32[]{:S(2)}, u32[]{:S(2)}) collective-permute-start(bf16[64,4096]{1,0:T(8,128)(2,1)S(1)} %get-tuple-element.251), channel_id=1, source_target_pairs={{0,4},{4,0},{1,5},{5,1},{2,6},{6,2},{3,7},{7,3},{8,12},{12,8},{9,1... | collective-permute-start | bytes 1572872 | tf_op jit(solution)/shard_map/ppermute | solution.py:160
  42.8 20.3 %collective-permute-start.44 = (bf16[64,4096]{1,0:T(8,128)(2,1)S(1)}, bf16[64,4096]{1,0:T(8,128)(2,1)S(1)}, u32[]{:S(2)}, u32[]{:S(2)}) collective-permute-start(bf16[64,4096]{1,0:T(8,128)(2,1)S(1)} %get-tuple-element.251), channel_id=1, source_target_pairs={{0,1},{1,0},{2,3},{3,2},{4,5},{5,4},{6,7},{7,6},{8,9},{9,8},{10,11... | collective-permute-start | bytes 1572872 | tf_op jit(solution)/shard_map/ppermute | solution.py:160
  42.8 41.0 %collective-permute-start.50 = (bf16[64,4096]{1,0:T(8,128)(2,1)S(1)}, bf16[64,4096]{1,0:T(8,128)(2,1)S(1)}, u32[]{:S(2)}, u32[]{:S(2)}) collective-permute-start(bf16[64,4096]{1,0:T(8,128)(2,1)S(1)} %get-tuple-element.250), channel_id=1, source_target_pairs={{0,4},{4,0},{1,5},{5,1},{2,6},{6,2},{3,7},{7,3},{8,12},{12,8},{9,1... | collective-permute-start | bytes 1572872 | tf_op jit(solution)/shard_map/ppermute | solution.py:160
  44.3 39.6 %collective-permute-start.51 = (bf16[64,4096]{1,0:T(8,128)(2,1)S(1)}, bf16[64,4096]{1,0:T(8,128)(2,1)S(1)}, u32[]{:S(2)}, u32[]{:S(2)}) collective-permute-start(bf16[64,4096]{1,0:T(8,128)(2,1)S(1)} %get-tuple-element.250), channel_id=1, source_target_pairs={{0,2},{2,0},{1,3},{3,1},{4,6},{6,4},{5,7},{7,5},{8,10},{10,8},{9,1... | collective-permute-start | bytes 1572872 | tf_op jit(solution)/shard_map/ppermute | solution.py:160
  55.2 30.4 %collective-permute-start.52 = (bf16[64,4096]{1,0:T(8,128)(2,1)S(1)}, bf16[64,4096]{1,0:T(8,128)(2,1)S(1)}, u32[]{:S(2)}, u32[]{:S(2)}) collective-permute-start(bf16[64,4096]{1,0:T(8,128)(2,1)S(1)} %get-tuple-element.250), channel_id=1, source_target_pairs={{0,1},{1,0},{2,3},{3,2},{4,5},{5,4},{6,7},{7,6},{8,9},{9,8},{10,11... | collective-permute-start | bytes 1572872 | tf_op jit(solution)/shard_map/ppermute | solution.py:160
  62.9 2.7 collective-permute-start.45
  63.2 20.5 %collective-permute-start.46 = (bf16[32,4096]{1,0:T(8,128)(2,1)S(1)}, bf16[32,4096]{1,0:T(8,128)(2,1)S(1)}, u32[]{:S(2)}, u32[]{:S(2)}) collective-permute-start(bf16[32,4096]{1,0:T(8,128)(2,1)S(1)} %slice.170), channel_id=1, source_target_pairs={{0,4},{4,0},{1,5},{5,1},{2,6},{6,2},{3,7},{7,3},{8,12},{12,8},{9,1... | collective-permute-start | bytes 786440 | tf_op jit(solution)/shard_map/ppermute | solution.py:160
  65.6 18.0 %collective-permute-start.47 = (bf16[32,4096]{1,0:T(8,128)(2,1)S(1)}, bf16[32,4096]{1,0:T(8,128)(2,1)S(1)}, u32[]{:S(2)}, u32[]{:S(2)}) collective-permute-start(bf16[32,4096]{1,0:T(8,128)(2,1)S(1)} %slice.171), channel_id=1, source_target_pairs={{0,2},{2,0},{1,3},{3,1},{4,6},{6,4},{5,7},{7,5},{8,10},{10,8},{9,1... | collective-permute-start | bytes 786440 | tf_op jit(solution)/shard_map/ppermute | solution.py:160
  83.7 14.2 %copy-start.2 = (bf16[1,4096,256]{2,1,0:T(8,128)(2,1)S(1)}, bf16[1,4096,256]{2,1,0:T(8,128)(2,1)}, u32[]{:S(2)}) copy-start(bf16[1,4096,256]{2,1,0:T(8,128)(2,1)} %param.23) | copy-start | bytes 6291460
  83.7 14.1 %collective-permute-start.48 = (bf16[64,4096]{1,0:T(8,128)(2,1)S(1)}, bf16[64,4096]{1,0:T(8,128)(2,1)S(1)}, u32[]{:S(2)}, u32[]{:S(2)}) collective-permute-start(bf16[64,4096]{1,0:T(8,128)(2,1)S(1)} %get-tuple-element.261), channel_id=1, source_target_pairs={{0,1},{1,0},{2,3},{3,2},{4,5},{5,4},{6,7},{7,6},{8,9},{9,8},{10,11... | collective-permute-start | bytes 1572872 | tf_op jit(solution)/shard_map/ppermute | solution.py:160
  84.0 15.2 %collective-permute-start.53 = (bf16[128,4096]{1,0:T(8,128)(2,1)S(1)}, bf16[128,4096]{1,0:T(8,128)(2,1)S(1)}, u32[]{:S(2)}, u32[]{:S(2)}) collective-permute-start(bf16[128,4096]{1,0:T(8,128)(2,1)S(1)} %pad_maximum_fusion.2), channel_id=1, source_target_pairs={{0,1},{1,0},{2,3},{3,2},{4,5},{5,4},{6,7},{7,6},{8,9},{9,8},{10,11... | collective-permute-start | bytes 3145736 | tf_op jit(solution)/shard_map/ppermute | solution.py:160
  84.6 13.0 %collective-permute-start.54 = (bf16[32,4096]{1,0:T(8,128)(2,1)S(1)}, bf16[32,4096]{1,0:T(8,128)(2,1)S(1)}, u32[]{:S(2)}, u32[]{:S(2)}) collective-permute-start(bf16[32,4096]{1,0:T(8,128)(2,1)S(1)} %slice.140), channel_id=1, source_target_pairs={{0,4},{4,0},{1,5},{5,1},{2,6},{6,2},{3,7},{7,3},{8,12},{12,8},{9,1... | collective-permute-start | bytes 786440 | tf_op jit(solution)/shard_map/ppermute | solution.py:160
  85.2 12.4 %collective-permute-start.55 = (bf16[32,4096]{1,0:T(8,128)(2,1)S(1)}, bf16[32,4096]{1,0:T(8,128)(2,1)S(1)}, u32[]{:S(2)}, u32[]{:S(2)}) collective-permute-start(bf16[32,4096]{1,0:T(8,128)(2,1)S(1)} %slice.141), channel_id=1, source_target_pairs={{0,2},{2,0},{1,3},{3,1},{4,6},{6,4},{5,7},{7,5},{8,10},{10,8},{9,1... | collective-permute-start | bytes 786440 | tf_op jit(solution)/shard_map/ppermute | solution.py:160
  97.6 2.2 collective-permute-start.56
  99.2 1.2 copy-start.3
  104.2 45.8 %copy-start.12 = (bf16[512,4096]{1,0:T(8,128)(2,1)}, bf16[512,4096]{1,0:T(8,128)(2,1)S(1)}, u32[]{:S(2)}) copy-start(bf16[512,4096]{1,0:T(8,128)(2,1)S(1)} %multiply_convert_fusion) | copy-start | bytes 12582916
  105.6 41.2 %collective-permute-start.57 = (bf16[2048,256]{1,0:T(8,128)(2,1)S(1)}, bf16[2048,256]{1,0:T(8,128)(2,1)S(1)}, u32[]{:S(2)}, u32[]{:S(2)}) collective-permute-start(bf16[2048,256]{1,0:T(8,128)(2,1)S(1)} %dynamic-slice_convert_fusion), channel_id=1, source_target_pairs={{0,64},{64,0},{1,65},{65,1},{2,66},{66,2},{3,67},{67,3},{4,68},{68... | collective-permute-start | bytes 3145736 | tf_op jit(solution)/shard_map/ppermute | solution.py:160
  109.0 35.0 %collective-permute-start.58 = (bf16[64,4096]{1,0:T(8,128)(2,1)S(1)}, bf16[64,4096]{1,0:T(8,128)(2,1)S(1)}, u32[]{:S(2)}, u32[]{:S(2)}) collective-permute-start(bf16[64,4096]{1,0:T(8,128)(2,1)S(1)} %dynamic-slice_convert_fusion.1), channel_id=1, source_target_pairs={{0,64},{64,0},{1,65},{65,1},{2,66},{66,2},{3,67},{67,3},{4,68},{68... | collective-permute-start | bytes 1572872 | tf_op jit(solution)/shard_map/ppermute | solution.py:160
  109.5 39.6 %collective-permute-start.59 = (bf16[128,4096]{1,0:T(8,128)(2,1)S(1)}, bf16[128,4096]{1,0:T(8,128)(2,1)S(1)}, u32[]{:S(2)}, u32[]{:S(2)}) collective-permute-start(bf16[128,4096]{1,0:T(8,128)(2,1)S(1)} %slice.178), channel_id=1, source_target_pairs={{0,1},{1,0},{2,3},{3,2},{4,5},{5,4},{6,7},{7,6},{8,9},{9,8},{10,11... | collective-permute-start | bytes 3145736 | tf_op jit(solution)/shard_map/ppermute | solution.py:160
  110.4 3.1 %collective-permute-start.60 = (bf16[64,4096]{1,0:T(8,128)(2,1)S(1)}, bf16[64,4096]{1,0:T(8,128)(2,1)S(1)}, u32[]{:S(2)}, u32[]{:S(2)}) collective-permute-start(bf16[64,4096]{1,0:T(8,128)(2,1)S(1)} %get-tuple-element.239), channel_id=1, source_target_pairs={{0,1},{1,0},{2,3},{3,2},{4,5},{5,4},{6,7},{7,6},{8,9},{9,8},{10,11... | collective-permute-start | bytes 1572872 | tf_op jit(solution)/shard_map/ppermute | solution.py:160
  112.3 39.7 %copy-start.13 = (bf16[512,4096]{1,0:T(8,128)(2,1)}, bf16[512,4096]{1,0:T(8,128)(2,1)S(1)}, u32[]{:S(2)}) copy-start(bf16[512,4096]{1,0:T(8,128)(2,1)S(1)} %convolution_convert_fusion) | copy-start | bytes 12582916
  112.3 39.6 %collective-permute-start.62 = (bf16[128,4096]{1,0:T(8,128)(2,1)S(1)}, bf16[128,4096]{1,0:T(8,128)(2,1)S(1)}, u32[]{:S(2)}, u32[]{:S(2)}) collective-permute-start(bf16[128,4096]{1,0:T(8,128)(2,1)S(1)} %slice.185), channel_id=1, source_target_pairs={{0,1},{1,0},{2,3},{3,2},{4,5},{5,4},{6,7},{7,6},{8,9},{9,8},{10,11... | collective-permute-start | bytes 3145736 | tf_op jit(solution)/shard_map/ppermute | solution.py:160
  113.6 2.4 collective-permute-start.63
  115.9 40.3 %collective-permute-start.65 = (bf16[32,4096]{1,0:T(8,128)(2,1)}, bf16[32,4096]{1,0:T(8,128)(2,1)}, u32[]{:S(2)}, u32[]{:S(2)}) collective-permute-start(bf16[32,4096]{1,0:T(8,128)(2,1)} %get-tuple-element.258), channel_id=1, source_target_pairs={{0,4},{4,0},{1,5},{5,1},{2,6},{6,2},{3,7},{7,3},{8,12},{12,8},{9,1... | collective-permute-start | bytes 786440 | tf_op jit(solution)/shard_map/ppermute | solution.py:160
  144.0 12.2 %collective-permute-start.61 = (bf16[32,4096]{1,0:T(8,128)(2,1)S(1)}, bf16[32,4096]{1,0:T(8,128)(2,1)}, u32[]{:S(2)}, u32[]{:S(2)}) collective-permute-start(bf16[32,4096]{1,0:T(8,128)(2,1)S(1)} %get-tuple-element.259), channel_id=1, source_target_pairs={{0,2},{2,0},{1,3},{3,1},{4,6},{6,4},{5,7},{7,5},{8,10},{10,8},{9,1... | collective-permute-start | bytes 786440 | tf_op jit(solution)/shard_map/ppermute | solution.py:160
  146.8 11.1 %collective-permute-start.66 = (bf16[32,4096]{1,0:T(8,128)(2,1)}, bf16[32,4096]{1,0:T(8,128)(2,1)}, u32[]{:S(2)}, u32[]{:S(2)}) collective-permute-start(bf16[32,4096]{1,0:T(8,128)(2,1)} %get-tuple-element.256), channel_id=1, source_target_pairs={{0,4},{4,0},{1,5},{5,1},{2,6},{6,2},{3,7},{7,3},{8,12},{12,8},{9,1... | collective-permute-start | bytes 786440 | tf_op jit(solution)/shard_map/ppermute | solution.py:160
  149.1 8.9 %collective-permute-start.64 = (bf16[32,4096]{1,0:T(8,128)(2,1)}, bf16[32,4096]{1,0:T(8,128)(2,1)}, u32[]{:S(2)}, u32[]{:S(2)}) collective-permute-start(bf16[32,4096]{1,0:T(8,128)(2,1)} %get-tuple-element.257), channel_id=1, source_target_pairs={{0,2},{2,0},{1,3},{3,1},{4,6},{6,4},{5,7},{7,5},{8,10},{10,8},{9,1... | collective-permute-start | bytes 786440 | tf_op jit(solution)/shard_map/ppermute | solution.py:160
  153.9 4.1 %copy-start.14 = (f32[128,4096]{1,0:T(8,128)S(1)}, f32[128,4096]{1,0:T(8,128)}, u32[]{:S(2)}) copy-start(f32[128,4096]{1,0:T(8,128)} %get-tuple-element.235) | copy-start | bytes 6291460
  156.2 3.0 copy-start.10
  156.3 3.0 copy-start.11
  159.3 25.0 %collective-permute-start.37 = (bf16[64,4096]{1,0:T(8,128)(2,1)S(1)}, bf16[64,4096]{1,0:T(8,128)(2,1)}, u32[]{:S(2)}, u32[]{:S(2)}) collective-permute-start(bf16[64,4096]{1,0:T(8,128)(2,1)S(1)} %convert_element_type.188), channel_id=1, source_target_pairs={{0,56},{1,57},{2,58},{3,59},{4,60},{5,61},{6,62},{7,63},{8,48},{9,... | collective-permute-start | bytes 1572872 | tf_op jit(solution)/shard_map/cond/branch_6_fun/ppermute | solution.py:212
  163.8 71.6 %collective-permute-start.36 = (bf16[2048,256]{1,0:T(8,128)(2,1)S(1)}, bf16[2048,256]{1,0:T(8,128)(2,1)}, u32[]{:S(2)}, u32[]{:S(2)}) collective-permute-start(bf16[2048,256]{1,0:T(8,128)(2,1)S(1)} %convert_element_type.187), channel_id=1, source_target_pairs={{0,56},{1,57},{2,58},{3,59},{4,60},{5,61},{6,62},{7,63},{8,48},{9,... | collective-permute-start | bytes 3145736 | tf_op jit(solution)/shard_map/cond/branch_6_fun/ppermute | solution.py:212
  165.2 51.8 %collective-permute-start.38 = (bf16[64,4096]{1,0:T(8,128)(2,1)S(1)}, bf16[64,4096]{1,0:T(8,128)(2,1)}, u32[]{:S(2)}, u32[]{:S(2)}) collective-permute-start(bf16[64,4096]{1,0:T(8,128)(2,1)S(1)} %get-tuple-element.164), channel_id=1, source_target_pairs={{0,4},{4,0},{1,5},{5,1},{2,6},{6,2},{3,7},{7,3},{8,12},{12,8},{9,1... | collective-permute-start | bytes 1572872 | tf_op jit(solution)/shard_map/cond/branch_6_fun/ppermute | solution.py:160
  166.8 50.3 %collective-permute-start.40 = (bf16[64,4096]{1,0:T(8,128)(2,1)S(1)}, bf16[64,4096]{1,0:T(8,128)(2,1)}, u32[]{:S(2)}, u32[]{:S(2)}) collective-permute-start(bf16[64,4096]{1,0:T(8,128)(2,1)S(1)} %get-tuple-element.166), channel_id=1, source_target_pairs={{0,2},{2,0},{1,3},{3,1},{4,6},{6,4},{5,7},{7,5},{8,10},{10,8},{9,1... | collective-permute-start | bytes 1572872 | tf_op jit(solution)/shard_map/cond/branch_6_fun/ppermute | solution.py:160
  167.7 67.7 %collective-permute-start.39 = (bf16[64,4096]{1,0:T(8,128)(2,1)S(1)}, bf16[64,4096]{1,0:T(8,128)(2,1)}, u32[]{:S(2)}, u32[]{:S(2)}) collective-permute-start(bf16[64,4096]{1,0:T(8,128)(2,1)S(1)} %get-tuple-element.165), channel_id=1, source_target_pairs={{0,4},{4,0},{1,5},{5,1},{2,6},{6,2},{3,7},{7,3},{8,12},{12,8},{9,1... | collective-permute-start | bytes 1572872 | tf_op jit(solution)/shard_map/cond/branch_6_fun/ppermute | solution.py:160
  184.4 51.0 %collective-permute-start.41 = (bf16[64,4096]{1,0:T(8,128)(2,1)S(1)}, bf16[64,4096]{1,0:T(8,128)(2,1)}, u32[]{:S(2)}, u32[]{:S(2)}) collective-permute-start(bf16[64,4096]{1,0:T(8,128)(2,1)S(1)} %get-tuple-element.167), channel_id=1, source_target_pairs={{0,2},{2,0},{1,3},{3,1},{4,6},{6,4},{5,7},{7,5},{8,10},{10,8},{9,1... | collective-permute-start | bytes 1572872 | tf_op jit(solution)/shard_map/cond/branch_6_fun/ppermute | solution.py:160
  235.4 2.1 collective-permute-start.67
  235.4 3.8 %collective-permute-start.49 = (bf16[64,4096]{1,0:T(8,128)(2,1)}, bf16[64,4096]{1,0:T(8,128)(2,1)S(1)}, u32[]{:S(2)}, u32[]{:S(2)}) collective-permute-start(bf16[64,4096]{1,0:T(8,128)(2,1)} %get-tuple-element.238), channel_id=1, source_target_pairs={{0,1},{1,0},{2,3},{3,2},{4,5},{5,4},{6,7},{7,6},{8,9},{9,8},{10,11... | collective-permute-start | bytes 1572872 | tf_op jit(solution)/shard_map/ppermute | solution.py:160
  237.5 8.7 %copy-start.15 = (f32[16,2]{0,1:T(2,128)S(1)}, f32[16,2]{0,1:T(2,128)}, u32[]{:S(2)}) copy-start(f32[16,2]{0,1:T(2,128)} %param.21) | copy-start | bytes 388
  237.5 31.1 %copy-start.9 = (s32[2]{0:T(128)S(1)}, s32[2]{0:T(128)}, u32[]{:S(2)}) copy-start(s32[2]{0:T(128)} %pad_add_fusion.at) | copy-start | bytes 28
  241.9 43.8 %all-to-all-start.1 = ((bf16[8,16,4096]{2,1,0:T(8,128)(2,1)}), bf16[8,16,4096]{2,1,0:T(8,128)(2,1)}, u32[]{:S(2)}, u32[]{:S(2)}) async-start(bf16[8,16,4096]{2,1,0:T(8,128)(2,1)} %pad_maximum_fusion.3), calls=%async_computation.2 | async-start | bytes 2097152 | tf_op jit(solution)/shard_map/all_to_all | solution.py:328
  268.7 1.6 copy-start.4
  270.3 1.6 copy-start.5
  271.9 2.3 copy-start.6
  274.2 1.2 copy-start.7
  275.4 1.2 copy-start.8
  276.6 14.1 %copy-start.1 = (bf16[16,4096]{1,0:T(8,128)(2,1)S(1)}, bf16[16,4096]{1,0:T(8,128)(2,1)}, u32[]{:S(2)}) copy-start(bf16[16,4096]{1,0:T(8,128)(2,1)} %param.18) | copy-start | bytes 393220
Sparse Core Ops, SparseCore 0:
  31.5 110.0 reduce-scatter.1
  154.0 114.5 all-gather.1

commit v3 on v2

--- a/solution.py
+++ b/solution.py
@@ -113,9 +113,11 @@
     lanes = first_in.shape[1]
     inner, outer = sections(first_in.shape[0], first_out.shape[0], lanes, first_out.shape[1])
     moved = at[1] == 1
+    one_column = at[2] == 1
 
     def placed(rows, stayed):
-        came = packed[0, rows, :].astype(jnp.float32) - stayed.astype(half_type).astype(jnp.float32)
+        came = packed[0, rows, :].astype(jnp.float32)
+        came = came - jnp.where(one_column, stayed.astype(half_type).astype(jnp.float32), 0.0)
         return jnp.where(moved, came, stayed.astype(jnp.float32))
 
     new_weight_in[...], new_first_in[...], new_second_in[...] = adam_step(
@@ -152,7 +154,7 @@
             for dtype in (jnp.bfloat16, jnp.float32, jnp.float32)
         ],
         cost_estimate=pl.CostEstimate(flops=16 << 20, bytes_accessed=30 << 20, transcendentals=1 << 20),
-        compiler_params=pltpu.CompilerParams(vmem_limit_bytes=24 * 1024 * 1024),
+        compiler_params=pltpu.CompilerParams(vmem_limit_bytes=52 * 1024 * 1024),
     )(at, packed, states[0], states[1], slot_in, states[2], states[3], slot_out, grad_in, grad_out, late_in, late_out)
 
 
@@ -190,31 +192,27 @@
     return [jnp.concatenate(parts) for parts in gathered]
 
 
-def reduce_start(array, share):
+def reduce_start(array):
     rows = array.shape[0] // 8
     piece = lambda start, count=1: array[start * rows : (start + count) * rows]
-    cut = split_at(rows, share)
     diag = (piece(6).astype(jnp.float32) + flip(piece(7), "c").astype(jnp.float32)).astype(half_type)
     sides = piece(1, 2).astype(jnp.float32) + flip(piece(4, 2), "c").astype(jnp.float32)
     own = piece(0).astype(jnp.float32) + flip(piece(3), "c").astype(jnp.float32)
+    return own, sides, diag
+
+
+def reduce_turn(sides, via_x, via_z):
+    rows = sides.shape[0] // 2
+    cut = via_x.shape[0]
     to_x, to_z = sides[:rows], sides[rows:]
-    if cut:
-        via_x = flip(diag[:cut], "xl").astype(jnp.float32)
-        to_z = jnp.concatenate([to_z[:cut] + via_x, to_z[cut:]])
-    if cut < rows:
-        via_z = flip(diag[cut:], "z").astype(jnp.float32)
-        to_x = jnp.concatenate([to_x[:cut], to_x[cut:] + via_z])
-    return own, to_x.astype(half_type), to_z.astype(half_type)
+    to_z = jnp.concatenate([to_z[:cut] + via_x.astype(jnp.float32), to_z[cut:]])
+    to_x = jnp.concatenate([to_x[:cut], to_x[cut:] + via_z.astype(jnp.float32)])
+    return to_x.astype(half_type), to_z.astype(half_type)
 
 
 def exchange(values, distance):
     pairs = [(slot, slot ^ (distance * 8)) for slot in range(64)]
     return tuple(lax.ppermute(value, PARTS, pairs) for value in values)
-
-
-def late_steps(values, rows_to_x, rows_to_z, distance):
-    moved = exchange(values, distance)
-    return moved, tuple(flip(rows, "xl") for rows in rows_to_x), tuple(flip(rows, "z") for rows in rows_to_z)
 
 
 def on_device(
@@ -244,13 +242,14 @@
     low = jnp.min(jnp.where(changed, columns, groups - 1))
     high = jnp.max(jnp.where(changed, columns, 0))
     case = jnp.clip((low ^ high) - 1, 0, 6)
+    one_column = (low % 2) == (high % 2)
     moved = (my_expert == low) | (my_expert == high)
     slot_in = weight_in[0]
     slot_out = weight_out[0]
     states = (first_in[0], second_in[0], first_out[0], second_out[0])
     rows_in_half = first_in.shape[1]
     rows_out_half = first_out.shape[1]
-    at = jnp.stack([data_half, moved]).astype(jnp.int32)
+    at = jnp.stack([data_half, moved, one_column]).astype(jnp.int32)
 
     flat_ids = expert_ids.reshape(routed)
     onehot = (flat_ids[:, None] == columns[None, :]).astype(jnp.int32)
@@ -270,7 +269,7 @@
         [group_inputs.reshape(groups, capacity, width), group_cots.reshape(groups, capacity, width)], axis=1
     )
     at, send = lax.optimization_barrier((at, send))
-    share = lax.psum_scatter(pack(at, states, slot_in, slot_out), GROUP, scatter_dimension=0, tiled=True)
+    share = lax.psum_scatter(pack(at, states, slot_in, slot_out), "y", scatter_dimension=0, tiled=True)
     received = lax.all_to_all(send, GROUP, split_axis=0, concat_axis=0, tiled=True)
     rows_piece = received[:, :capacity].reshape(groups * capacity, width)
     cots_piece = received[:, capacity:].reshape(groups * capacity, width)
@@ -279,6 +278,8 @@
     last_dims = (((1,), (1,)), ((), ()))
     first_dims = (((0,), (0,)), ((), ()))
     projected = jnp.dot(rows_in, slot_in, preferred_element_type=jnp.float32) * width ** (-0.5)
+    projected, share = lax.optimization_barrier((projected, share))
+    crossed = flip(share, "xh")
     gate_part = projected[:, :hidden]
     up_part = projected[:, hidden:]
     sigmoid = jax.nn.sigmoid(gate_part)
@@ -299,24 +300,32 @@
     away_out = lax.dynamic_slice_in_dim(grad_out, other_half * rows_out_half, rows_out_half, 0).astype(half_type)
     kept_in = lax.dynamic_slice_in_dim(grad_in, data_half * rows_in_half, rows_in_half, 0)
     kept_out = lax.dynamic_slice_in_dim(grad_out, data_half * rows_out_half, rows_out_half, 0)
+    away_in, away_out, share = lax.optimization_barrier((away_in, away_out, share))
     came_out = flip(away_out, "dp")
+    came_in = flip(away_in, "dp")
+
+    own_out, sides_out, diag_out = reduce_start(outputs)
+    own_grad, sides_grad, diag_grad = reduce_start(grad_rows)
+    diag_out, diag_grad, crossed = lax.optimization_barrier((diag_out, diag_grad, crossed))
+    early = lax.all_gather(jnp.where(one_column, share, crossed), "y", axis=0, tiled=True)
+    cut = diag_out.shape[0] // 2
+    to_x, to_z = zip(
+        *[
+            reduce_turn(sides, flip(diag[:cut], "xl"), flip(diag[cut:], "z"))
+            for sides, diag in ((sides_out, diag_out), (sides_grad, diag_grad))
+        ]
+    )
+    came_in, came_out, to_x, to_z = lax.optimization_barrier((came_in, came_out, to_x, to_z))
     half_out = kept_out + came_out.astype(jnp.float32)
-    half_in = kept_in + flip(away_in, "dp").astype(jnp.float32)
-    half_in, half_out, share = lax.optimization_barrier((half_in, half_out, share))
-    early = lax.all_gather(share, GROUP, axis=0, tiled=True)
-
-    own_out, out_to_x, out_to_z = reduce_start(outputs, 0.5)
-    own_grad, grad_to_x, grad_to_z = reduce_start(grad_rows, 0.5)
-    (late_in, late_out), from_x, from_z = lax.switch(
+    half_in = kept_in + came_in.astype(jnp.float32)
+    late_in, late_out = lax.switch(
         case,
-        [functools.partial(late_steps, distance=distance) for distance in DISTANCES],
+        [functools.partial(exchange, distance=distance) for distance in DISTANCES],
         (half_in.astype(half_type), half_out.astype(half_type)),
-        (out_to_x, grad_to_x),
-        (out_to_z, grad_to_z),
     )
     out_sum, grad_sum = (
-        own + part_x.astype(jnp.float32) + part_z.astype(jnp.float32)
-        for own, part_x, part_z in zip((own_out, own_grad), from_x, from_z)
+        own + flip(part_x, "xl").astype(jnp.float32) + flip(part_z, "z").astype(jnp.float32)
+        for own, part_x, part_z in zip((own_out, own_grad), to_x, to_z)
     )
     back = jnp.concatenate(
         [

time: 296 us -> 264 us (0.89)
  waiting for transfers between devices: 175 us -> 129 us
  starting transfers between devices: 37.6 us -> 41.5 us
  between operations: 17.3 us -> 21.1 us
    ppermute x30 -> x31, waiting for transfers between devices: 129 us -> 80.5 us  [flip(): return lax.ppermute(value, axis, FLIP)]
    ppermute x2, waiting for transfers between devices: 15.9 us -> 40.8 us  [exchange(): return tuple((lax.ppermute(value, PARTS, pairs) for value in values))]
    all_gather x1, waiting for transfers between devices: 22.5 us -> 0.01 us  [on_device(): lax.all_gather(jnp.where(one_column, share, crossed), 'y', axis=0, tiled=...]
    ppermute x30 -> x31, starting transfers between devices: 20.4 us -> 23.5 us  [flip(): return lax.ppermute(value, axis, FLIP)]
    another operation x5, other arithmetic: 7.25 us -> 4.26 us
  transfers between devices with their start and end apart: 36 -> 37, of which waited for: 14 -> 19; matrix products, arithmetic and copies ran while one was open for 10% -> 11% of each run, Pallas kernels for 6% -> 8%
where the time goes in v3:
time: 264 us
  waiting for transfers between devices  129 us (49%)
  starting transfers between devices  41.5 us (16%)
  between operations  21.1 us (8%)
  Pallas kernels  20.2 us (8%)
  other arithmetic  19.5 us (7%)
  local copies, waits for them, and re-layouts  17.1 us (6%)
  matrix products  15.9 us (6%)
    ppermute x31, waiting for transfers between devices, flip(): return lax.ppermute(value, axis, FLIP)  80.5 us
    ppermute x2, waiting for transfers between devices, exchange(): return tuple((lax.ppermute(value, PARTS, pairs) for value in values))  40.8 us
    ppermute x31, starting transfers between devices, flip(): return lax.ppermute(value, axis, FLIP)  23.5 us
    pallas_call x1, Pallas kernels, adam(): pl.pallas_call(adam_kernel, grid_spec=pltpu.PrefetchScalarGridSpec(num_sc...  11.9 us
    unnamed x45, local copies, waits for them, and re-layouts  10.3 us
    pallas_call x1, Pallas kernels, pack(): pl.pallas_call(pack_kernel, grid_spec=pltpu.PrefetchScalarGridSpec(num_sc...  8.33 us
    all_to_all x1, waiting for transfers between devices, on_device(): lax.all_to_all(send, GROUP, split_axis=0, concat_axis=0, tiled=True)  7.42 us
    all_to_all x1, starting transfers between devices, on_device(): lax.all_to_all(send, GROUP, split_axis=0, concat_axis=0, tiled=True)  7.01 us
  transfers between devices with their start and end apart: 37, of which 19 were waited for; matrix products, arithmetic and copies ran while one was open for 11% of the time, Pallas kernels for 8%

profile of v3, /device:TPU:0, one launch (start us, length us, event | category | flops | bytes accessed | tf_op | source)
XLA Modules:
  0.0 264.1 jit_solution(3747471999971288592)
XLA Ops:
  7.2 1.3 select_reduce_fusion.2
  17.0 1.2 fusion.2
  18.2 1.0 pad_maximum_fusion
  19.9 7.0 %all-to-all-start = ((bf16[8,16,4096]{2,1,0:T(8,128)(2,1)}), bf16[8,16,4096]{2,1,0:T(8,128)(2,1)S(1)}, u32[]{:S(2)}, u32[]{:S(2)}) async-start(bf16[8,16,4096]{2,1,0:T(8,128)(2,1)} %pad_maximum_fusion), calls=%async_computation | async-start | bytes 2097152 | tf_op jit(solution)/shard_map/all_to_all | solution.py:273
  27.0 8.3 %shard_map.170 = bf16[8,1152,256]{2,1,0:T(8,128)(2,1)} custom-call(s32[3]{0:T(128)} %pad_add_fusion.at, f32[2048,256]{1,0:T(8,128)} %bitcast.76, f32[2048,256]{1,0:T(8,128)} %bitcast.78, bf16[4096,256]{1,0:T(8,128)(2,1)} %bitcast.72, f32[64,4096]{1,0:T(8,128)} %bitcast.70, f32[64,4096]{1,0:T(8,128)} %bitcast.80, bf16[128,4096]{1,0:T(8,128)(2,1)} %bitcast.74), custom_call_target="tpu_custom_call" | custom-call | flops 4194304 | bytes 25165824 | tf_op jit(solution)/shard_map/pallas_call | solution.py:80
  36.7 7.4 %all-to-all-done = bf16[8,16,4096]{2,1,0:T(8,128)(2,1)S(1)} async-done(((bf16[8,16,4096]{2,1,0:T(8,128)(2,1)}), bf16[8,16,4096]{2,1,0:T(8,128)(2,1)S(1)}, u32[]{:S(2)}, u32[]{:S(2)}) %all-to-all-start) | async-done | bytes 1048608 | tf_op jit(solution)/shard_map/all_to_all | solution.py:273
  44.2 2.0 collective-permute-start.15
  46.8 1.4 collective-permute-start.22
  48.4 0.9 constant_dynamic-update-slice_fusion.17
  49.2 9.9 %collective-permute-done.15 = bf16[64,4096]{1,0:T(8,128)(2,1)S(1)} collective-permute-done((bf16[64,4096]{1,0:T(8,128)(2,1)S(1)}, bf16[64,4096]{1,0:T(8,128)(2,1)S(1)}, u32[]{:S(2)}, u32[]{:S(2)}) %collective-permute-start.15) | collective-permute-done | bytes 524320 | tf_op jit(solution)/shard_map/ppermute | solution.py:162
  59.2 1.9 collective-permute-done.14
  62.1 1.8 collective-permute-done.17
  64.6 10.4 %collective-permute-done.18 = bf16[32,4096]{1,0:T(8,128)(2,1)S(1)} collective-permute-done((bf16[32,4096]{1,0:T(8,128)(2,1)S(1)}, bf16[32,4096]{1,0:T(8,128)(2,1)S(1)}, u32[]{:S(2)}, u32[]{:S(2)}) %collective-permute-start.18) | collective-permute-done | bytes 262176 | tf_op jit(solution)/shard_map/ppermute | solution.py:162
  75.2 0.9 constant_dynamic-update-slice_fusion.16
  77.7 0.8 constant_dynamic-update-slice_fusion.15
  78.5 0.8 constant_dynamic-update-slice_fusion.14
  79.4 5.6 %collective-permute-done.26 = bf16[32,4096]{1,0:T(8,128)(2,1)S(1)} collective-permute-done((bf16[32,4096]{1,0:T(8,128)(2,1)S(1)}, bf16[32,4096]{1,0:T(8,128)(2,1)S(1)}, u32[]{:S(2)}, u32[]{:S(2)}) %collective-permute-start.26) | collective-permute-done | bytes 262176 | tf_op jit(solution)/shard_map/ppermute | solution.py:162
  85.7 2.2 convolution_multiply_fusion.4
  87.9 1.1 constant_dynamic-update-slice_fusion.13
  90.5 0.8 constant_dynamic-update-slice_fusion.10
  91.4 3.5 %multiply_multiply_fusion = (f32[512,128]{1,0:T(8,128)S(1)}, f32[512,128]{1,0:T(8,128)S(1)}, bf16[512,128]{1,0:T(8,128)(2,1)S(1)}) fusion(f32[512,256]{1,0:T(8,128)} %convolution_multiply_fusion.4, bf16[512,4096]{1,0:T(8,128)(2,1)} %constant_dynamic-update-slice_fusion.10, bf16[1,128,4096]{2,1,0:T(8,128)(2,1)S(1)} %copy-done.9), kind=kOutput, calls=%fused_computation.55 | convolution fusion | flops 537788416 | bytes 6422528 | tf_op jit(solution)/shard_map/dot_general | solution.py:289
  94.9 2.9 %convolution_multiply_fusion = f32[128,4096]{1,0:T(8,128)S(1)} fusion(bf16[512,128]{1,0:T(8,128)(2,1)S(1)} %get-tuple-element.138, bf16[512,4096]{1,0:T(8,128)(2,1)} %constant_dynamic-update-slice_fusion.10), kind=kOutput, calls=%fused_computation.2 | convolution fusion | flops 537395200 | bytes 6422528 | tf_op jit(solution)/shard_map/dot_general | solution.py:296
  97.9 1.2 multiply_convert_fusion
  99.2 0.9 fusion.37
  100.1 2.4 copy-done.12
  102.5 1.3 fusion.23
  103.8 1.3 convolution_convert_fusion
  105.1 0.8 copy-done.13
  106.0 1.6 collective-permute-start.34
  107.6 1.1 dynamic-slice_convert_fusion
  108.7 0.8 dynamic-slice_convert_fusion.1
  109.5 3.6 %collective-permute-start.29 = (bf16[2048,256]{1,0:T(8,128)(2,1)}, bf16[2048,256]{1,0:T(8,128)(2,1)}, u32[]{:S(2)}, u32[]{:S(2)}) collective-permute-start(bf16[2048,256]{1,0:T(8,128)(2,1)} %dynamic-slice_convert_fusion), channel_id=1, source_target_pairs={{0,64},{64,0},{1,65},{65,1},{2,66},{66,2},{3,67},{67,3},{4,68},{68... | collective-permute-start | bytes 3145736 | tf_op jit(solution)/shard_map/ppermute | solution.py:162
  113.7 0.9 fusion.38
  114.6 1.9 collective-permute-done.32
  116.8 1.6 collective-permute-done.33
  119.2 1.6 fusion.33
  122.2 13.6 %collective-permute-done.34 = bf16[2,1152,256]{2,1,0:T(8,128)(2,1)S(1)} collective-permute-done((bf16[2,1152,256]{2,1,0:T(8,128)(2,1)S(1)}, bf16[2,1152,256]{2,1,0:T(8,128)(2,1)S(1)}, u32[]{:S(2)}, u32[]{:S(2)}) %collective-permute-start.34) | collective-permute-done | bytes 1179680 | tf_op jit(solution)/shard_map/ppermute | solution.py:162
  135.8 0.9 fusion.42
  136.7 1.4 collective-permute-start.38
  138.5 1.2 broadcast_select_fusion
  139.7 5.3 %collective-permute-done.38 = bf16[32,4096]{1,0:T(8,128)(2,1)} collective-permute-done((bf16[32,4096]{1,0:T(8,128)(2,1)}, bf16[32,4096]{1,0:T(8,128)(2,1)}, u32[]{:S(2)}, u32[]{:S(2)}) %collective-permute-start.38) | collective-permute-done | bytes 262176 | tf_op jit(solution)/shard_map/ppermute | solution.py:162
  145.0 1.4 collective-permute-start.39
  146.4 6.9 %collective-permute-done.35 = bf16[32,4096]{1,0:T(8,128)(2,1)} collective-permute-done((bf16[32,4096]{1,0:T(8,128)(2,1)}, bf16[32,4096]{1,0:T(8,128)(2,1)}, u32[]{:S(2)}, u32[]{:S(2)}) %collective-permute-start.35) | collective-permute-done | bytes 262176 | tf_op jit(solution)/shard_map/ppermute | solution.py:162
  153.3 2.2 collective-permute-start.37
  155.6 1.6 fusion.8
  157.3 4.1 %collective-permute-done.37 = bf16[32,4096]{1,0:T(8,128)(2,1)S(1)} collective-permute-done((bf16[32,4096]{1,0:T(8,128)(2,1)S(1)}, bf16[32,4096]{1,0:T(8,128)(2,1)S(1)}, u32[]{:S(2)}, u32[]{:S(2)}) %collective-permute-start.37) | collective-permute-done | bytes 262176 | tf_op jit(solution)/shard_map/ppermute | solution.py:162
  161.7 1.8 collective-permute-start.44
  164.4 2.9 %fusion.36 = (bf16[2048,256]{1,0:T(8,128)(2,1)S(1)}, f32[2048,256]{1,0:T(8,128)}) fusion(bf16[2048,256]{1,0:T(8,128)(2,1)} %collective-permute-done.29, f32[4096,256]{1,0:T(8,128)S(1)} %copy-done.8, s32[]{:T(128)S(6)} %select_n.51), kind=kLoop, calls=%fused_computation.105 | loop fusion | flops 1572864 | bytes 6291460 | tf_op jit(solution)/shard_map/convert_element_type | solution.py:324
  167.4 1.4 collective-permute-start.40
  168.7 7.9 %collective-permute-done.44 = bf16[64,4096]{1,0:T(8,128)(2,1)S(1)} collective-permute-done((bf16[64,4096]{1,0:T(8,128)(2,1)S(1)}, bf16[64,4096]{1,0:T(8,128)(2,1)S(1)}, u32[]{:S(2)}, u32[]{:S(2)}) %collective-permute-start.44) | collective-permute-done | bytes 524320 | tf_op jit(solution)/shard_map/ppermute | solution.py:162
  176.6 1.7 collective-permute-done.43
  178.4 1.5 fusion.6
  179.8 5.8 %collective-permute-done.41 = bf16[64,4096]{1,0:T(8,128)(2,1)S(1)} collective-permute-done((bf16[64,4096]{1,0:T(8,128)(2,1)S(1)}, bf16[64,4096]{1,0:T(8,128)(2,1)S(1)}, u32[]{:S(2)}, u32[]{:S(2)}) %collective-permute-start.41) | collective-permute-done | bytes 524320 | tf_op jit(solution)/shard_map/ppermute | solution.py:162
  185.7 1.2 collective-permute-done.40
  186.8 1.3 fusion.5
  188.2 1.1 pad_maximum_fusion.3
  189.2 4.9 %all-to-all-start.1 = ((bf16[8,16,4096]{2,1,0:T(8,128)(2,1)}), bf16[8,16,4096]{2,1,0:T(8,128)(2,1)S(1)}, u32[]{:S(2)}, u32[]{:S(2)}) async-start(bf16[8,16,4096]{2,1,0:T(8,128)(2,1)} %pad_maximum_fusion.3), calls=%async_computation.2 | async-start | bytes 2097152 | tf_op jit(solution)/shard_map/all_to_all | solution.py:337
  194.1 2.5 fusion.35
  196.6 46.8 %conditional.1 = (bf16[2048,256]{1,0:T(8,128)(2,1)}, bf16[64,4096]{1,0:T(8,128)(2,1)}) conditional(s32[]{:T(128)} %clamp.3, (bf16[2048,256]{1,0:T(8,128)(2,1)S(1)}, bf16[64,4096]{1,0:T(8,128)(2,1)S(1)}) %tuple.49, (bf16[2048,256]{1,0:T(8,128)(2,1)S(1)}, bf16[64,4096]{1,0:T(8,128)(2,1)S(1)}) %tuple.49, ...), branch_computations={%region_7.8_spmd, %region_8.9_spmd, %region_9.10_spmd, %region_10.... | conditional | bytes 6291552 | solution.py:321
  196.6 5.9 %collective-permute-start.8 = (bf16[2048,256]{1,0:T(8,128)(2,1)S(1)}, bf16[2048,256]{1,0:T(8,128)(2,1)}, u32[]{:S(2)}, u32[]{:S(2)}) collective-permute-start(bf16[2048,256]{1,0:T(8,128)(2,1)S(1)} %get-tuple-element.36), channel_id=1, source_target_pairs={{0,40},{1,41},{2,42},{3,43},{4,44},{5,45},{6,46},{7,47},{8,32},{9,... | collective-permute-start | bytes 3145736 | tf_op jit(solution)/shard_map/cond/branch_4_fun/ppermute | solution.py:215
  202.6 40.8 %collective-permute-done.9 = bf16[64,4096]{1,0:T(8,128)(2,1)} collective-permute-done((bf16[64,4096]{1,0:T(8,128)(2,1)S(1)}, bf16[64,4096]{1,0:T(8,128)(2,1)}, u32[]{:S(2)}, u32[]{:S(2)}) %collective-permute-start.9) | collective-permute-done | bytes 524320 | tf_op jit(solution)/shard_map/cond/branch_4_fun/ppermute | solution.py:215
  243.5 11.9 %shard_map.171 = (bf16[2048,256]{1,0:T(8,128)(2,1)}, f32[2048,256]{1,0:T(8,128)}, f32[2048,256]{1,0:T(8,128)}, bf16[64,4096]{1,0:T(8,128)(2,1)}, f32[64,4096]{1,0:T(8,128)}, /*index=5*/f32[64,4096]{1,0:T(8,128)}) custom-call(s32[3]{0:T(128)S(1)} %copy-done.3, bf16[8,1152,256]{2,1,0:T(8,128)(2,1)} %all-gather.2.cloned.1.call-done.packed, ...), custom_call_target="tpu_custom_call" | custom-call | flops 16777216 | bytes 31457280 | tf_op jit(solution)/shard_map/pallas_call | solution.py:142
  255.4 0.8 convolution_convert_fusion.2
  256.4 0.9 fusion.4
  (119 shorter events, 15.4 us)
Async XLA Ops:
  7.2 9.4 %copy-start = (bf16[16,4096]{1,0:T(8,128)(2,1)S(1)}, bf16[16,4096]{1,0:T(8,128)(2,1)}, u32[]{:S(2)}) copy-start(bf16[16,4096]{1,0:T(8,128)(2,1)} %param.18) | copy-start | bytes 393220
  19.9 24.2 %all-to-all-start = ((bf16[8,16,4096]{2,1,0:T(8,128)(2,1)}), bf16[8,16,4096]{2,1,0:T(8,128)(2,1)S(1)}, u32[]{:S(2)}, u32[]{:S(2)}) async-start(bf16[8,16,4096]{2,1,0:T(8,128)(2,1)} %pad_maximum_fusion), calls=%async_computation | async-start | bytes 2097152 | tf_op jit(solution)/shard_map/all_to_all | solution.py:273
  26.9 64.4 %reduce-scatter.2.cloned.1.call-start = ((), (), s32[]{:S(2)}) async-start(), calls=%async_computation.3 | async-start | bytes 5898240 | tf_op jit(solution)/shard_map/reduce_scatter | solution.py:272
  35.3 1.4 copy-start.15
  35.3 208.1 %all-gather.2.cloned.1.call-start = ((), (), s32[]{:S(2)}) async-start(), calls=%async_computation.4 | async-start | bytes 5898240 | tf_op jit(solution)/shard_map/all_gather | solution.py:310
  44.2 14.9 %collective-permute-start.15 = (bf16[64,4096]{1,0:T(8,128)(2,1)S(1)}, bf16[64,4096]{1,0:T(8,128)(2,1)S(1)}, u32[]{:S(2)}, u32[]{:S(2)}) collective-permute-start(bf16[64,4096]{1,0:T(8,128)(2,1)S(1)} %get-tuple-element.129), channel_id=1, source_target_pairs={{0,2},{2,0},{1,3},{3,1},{4,6},{6,4},{5,7},{7,5},{8,10},{10,8},{9,1... | collective-permute-start | bytes 1572872 | tf_op jit(solution)/shard_map/ppermute | solution.py:162
  46.2 14.9 %collective-permute-start.14 = (bf16[64,4096]{1,0:T(8,128)(2,1)S(1)}, bf16[64,4096]{1,0:T(8,128)(2,1)S(1)}, u32[]{:S(2)}, u32[]{:S(2)}) collective-permute-start(bf16[64,4096]{1,0:T(8,128)(2,1)S(1)} %get-tuple-element.129), channel_id=1, source_target_pairs={{0,4},{4,0},{1,5},{5,1},{2,6},{6,2},{3,7},{7,3},{8,12},{12,8},{9,1... | collective-permute-start | bytes 1572872 | tf_op jit(solution)/shard_map/ppermute | solution.py:162
  46.8 14.6 %collective-permute-start.16 = (bf16[64,4096]{1,0:T(8,128)(2,1)S(1)}, bf16[64,4096]{1,0:T(8,128)(2,1)S(1)}, u32[]{:S(2)}, u32[]{:S(2)}) collective-permute-start(bf16[64,4096]{1,0:T(8,128)(2,1)S(1)} %get-tuple-element.129), channel_id=1, source_target_pairs={{0,1},{1,0},{2,3},{3,2},{4,5},{5,4},{6,7},{7,6},{8,9},{9,8},{10,11... | collective-permute-start | bytes 1572872 | tf_op jit(solution)/shard_map/ppermute | solution.py:162
  46.8 28.3 %collective-permute-start.22 = (bf16[64,4096]{1,0:T(8,128)(2,1)S(1)}, bf16[64,4096]{1,0:T(8,128)(2,1)S(1)}, u32[]{:S(2)}, u32[]{:S(2)}) collective-permute-start(bf16[64,4096]{1,0:T(8,128)(2,1)S(1)} %get-tuple-element.128), channel_id=1, source_target_pairs={{0,4},{4,0},{1,5},{5,1},{2,6},{6,2},{3,7},{7,3},{8,12},{12,8},{9,1... | collective-permute-start | bytes 1572872 | tf_op jit(solution)/shard_map/ppermute | solution.py:162
  48.2 26.9 %collective-permute-start.23 = (bf16[64,4096]{1,0:T(8,128)(2,1)S(1)}, bf16[64,4096]{1,0:T(8,128)(2,1)S(1)}, u32[]{:S(2)}, u32[]{:S(2)}) collective-permute-start(bf16[64,4096]{1,0:T(8,128)(2,1)S(1)} %get-tuple-element.128), channel_id=1, source_target_pairs={{0,2},{2,0},{1,3},{3,1},{4,6},{6,4},{5,7},{7,5},{8,10},{10,8},{9,1... | collective-permute-start | bytes 1572872 | tf_op jit(solution)/shard_map/ppermute | solution.py:162
  59.2 19.4 %collective-permute-start.24 = (bf16[64,4096]{1,0:T(8,128)(2,1)S(1)}, bf16[64,4096]{1,0:T(8,128)(2,1)S(1)}, u32[]{:S(2)}, u32[]{:S(2)}) collective-permute-start(bf16[64,4096]{1,0:T(8,128)(2,1)S(1)} %get-tuple-element.128), channel_id=1, source_target_pairs={{0,1},{1,0},{2,3},{3,2},{4,5},{5,4},{6,7},{7,6},{8,9},{9,8},{10,11... | collective-permute-start | bytes 1572872 | tf_op jit(solution)/shard_map/ppermute | solution.py:162
  61.2 2.7 %collective-permute-start.17 = (bf16[128,4096]{1,0:T(8,128)(2,1)S(1)}, bf16[128,4096]{1,0:T(8,128)(2,1)S(1)}, u32[]{:S(2)}, u32[]{:S(2)}) collective-permute-start(bf16[128,4096]{1,0:T(8,128)(2,1)S(1)} %pad_maximum_fusion.1), channel_id=1, source_target_pairs={{0,1},{1,0},{2,3},{3,2},{4,5},{5,4},{6,7},{7,6},{8,9},{9,8},{10,11... | collective-permute-start | bytes 3145736 | tf_op jit(solution)/shard_map/ppermute | solution.py:162
  61.4 13.5 %collective-permute-start.18 = (bf16[32,4096]{1,0:T(8,128)(2,1)S(1)}, bf16[32,4096]{1,0:T(8,128)(2,1)S(1)}, u32[]{:S(2)}, u32[]{:S(2)}) collective-permute-start(bf16[32,4096]{1,0:T(8,128)(2,1)S(1)} %slice.170), channel_id=1, source_target_pairs={{0,4},{4,0},{1,5},{5,1},{2,6},{6,2},{3,7},{7,3},{8,12},{12,8},{9,1... | collective-permute-start | bytes 786440 | tf_op jit(solution)/shard_map/ppermute | solution.py:162
  63.9 11.1 %collective-permute-start.19 = (bf16[32,4096]{1,0:T(8,128)(2,1)S(1)}, bf16[32,4096]{1,0:T(8,128)(2,1)S(1)}, u32[]{:S(2)}, u32[]{:S(2)}) collective-permute-start(bf16[32,4096]{1,0:T(8,128)(2,1)S(1)} %slice.171), channel_id=1, source_target_pairs={{0,2},{2,0},{1,3},{3,1},{4,6},{6,4},{5,7},{7,5},{8,10},{10,8},{9,1... | collective-permute-start | bytes 786440 | tf_op jit(solution)/shard_map/ppermute | solution.py:162
  75.0 10.7 %copy-start.6 = (bf16[1,4096,256]{2,1,0:T(8,128)(2,1)S(1)}, bf16[1,4096,256]{2,1,0:T(8,128)(2,1)}, u32[]{:S(2)}) copy-start(bf16[1,4096,256]{2,1,0:T(8,128)(2,1)} %param.23) | copy-start | bytes 6291460
  75.1 10.6 %collective-permute-start.20 = (bf16[64,4096]{1,0:T(8,128)(2,1)S(1)}, bf16[64,4096]{1,0:T(8,128)(2,1)S(1)}, u32[]{:S(2)}, u32[]{:S(2)}) collective-permute-start(bf16[64,4096]{1,0:T(8,128)(2,1)S(1)} %get-tuple-element.139), channel_id=1, source_target_pairs={{0,1},{1,0},{2,3},{3,2},{4,5},{5,4},{6,7},{7,6},{8,9},{9,8},{10,11... | collective-permute-start | bytes 1572872 | tf_op jit(solution)/shard_map/ppermute | solution.py:162
  76.1 11.7 %collective-permute-start.25 = (bf16[128,4096]{1,0:T(8,128)(2,1)S(1)}, bf16[128,4096]{1,0:T(8,128)(2,1)S(1)}, u32[]{:S(2)}, u32[]{:S(2)}) collective-permute-start(bf16[128,4096]{1,0:T(8,128)(2,1)S(1)} %pad_maximum_fusion.2), channel_id=1, source_target_pairs={{0,1},{1,0},{2,3},{3,2},{4,5},{5,4},{6,7},{7,6},{8,9},{9,8},{10,11... | collective-permute-start | bytes 3145736 | tf_op jit(solution)/shard_map/ppermute | solution.py:162
  76.7 8.3 %collective-permute-start.26 = (bf16[32,4096]{1,0:T(8,128)(2,1)S(1)}, bf16[32,4096]{1,0:T(8,128)(2,1)S(1)}, u32[]{:S(2)}, u32[]{:S(2)}) collective-permute-start(bf16[32,4096]{1,0:T(8,128)(2,1)S(1)} %slice.140), channel_id=1, source_target_pairs={{0,4},{4,0},{1,5},{5,1},{2,6},{6,2},{3,7},{7,3},{8,12},{12,8},{9,1... | collective-permute-start | bytes 786440 | tf_op jit(solution)/shard_map/ppermute | solution.py:162
  77.3 8.0 %collective-permute-start.27 = (bf16[32,4096]{1,0:T(8,128)(2,1)S(1)}, bf16[32,4096]{1,0:T(8,128)(2,1)S(1)}, u32[]{:S(2)}, u32[]{:S(2)}) collective-permute-start(bf16[32,4096]{1,0:T(8,128)(2,1)S(1)} %slice.141), channel_id=1, source_target_pairs={{0,2},{2,0},{1,3},{3,1},{4,6},{6,4},{5,7},{7,5},{8,10},{10,8},{9,1... | collective-permute-start | bytes 786440 | tf_op jit(solution)/shard_map/ppermute | solution.py:162
  85.4 5.1 %collective-permute-start.28 = (bf16[64,4096]{1,0:T(8,128)(2,1)S(1)}, bf16[64,4096]{1,0:T(8,128)(2,1)S(1)}, u32[]{:S(2)}, u32[]{:S(2)}) collective-permute-start(bf16[64,4096]{1,0:T(8,128)(2,1)S(1)} %pad_maximum_fusion.4), channel_id=1, source_target_pairs={{0,1},{1,0},{2,3},{3,2},{4,5},{5,4},{6,7},{7,6},{8,9},{9,8},{10,11... | collective-permute-start | bytes 1572872 | tf_op jit(solution)/shard_map/ppermute | solution.py:162
  85.7 3.3 %copy-start.11 = (bf16[512,4096]{1,0:T(8,128)(2,1)}, bf16[512,4096]{1,0:T(8,128)(2,1)S(1)}, u32[]{:S(2)}) copy-start(bf16[512,4096]{1,0:T(8,128)(2,1)S(1)} %constant_dynamic-update-slice_fusion.2) | copy-start | bytes 12582916
  85.7 5.6 %copy-start.9 = (bf16[1,128,4096]{2,1,0:T(8,128)(2,1)S(1)}, bf16[1,128,4096]{2,1,0:T(8,128)(2,1)}, u32[]{:S(2)}) copy-start(bf16[1,128,4096]{2,1,0:T(8,128)(2,1)} %param.24) | copy-start | bytes 3145732
  97.9 10.8 %copy-start.10 = (f32[128,4096]{1,0:T(8,128)}, f32[128,4096]{1,0:T(8,128)S(1)}, u32[]{:S(2)}) copy-start(f32[128,4096]{1,0:T(8,128)S(1)} %convolution_multiply_fusion) | copy-start | bytes 6291460
  97.9 4.6 %copy-start.12 = (bf16[512,4096]{1,0:T(8,128)(2,1)S(1)}, bf16[512,4096]{1,0:T(8,128)(2,1)}, u32[]{:S(2)}) copy-start(bf16[512,4096]{1,0:T(8,128)(2,1)} %copy-done.11) | copy-start | bytes 12582916
  99.1 20.1 %copy-start.4 = (bf16[512,4096]{1,0:T(8,128)(2,1)}, bf16[512,4096]{1,0:T(8,128)(2,1)S(1)}, u32[]{:S(2)}) copy-start(bf16[512,4096]{1,0:T(8,128)(2,1)S(1)} %multiply_convert_fusion) | copy-start | bytes 12582916
  103.8 3.8 %copy-start.7 = (f32[4096,256]{1,0:T(8,128)}, f32[4096,256]{1,0:T(8,128)S(1)}, u32[]{:S(2)}) copy-start(f32[4096,256]{1,0:T(8,128)S(1)} %fusion.23) | copy-start | bytes 12582916
  103.8 2.1 copy-start.13
  106.0 15.2 %copy-start.5 = (bf16[512,4096]{1,0:T(8,128)(2,1)}, bf16[512,4096]{1,0:T(8,128)(2,1)S(1)}, u32[]{:S(2)}) copy-start(bf16[512,4096]{1,0:T(8,128)(2,1)S(1)} %convolution_convert_fusion) | copy-start | bytes 12582916
  106.0 29.9 %collective-permute-start.34 = (bf16[2,1152,256]{2,1,0:T(8,128)(2,1)S(1)}, bf16[2,1152,256]{2,1,0:T(8,128)(2,1)S(1)}, u32[]{:S(2)}, u32[]{:S(2)}) collective-permute-start(bf16[2,1152,256]{2,1,0:T(8,128)(2,1)S(1)} %copy-done.13), channel_id=1, source_target_pairs={{0,8},{8,0},{1,9},{9,1},{2,10},{10,2},{3,11},{11,3},{4,12},{12,4},... | collective-permute-start | bytes 3538952 | tf_op jit(solution)/shard_map/ppermute | solution.py:162
  109.5 52.1 %collective-permute-start.29 = (bf16[2048,256]{1,0:T(8,128)(2,1)}, bf16[2048,256]{1,0:T(8,128)(2,1)}, u32[]{:S(2)}, u32[]{:S(2)}) collective-permute-start(bf16[2048,256]{1,0:T(8,128)(2,1)} %dynamic-slice_convert_fusion), channel_id=1, source_target_pairs={{0,64},{64,0},{1,65},{65,1},{2,66},{66,2},{3,67},{67,3},{4,68},{68... | collective-permute-start | bytes 3145736 | tf_op jit(solution)/shard_map/ppermute | solution.py:162
  113.1 48.5 %collective-permute-start.30 = (bf16[64,4096]{1,0:T(8,128)(2,1)}, bf16[64,4096]{1,0:T(8,128)(2,1)}, u32[]{:S(2)}, u32[]{:S(2)}) collective-permute-start(bf16[64,4096]{1,0:T(8,128)(2,1)} %dynamic-slice_convert_fusion.1), channel_id=1, source_target_pairs={{0,64},{64,0},{1,65},{65,1},{2,66},{66,2},{3,67},{67,3},{4,68},{68... | collective-permute-start | bytes 1572872 | tf_op jit(solution)/shard_map/ppermute | solution.py:162
  113.2 5.6 %collective-permute-start.31 = (bf16[128,4096]{1,0:T(8,128)(2,1)S(1)}, bf16[128,4096]{1,0:T(8,128)(2,1)S(1)}, u32[]{:S(2)}, u32[]{:S(2)}) collective-permute-start(bf16[128,4096]{1,0:T(8,128)(2,1)S(1)} %slice.176), channel_id=1, source_target_pairs={{0,1},{1,0},{2,3},{3,2},{4,5},{5,4},{6,7},{7,6},{8,9},{9,8},{10,11... | collective-permute-start | bytes 3145736 | tf_op jit(solution)/shard_map/ppermute | solution.py:162
  113.2 3.4 %collective-permute-start.32 = (bf16[64,4096]{1,0:T(8,128)(2,1)S(1)}, bf16[64,4096]{1,0:T(8,128)(2,1)S(1)}, u32[]{:S(2)}, u32[]{:S(2)}) collective-permute-start(bf16[64,4096]{1,0:T(8,128)(2,1)S(1)} %get-tuple-element.117), channel_id=1, source_target_pairs={{0,1},{1,0},{2,3},{3,2},{4,5},{5,4},{6,7},{7,6},{8,9},{9,8},{10,11... | collective-permute-start | bytes 1572872 | tf_op jit(solution)/shard_map/ppermute | solution.py:162
  116.6 1.9 collective-permute-start.33
  118.5 2.7 %collective-permute-start.36 = (bf16[128,4096]{1,0:T(8,128)(2,1)S(1)}, bf16[128,4096]{1,0:T(8,128)(2,1)S(1)}, u32[]{:S(2)}, u32[]{:S(2)}) collective-permute-start(bf16[128,4096]{1,0:T(8,128)(2,1)S(1)} %slice.184), channel_id=1, source_target_pairs={{0,1},{1,0},{2,3},{3,2},{4,5},{5,4},{6,7},{7,6},{8,9},{9,8},{10,11... | collective-permute-start | bytes 3145736 | tf_op jit(solution)/shard_map/ppermute | solution.py:162
  118.8 48.6 %collective-permute-start.42 = (bf16[64,4096]{1,0:T(8,128)(2,1)}, bf16[64,4096]{1,0:T(8,128)(2,1)}, u32[]{:S(2)}, u32[]{:S(2)}) collective-permute-start(bf16[64,4096]{1,0:T(8,128)(2,1)} %get-tuple-element.118), channel_id=1, source_target_pairs={{0,1},{1,0},{2,3},{3,2},{4,5},{5,4},{6,7},{7,6},{8,9},{9,8},{10,11... | collective-permute-start | bytes 1572872 | tf_op jit(solution)/shard_map/ppermute | solution.py:162
  136.7 8.3 %collective-permute-start.38 = (bf16[32,4096]{1,0:T(8,128)(2,1)}, bf16[32,4096]{1,0:T(8,128)(2,1)}, u32[]{:S(2)}, u32[]{:S(2)}) collective-permute-start(bf16[32,4096]{1,0:T(8,128)(2,1)} %get-tuple-element.136), channel_id=1, source_target_pairs={{0,4},{4,0},{1,5},{5,1},{2,6},{6,2},{3,7},{7,3},{8,12},{12,8},{9,1... | collective-permute-start | bytes 786440 | tf_op jit(solution)/shard_map/ppermute | solution.py:162
  138.1 15.2 %collective-permute-start.35 = (bf16[32,4096]{1,0:T(8,128)(2,1)}, bf16[32,4096]{1,0:T(8,128)(2,1)}, u32[]{:S(2)}, u32[]{:S(2)}) collective-permute-start(bf16[32,4096]{1,0:T(8,128)(2,1)} %get-tuple-element.137), channel_id=1, source_target_pairs={{0,2},{2,0},{1,3},{3,1},{4,6},{6,4},{5,7},{7,5},{8,10},{10,8},{9,1... | collective-permute-start | bytes 786440 | tf_op jit(solution)/shard_map/ppermute | solution.py:162
  139.6 21.9 %copy-start.14 = (bf16[32,4096]{1,0:T(8,128)(2,1)S(1)}, bf16[32,4096]{1,0:T(8,128)(2,1)}, u32[]{:S(2)}) copy-start(bf16[32,4096]{1,0:T(8,128)(2,1)} %get-tuple-element.127) | copy-start | bytes 786436
  145.0 12.1 %collective-permute-start.39 = (bf16[32,4096]{1,0:T(8,128)(2,1)S(1)}, bf16[32,4096]{1,0:T(8,128)(2,1)S(1)}, u32[]{:S(2)}, u32[]{:S(2)}) collective-permute-start(bf16[32,4096]{1,0:T(8,128)(2,1)S(1)} %get-tuple-element.134), channel_id=1, source_target_pairs={{0,4},{4,0},{1,5},{5,1},{2,6},{6,2},{3,7},{7,3},{8,12},{12,8},{9,1... | collective-permute-start | bytes 786440 | tf_op jit(solution)/shard_map/ppermute | solution.py:162
  153.3 8.1 %collective-permute-start.37 = (bf16[32,4096]{1,0:T(8,128)(2,1)S(1)}, bf16[32,4096]{1,0:T(8,128)(2,1)S(1)}, u32[]{:S(2)}, u32[]{:S(2)}) collective-permute-start(bf16[32,4096]{1,0:T(8,128)(2,1)S(1)} %get-tuple-element.135), channel_id=1, source_target_pairs={{0,2},{2,0},{1,3},{3,1},{4,6},{6,4},{5,7},{7,5},{8,10},{10,8},{9,1... | collective-permute-start | bytes 786440 | tf_op jit(solution)/shard_map/ppermute | solution.py:162
  155.6 8.9 %copy-start.8 = (f32[4096,256]{1,0:T(8,128)S(1)}, f32[4096,256]{1,0:T(8,128)}, u32[]{:S(2)}) copy-start(f32[4096,256]{1,0:T(8,128)} %copy-done.7) | copy-start | bytes 12582916
  157.2 22.7 %collective-permute-start.21 = (bf16[64,4096]{1,0:T(8,128)(2,1)}, bf16[64,4096]{1,0:T(8,128)(2,1)S(1)}, u32[]{:S(2)}, u32[]{:S(2)}) collective-permute-start(bf16[64,4096]{1,0:T(8,128)(2,1)} %get-tuple-element.116), channel_id=1, source_target_pairs={{0,1},{1,0},{2,3},{3,2},{4,5},{5,4},{6,7},{7,6},{8,9},{9,8},{10,11... | collective-permute-start | bytes 1572872 | tf_op jit(solution)/shard_map/ppermute | solution.py:162
  161.7 14.9 %collective-permute-start.44 = (bf16[64,4096]{1,0:T(8,128)(2,1)S(1)}, bf16[64,4096]{1,0:T(8,128)(2,1)S(1)}, u32[]{:S(2)}, u32[]{:S(2)}) collective-permute-start(bf16[64,4096]{1,0:T(8,128)(2,1)S(1)} %get-tuple-element.91), channel_id=1, source_target_pairs={{0,2},{2,0},{1,3},{3,1},{4,6},{6,4},{5,7},{7,5},{8,10},{10,8},{9,1... | collective-permute-start | bytes 1572872 | tf_op jit(solution)/shard_map/ppermute | solution.py:162
  163.5 14.9 %collective-permute-start.43 = (bf16[64,4096]{1,0:T(8,128)(2,1)S(1)}, bf16[64,4096]{1,0:T(8,128)(2,1)S(1)}, u32[]{:S(2)}, u32[]{:S(2)}) collective-permute-start(bf16[64,4096]{1,0:T(8,128)(2,1)S(1)} %get-tuple-element.90), channel_id=1, source_target_pairs={{0,4},{4,0},{1,5},{5,1},{2,6},{6,2},{3,7},{7,3},{8,12},{12,8},{9,1... | collective-permute-start | bytes 1572872 | tf_op jit(solution)/shard_map/ppermute | solution.py:162
  164.2 21.5 %collective-permute-start.41 = (bf16[64,4096]{1,0:T(8,128)(2,1)S(1)}, bf16[64,4096]{1,0:T(8,128)(2,1)S(1)}, u32[]{:S(2)}, u32[]{:S(2)}) collective-permute-start(bf16[64,4096]{1,0:T(8,128)(2,1)S(1)} %get-tuple-element.89), channel_id=1, source_target_pairs={{0,2},{2,0},{1,3},{3,1},{4,6},{6,4},{5,7},{7,5},{8,10},{10,8},{9,1... | collective-permute-start | bytes 1572872 | tf_op jit(solution)/shard_map/ppermute | solution.py:162
  167.4 19.5 %collective-permute-start.40 = (bf16[64,4096]{1,0:T(8,128)(2,1)S(1)}, bf16[64,4096]{1,0:T(8,128)(2,1)S(1)}, u32[]{:S(2)}, u32[]{:S(2)}) collective-permute-start(bf16[64,4096]{1,0:T(8,128)(2,1)S(1)} %get-tuple-element.88), channel_id=1, source_target_pairs={{0,4},{4,0},{1,5},{5,1},{2,6},{6,2},{3,7},{7,3},{8,12},{12,8},{9,1... | collective-permute-start | bytes 1572872 | tf_op jit(solution)/shard_map/ppermute | solution.py:162
  188.2 55.3 %copy-start.2 = (f32[1,64,4096]{2,1,0:T(8,128)S(1)}, f32[1,64,4096]{2,1,0:T(8,128)}, u32[]{:S(2)}) copy-start(f32[1,64,4096]{2,1,0:T(8,128)} %param.27) | copy-start | bytes 3145732
  188.2 55.3 %copy-start.3 = (s32[3]{0:T(128)S(1)}, s32[3]{0:T(128)}, u32[]{:S(2)}) copy-start(s32[3]{0:T(128)} %pad_add_fusion.at) | copy-start | bytes 40
  189.2 66.1 %all-to-all-start.1 = ((bf16[8,16,4096]{2,1,0:T(8,128)(2,1)}), bf16[8,16,4096]{2,1,0:T(8,128)(2,1)S(1)}, u32[]{:S(2)}, u32[]{:S(2)}) async-start(bf16[8,16,4096]{2,1,0:T(8,128)(2,1)} %pad_maximum_fusion.3), calls=%async_computation.2 | async-start | bytes 2097152 | tf_op jit(solution)/shard_map/all_to_all | solution.py:337
  196.6 46.8 %collective-permute-start.8 = (bf16[2048,256]{1,0:T(8,128)(2,1)S(1)}, bf16[2048,256]{1,0:T(8,128)(2,1)}, u32[]{:S(2)}, u32[]{:S(2)}) collective-permute-start(bf16[2048,256]{1,0:T(8,128)(2,1)S(1)} %get-tuple-element.36), channel_id=1, source_target_pairs={{0,40},{1,41},{2,42},{3,43},{4,44},{5,45},{6,46},{7,47},{8,32},{9,... | collective-permute-start | bytes 3145736 | tf_op jit(solution)/shard_map/cond/branch_4_fun/ppermute | solution.py:215
  202.6 40.9 %collective-permute-start.9 = (bf16[64,4096]{1,0:T(8,128)(2,1)S(1)}, bf16[64,4096]{1,0:T(8,128)(2,1)}, u32[]{:S(2)}, u32[]{:S(2)}) collective-permute-start(bf16[64,4096]{1,0:T(8,128)(2,1)S(1)} %get-tuple-element.37), channel_id=1, source_target_pairs={{0,40},{1,41},{2,42},{3,43},{4,44},{5,45},{6,46},{7,47},{8,32},{9,... | collective-permute-start | bytes 1572872 | tf_op jit(solution)/shard_map/cond/branch_4_fun/ppermute | solution.py:215
  243.5 13.8 %copy-start.1 = (bf16[16,4096]{1,0:T(8,128)(2,1)S(1)}, bf16[16,4096]{1,0:T(8,128)(2,1)}, u32[]{:S(2)}) copy-start(bf16[16,4096]{1,0:T(8,128)(2,1)} %param.18) | copy-start | bytes 393220
Sparse Core Ops, SparseCore 0:
  35.5 53.7 reduce-scatter.1
  139.8 52.2 all-gather.1

commit v4 on v3

--- a/solution.py
+++ b/solution.py
@@ -315,6 +315,7 @@
             for sides, diag in ((sides_out, diag_out), (sides_grad, diag_grad))
         ]
     )
+    to_x, to_z = jnp.stack(to_x), jnp.stack(to_z)
     came_in, came_out, to_x, to_z = lax.optimization_barrier((came_in, came_out, to_x, to_z))
     half_out = kept_out + came_out.astype(jnp.float32)
     half_in = kept_in + came_in.astype(jnp.float32)
@@ -323,9 +324,12 @@
         [functools.partial(exchange, distance=distance) for distance in DISTANCES],
         (half_in.astype(half_type), half_out.astype(half_type)),
     )
+    last_x = flip(to_x, "xl")
+    last_z = flip(to_z, "z")
+    last_x, last_z, late_in, late_out = lax.optimization_barrier((last_x, last_z, late_in, late_out))
     out_sum, grad_sum = (
-        own + flip(part_x, "xl").astype(jnp.float32) + flip(part_z, "z").astype(jnp.float32)
-        for own, part_x, part_z in zip((own_out, own_grad), to_x, to_z)
+        own + part_x.astype(jnp.float32) + part_z.astype(jnp.float32)
+        for own, part_x, part_z in zip((own_out, own_grad), last_x, last_z)
     )
     back = jnp.concatenate(
         [

time: 264 us -> 261 us (0.989)
    ppermute x31 -> x29, waiting for transfers between devices: 80.5 us -> 63.7 us  [flip(): return lax.ppermute(value, axis, FLIP)]
    ppermute x2, waiting for transfers between devices: 40.8 us -> 53.2 us  [exchange(): return tuple((lax.ppermute(value, PARTS, pairs) for value in values))]
    all_to_all x1, waiting for transfers between devices: 0.01 us -> 5.59 us  [on_device(): back = lax.all_to_all(back, GROUP, split_axis=0, concat_axis=0, tiled=True)]
    ppermute x2, starting transfers between devices: 5.96 us -> 3.25 us  [exchange(): return tuple((lax.ppermute(value, PARTS, pairs) for value in values))]
    unnamed x45 -> x48, local copies, waits for them, and re-layouts: 10.3 us -> 8.01 us
    ppermute x31 -> x29, starting transfers between devices: 23.5 us -> 23.7 us  [flip(): return lax.ppermute(value, axis, FLIP)]
  transfers between devices with their start and end apart: 37 -> 35, of which waited for: 19 -> 18; matrix products, arithmetic and copies ran while one was open for 11% -> 11% of each run, Pallas kernels for 8% -> 8%
where the time goes in v4:
time: 261 us; the launch traced here: 262 us
  waiting for transfers between devices  130 us (50%)
  starting transfers between devices  38.9 us (15%)
  between operations  21.1 us (8%)
  Pallas kernels  20.2 us (8%)
  other arithmetic  19.7 us (8%)
  matrix products  17.5 us (7%)
  local copies, waits for them, and re-layouts  14.8 us (6%)
    ppermute x29, waiting for transfers between devices, flip(): return lax.ppermute(value, axis, FLIP)  63.7 us
    ppermute x2, waiting for transfers between devices, exchange(): return tuple((lax.ppermute(value, PARTS, pairs) for value in values))  53.2 us
    ppermute x29, starting transfers between devices, flip(): return lax.ppermute(value, axis, FLIP)  23.7 us
    pallas_call x1, Pallas kernels, adam(): pl.pallas_call(adam_kernel, grid_spec=pltpu.PrefetchScalarGridSpec(num_sc...  11.9 us
    pallas_call x1, Pallas kernels, pack(): pl.pallas_call(pack_kernel, grid_spec=pltpu.PrefetchScalarGridSpec(num_sc...  8.29 us
    unnamed x48, local copies, waits for them, and re-layouts  8.01 us
    all_to_all x1, waiting for transfers between devices, on_device(): lax.all_to_all(send, GROUP, split_axis=0, concat_axis=0, tiled=True)  7.49 us
    all_to_all x1, starting transfers between devices, on_device(): lax.all_to_all(send, GROUP, split_axis=0, concat_axis=0, tiled=True)  7.01 us
  transfers between devices with their start and end apart: 35, of which 18 were waited for; matrix products, arithmetic and copies ran while one was open for 11% of the time, Pallas kernels for 8%

profile of v4, /device:TPU:0, one launch (start us, length us, event | category | flops | bytes accessed | tf_op | source)
XLA Modules:
  0.0 262.2 jit_solution(1763371622391760822)
XLA Ops:
  7.2 1.3 select_reduce_fusion.2
  13.7 0.8 copy.34
  15.8 0.8 select_reduce_fusion
  17.0 1.2 fusion.2
  18.2 1.0 pad_maximum_fusion
  19.9 7.0 %all-to-all-start = ((bf16[8,16,4096]{2,1,0:T(8,128)(2,1)}), bf16[8,16,4096]{2,1,0:T(8,128)(2,1)S(1)}, u32[]{:S(2)}, u32[]{:S(2)}) async-start(bf16[8,16,4096]{2,1,0:T(8,128)(2,1)} %pad_maximum_fusion), calls=%async_computation | async-start | bytes 2097152 | tf_op jit(solution)/shard_map/all_to_all | solution.py:273
  27.0 8.3 %shard_map.170 = bf16[8,1152,256]{2,1,0:T(8,128)(2,1)} custom-call(s32[3]{0:T(128)} %pad_add_fusion.at, f32[2048,256]{1,0:T(8,128)} %bitcast.104, f32[2048,256]{1,0:T(8,128)} %bitcast.106, bf16[4096,256]{1,0:T(8,128)(2,1)} %bitcast.100, f32[64,4096]{1,0:T(8,128)} %bitcast.98, f32[64,4096]{1,0:T(8,128)} %bitcast.108, bf16[128,4096]{1,0:T(8,128)(2,1)} %bitcast.102), custom_call_target="tpu_custom_call" | custom-call | flops 4194304 | bytes 25165824 | tf_op jit(solution)/shard_map/pallas_call | solution.py:80
  36.6 7.5 %all-to-all-done = bf16[8,16,4096]{2,1,0:T(8,128)(2,1)S(1)} async-done(((bf16[8,16,4096]{2,1,0:T(8,128)(2,1)}), bf16[8,16,4096]{2,1,0:T(8,128)(2,1)S(1)}, u32[]{:S(2)}, u32[]{:S(2)}) %all-to-all-start) | async-done | bytes 1048608 | tf_op jit(solution)/shard_map/all_to_all | solution.py:273
  44.9 1.9 collective-permute-start.15
  46.8 1.4 collective-permute-start.22
  48.3 0.9 constant_dynamic-update-slice_fusion.9
  49.2 9.9 %collective-permute-done.14 = bf16[64,4096]{1,0:T(8,128)(2,1)S(1)} collective-permute-done((bf16[64,4096]{1,0:T(8,128)(2,1)S(1)}, bf16[64,4096]{1,0:T(8,128)(2,1)S(1)}, u32[]{:S(2)}, u32[]{:S(2)}) %collective-permute-start.14) | collective-permute-done | bytes 524320 | tf_op jit(solution)/shard_map/ppermute | solution.py:162
  60.1 1.5 collective-permute-start.18
  61.6 0.9 collective-permute-done.17
  62.6 1.9 collective-permute-start.19
  64.6 8.7 %collective-permute-done.18 = bf16[32,4096]{1,0:T(8,128)(2,1)S(1)} collective-permute-done((bf16[32,4096]{1,0:T(8,128)(2,1)S(1)}, bf16[32,4096]{1,0:T(8,128)(2,1)S(1)}, u32[]{:S(2)}, u32[]{:S(2)}) %collective-permute-start.18) | collective-permute-done | bytes 262176 | tf_op jit(solution)/shard_map/ppermute | solution.py:162
  74.0 0.8 constant_dynamic-update-slice_fusion.16
  75.5 1.4 collective-permute-start.26
  76.9 1.7 collective-permute-start.27
  78.7 0.8 constant_dynamic-update-slice_fusion.15
  79.5 0.9 constant_dynamic-update-slice_fusion.14
  80.4 3.4 %collective-permute-done.26 = bf16[32,4096]{1,0:T(8,128)(2,1)S(1)} collective-permute-done((bf16[32,4096]{1,0:T(8,128)(2,1)S(1)}, bf16[32,4096]{1,0:T(8,128)(2,1)S(1)}, u32[]{:S(2)}, u32[]{:S(2)}) %collective-permute-start.26) | collective-permute-done | bytes 262176 | tf_op jit(solution)/shard_map/ppermute | solution.py:162
  83.8 1.2 collective-permute-done.27
  85.4 2.2 convolution_multiply_fusion.4
  87.5 1.1 constant_dynamic-update-slice_fusion.13
  90.0 0.9 constant_dynamic-update-slice_fusion.10
  90.9 3.6 %multiply_multiply_fusion = (f32[512,128]{1,0:T(8,128)S(1)}, f32[512,128]{1,0:T(8,128)S(1)}, bf16[512,128]{1,0:T(8,128)(2,1)S(1)}) fusion(f32[512,256]{1,0:T(8,128)} %convolution_multiply_fusion.4, bf16[512,4096]{1,0:T(8,128)(2,1)} %constant_dynamic-update-slice_fusion.10, bf16[1,128,4096]{2,1,0:T(8,128)(2,1)S(1)} %copy-done.9), kind=kOutput, calls=%fused_computation.65 | convolution fusion | flops 537788416 | bytes 6422528 | tf_op jit(solution)/shard_map/dot_general | solution.py:289
  94.4 1.2 multiply_convert_fusion
  95.7 4.5 %convolution_multiply_fusion = f32[128,4096]{1,0:T(8,128)S(1)} fusion(bf16[512,128]{1,0:T(8,128)(2,1)S(1)} %get-tuple-element.144, bf16[512,4096]{1,0:T(8,128)(2,1)} %constant_dynamic-update-slice_fusion.10), kind=kOutput, calls=%fused_computation.2 | convolution fusion | flops 537395200 | bytes 6422528 | tf_op jit(solution)/shard_map/dot_general | solution.py:296
  100.7 1.3 fusion.29
  102.0 1.3 convolution_convert_fusion
  103.3 0.9 fusion.43
  105.4 1.2 collective-permute-start.34
  106.6 1.1 dynamic-slice_convert_fusion
  107.7 0.9 dynamic-slice_convert_fusion.1
  108.6 3.5 %collective-permute-start.29 = (bf16[2048,256]{1,0:T(8,128)(2,1)}, bf16[2048,256]{1,0:T(8,128)(2,1)}, u32[]{:S(2)}, u32[]{:S(2)}) collective-permute-start(bf16[2048,256]{1,0:T(8,128)(2,1)} %dynamic-slice_convert_fusion), channel_id=1, source_target_pairs={{0,64},{64,0},{1,65},{65,1},{2,66},{66,2},{3,67},{67,3},{4,68},{68... | collective-permute-start | bytes 3145736 | tf_op jit(solution)/shard_map/ppermute | solution.py:162
  112.1 0.9 fusion.44
  114.2 0.8 collective-permute-done.33
  115.6 1.0 collective-permute-done.36
  116.7 1.6 fusion.40
  119.4 15.8 %collective-permute-done.34 = bf16[2,1152,256]{2,1,0:T(8,128)(2,1)S(1)} collective-permute-done((bf16[2,1152,256]{2,1,0:T(8,128)(2,1)S(1)}, bf16[2,1152,256]{2,1,0:T(8,128)(2,1)S(1)}, u32[]{:S(2)}, u32[]{:S(2)}) %collective-permute-start.34) | collective-permute-done | bytes 1179680 | tf_op jit(solution)/shard_map/ppermute | solution.py:162
  135.2 0.8 fusion.46
  136.7 1.7 collective-permute-start.37
  138.4 1.2 broadcast_select_fusion
  139.6 4.8 %collective-permute-done.39 = bf16[32,4096]{1,0:T(8,128)(2,1)} collective-permute-done((bf16[32,4096]{1,0:T(8,128)(2,1)}, bf16[32,4096]{1,0:T(8,128)(2,1)}, u32[]{:S(2)}, u32[]{:S(2)}) %collective-permute-start.39) | collective-permute-done | bytes 262176 | tf_op jit(solution)/shard_map/ppermute | solution.py:162
  145.0 8.5 %collective-permute-done.37 = bf16[32,4096]{1,0:T(8,128)(2,1)} collective-permute-done((bf16[32,4096]{1,0:T(8,128)(2,1)}, bf16[32,4096]{1,0:T(8,128)(2,1)}, u32[]{:S(2)}, u32[]{:S(2)}) %collective-permute-start.37) | collective-permute-done | bytes 262176 | tf_op jit(solution)/shard_map/ppermute | solution.py:162
  153.5 1.0 collective-permute-start.35
  154.5 1.6 fusion.23
  156.1 4.9 %collective-permute-done.35 = bf16[32,4096]{1,0:T(8,128)(2,1)S(1)} collective-permute-done((bf16[32,4096]{1,0:T(8,128)(2,1)S(1)}, bf16[32,4096]{1,0:T(8,128)(2,1)S(1)}, u32[]{:S(2)}, u32[]{:S(2)}) %collective-permute-start.35) | collective-permute-done | bytes 262176 | tf_op jit(solution)/shard_map/ppermute | solution.py:162
  161.2 1.5 maximum_maximum_fusion
  163.3 1.0 collective-permute-start.41
  164.3 2.2 fusion.41
  166.5 2.9 %fusion.42 = (bf16[2048,256]{1,0:T(8,128)(2,1)S(1)}, f32[2048,256]{1,0:T(8,128)}) fusion(bf16[2048,256]{1,0:T(8,128)(2,1)} %collective-permute-done.29, f32[4096,256]{1,0:T(8,128)S(1)} %copy-done.8, s32[]{:T(128)S(6)} %select_n.49), kind=kLoop, calls=%fused_computation.115 | loop fusion | flops 1572864 | bytes 6291460 | tf_op jit(solution)/shard_map/convert_element_type | solution.py:325
  169.3 56.5 %conditional.1 = (bf16[2048,256]{1,0:T(8,128)(2,1)}, bf16[64,4096]{1,0:T(8,128)(2,1)}) conditional(s32[]{:T(128)} %clamp.3, (bf16[2048,256]{1,0:T(8,128)(2,1)S(1)}, bf16[64,4096]{1,0:T(8,128)(2,1)S(1)}) %tuple.50, (bf16[2048,256]{1,0:T(8,128)(2,1)S(1)}, bf16[64,4096]{1,0:T(8,128)(2,1)S(1)}) %tuple.50, ...), branch_computations={%region_7.8_spmd, %region_8.9_spmd, %region_9.10_spmd, %region_10.... | conditional | bytes 6291552 | solution.py:322
  169.3 2.7 %collective-permute-start.10 = (bf16[2048,256]{1,0:T(8,128)(2,1)S(1)}, bf16[2048,256]{1,0:T(8,128)(2,1)}, u32[]{:S(2)}, u32[]{:S(2)}) collective-permute-start(bf16[2048,256]{1,0:T(8,128)(2,1)S(1)} %get-tuple-element.38), channel_id=1, source_target_pairs={{0,48},{1,49},{2,50},{3,51},{4,52},{5,53},{6,54},{7,55},{8,56},{9,... | collective-permute-start | bytes 3145736 | tf_op jit(solution)/shard_map/cond/branch_5_fun/ppermute | solution.py:215
  172.6 53.2 %collective-permute-done.11 = bf16[64,4096]{1,0:T(8,128)(2,1)} collective-permute-done((bf16[64,4096]{1,0:T(8,128)(2,1)S(1)}, bf16[64,4096]{1,0:T(8,128)(2,1)}, u32[]{:S(2)}, u32[]{:S(2)}) %collective-permute-start.11) | collective-permute-done | bytes 524320 | tf_op jit(solution)/shard_map/cond/branch_5_fun/ppermute | solution.py:215
  225.9 2.1 collective-permute-done.42
  227.9 2.0 fusion.7
  229.9 1.1 pad_maximum_fusion.3
  231.0 4.9 %all-to-all-start.1 = ((bf16[8,16,4096]{2,1,0:T(8,128)(2,1)}), bf16[8,16,4096]{2,1,0:T(8,128)(2,1)S(1)}, u32[]{:S(2)}, u32[]{:S(2)}) async-start(bf16[8,16,4096]{2,1,0:T(8,128)(2,1)} %pad_maximum_fusion.3), calls=%async_computation.2 | async-start | bytes 2097152 | tf_op jit(solution)/shard_map/all_to_all | solution.py:341
  236.0 11.9 %shard_map.171 = (bf16[2048,256]{1,0:T(8,128)(2,1)}, f32[2048,256]{1,0:T(8,128)}, f32[2048,256]{1,0:T(8,128)}, bf16[64,4096]{1,0:T(8,128)(2,1)}, f32[64,4096]{1,0:T(8,128)}, /*index=5*/f32[64,4096]{1,0:T(8,128)}) custom-call(s32[3]{0:T(128)S(1)} %copy-done.3, bf16[8,1152,256]{2,1,0:T(8,128)(2,1)} %all-gather.2.cloned.1.call-done.packed, ...), custom_call_target="tpu_custom_call" | custom-call | flops 16777216 | bytes 31457280 | tf_op jit(solution)/shard_map/pallas_call | solution.py:142
  247.8 5.6 %all-to-all-done.1 = bf16[8,16,4096]{2,1,0:T(8,128)(2,1)S(1)} async-done(((bf16[8,16,4096]{2,1,0:T(8,128)(2,1)}), bf16[8,16,4096]{2,1,0:T(8,128)(2,1)S(1)}, u32[]{:S(2)}, u32[]{:S(2)}) %all-to-all-start.1) | async-done | bytes 1048608 | tf_op jit(solution)/shard_map/all_to_all | solution.py:341
  253.4 0.8 convolution_convert_fusion.2
  254.5 0.9 fusion.4
  (115 shorter events, 14.7 us)
Async XLA Ops:
  7.2 9.4 %copy-start = (bf16[16,4096]{1,0:T(8,128)(2,1)S(1)}, bf16[16,4096]{1,0:T(8,128)(2,1)}, u32[]{:S(2)}) copy-start(bf16[16,4096]{1,0:T(8,128)(2,1)} %param.18) | copy-start | bytes 393220
  19.9 24.2 %all-to-all-start = ((bf16[8,16,4096]{2,1,0:T(8,128)(2,1)}), bf16[8,16,4096]{2,1,0:T(8,128)(2,1)S(1)}, u32[]{:S(2)}, u32[]{:S(2)}) async-start(bf16[8,16,4096]{2,1,0:T(8,128)(2,1)} %pad_maximum_fusion), calls=%async_computation | async-start | bytes 2097152 | tf_op jit(solution)/shard_map/all_to_all | solution.py:273
  26.9 64.0 %reduce-scatter.2.cloned.1.call-start = ((), (), s32[]{:S(2)}) async-start(), calls=%async_computation.3 | async-start | bytes 5898240 | tf_op jit(solution)/shard_map/reduce_scatter | solution.py:272
  35.3 200.6 %all-gather.2.cloned.1.call-start = ((), (), s32[]{:S(2)}) async-start(), calls=%async_computation.4 | async-start | bytes 5898240 | tf_op jit(solution)/shard_map/all_gather | solution.py:310
  44.2 14.9 %collective-permute-start.14 = (bf16[64,4096]{1,0:T(8,128)(2,1)S(1)}, bf16[64,4096]{1,0:T(8,128)(2,1)S(1)}, u32[]{:S(2)}, u32[]{:S(2)}) collective-permute-start(bf16[64,4096]{1,0:T(8,128)(2,1)S(1)} %get-tuple-element.136), channel_id=1, source_target_pairs={{0,4},{4,0},{1,5},{5,1},{2,6},{6,2},{3,7},{7,3},{8,12},{12,8},{9,1... | collective-permute-start | bytes 1572872 | tf_op jit(solution)/shard_map/ppermute | solution.py:162
  44.9 14.9 %collective-permute-start.15 = (bf16[64,4096]{1,0:T(8,128)(2,1)S(1)}, bf16[64,4096]{1,0:T(8,128)(2,1)S(1)}, u32[]{:S(2)}, u32[]{:S(2)}) collective-permute-start(bf16[64,4096]{1,0:T(8,128)(2,1)S(1)} %get-tuple-element.136), channel_id=1, source_target_pairs={{0,2},{2,0},{1,3},{3,1},{4,6},{6,4},{5,7},{7,5},{8,10},{10,8},{9,1... | collective-permute-start | bytes 1572872 | tf_op jit(solution)/shard_map/ppermute | solution.py:162
  46.8 13.3 %collective-permute-start.16 = (bf16[64,4096]{1,0:T(8,128)(2,1)S(1)}, bf16[64,4096]{1,0:T(8,128)(2,1)S(1)}, u32[]{:S(2)}, u32[]{:S(2)}) collective-permute-start(bf16[64,4096]{1,0:T(8,128)(2,1)S(1)} %get-tuple-element.136), channel_id=1, source_target_pairs={{0,1},{1,0},{2,3},{3,2},{4,5},{5,4},{6,7},{7,6},{8,9},{9,8},{10,11... | collective-permute-start | bytes 1572872 | tf_op jit(solution)/shard_map/ppermute | solution.py:162
  46.8 27.2 %collective-permute-start.22 = (bf16[64,4096]{1,0:T(8,128)(2,1)S(1)}, bf16[64,4096]{1,0:T(8,128)(2,1)S(1)}, u32[]{:S(2)}, u32[]{:S(2)}) collective-permute-start(bf16[64,4096]{1,0:T(8,128)(2,1)S(1)} %get-tuple-element.137), channel_id=1, source_target_pairs={{0,4},{4,0},{1,5},{5,1},{2,6},{6,2},{3,7},{7,3},{8,12},{12,8},{9,1... | collective-permute-start | bytes 1572872 | tf_op jit(solution)/shard_map/ppermute | solution.py:162
  48.2 25.7 %collective-permute-start.23 = (bf16[64,4096]{1,0:T(8,128)(2,1)S(1)}, bf16[64,4096]{1,0:T(8,128)(2,1)S(1)}, u32[]{:S(2)}, u32[]{:S(2)}) collective-permute-start(bf16[64,4096]{1,0:T(8,128)(2,1)S(1)} %get-tuple-element.137), channel_id=1, source_target_pairs={{0,2},{2,0},{1,3},{3,1},{4,6},{6,4},{5,7},{7,5},{8,10},{10,8},{9,1... | collective-permute-start | bytes 1572872 | tf_op jit(solution)/shard_map/ppermute | solution.py:162
  59.1 20.4 %collective-permute-start.24 = (bf16[64,4096]{1,0:T(8,128)(2,1)S(1)}, bf16[64,4096]{1,0:T(8,128)(2,1)S(1)}, u32[]{:S(2)}, u32[]{:S(2)}) collective-permute-start(bf16[64,4096]{1,0:T(8,128)(2,1)S(1)} %get-tuple-element.137), channel_id=1, source_target_pairs={{0,1},{1,0},{2,3},{3,2},{4,5},{5,4},{6,7},{7,6},{8,9},{9,8},{10,11... | collective-permute-start | bytes 1572872 | tf_op jit(solution)/shard_map/ppermute | solution.py:162
  59.8 2.7 %collective-permute-start.17 = (bf16[128,4096]{1,0:T(8,128)(2,1)S(1)}, bf16[128,4096]{1,0:T(8,128)(2,1)S(1)}, u32[]{:S(2)}, u32[]{:S(2)}) collective-permute-start(bf16[128,4096]{1,0:T(8,128)(2,1)S(1)} %pad_maximum_fusion.1), channel_id=1, source_target_pairs={{0,1},{1,0},{2,3},{3,2},{4,5},{5,4},{6,7},{7,6},{8,9},{9,8},{10,11... | collective-permute-start | bytes 3145736 | tf_op jit(solution)/shard_map/ppermute | solution.py:162
  60.1 13.2 %collective-permute-start.18 = (bf16[32,4096]{1,0:T(8,128)(2,1)S(1)}, bf16[32,4096]{1,0:T(8,128)(2,1)S(1)}, u32[]{:S(2)}, u32[]{:S(2)}) collective-permute-start(bf16[32,4096]{1,0:T(8,128)(2,1)S(1)} %slice.170), channel_id=1, source_target_pairs={{0,4},{4,0},{1,5},{5,1},{2,6},{6,2},{3,7},{7,3},{8,12},{12,8},{9,1... | collective-permute-start | bytes 786440 | tf_op jit(solution)/shard_map/ppermute | solution.py:162
  62.6 11.2 %collective-permute-start.19 = (bf16[32,4096]{1,0:T(8,128)(2,1)S(1)}, bf16[32,4096]{1,0:T(8,128)(2,1)S(1)}, u32[]{:S(2)}, u32[]{:S(2)}) collective-permute-start(bf16[32,4096]{1,0:T(8,128)(2,1)S(1)} %slice.171), channel_id=1, source_target_pairs={{0,2},{2,0},{1,3},{3,1},{4,6},{6,4},{5,7},{7,5},{8,10},{10,8},{9,1... | collective-permute-start | bytes 786440 | tf_op jit(solution)/shard_map/ppermute | solution.py:162
  73.8 11.5 %copy-start.6 = (bf16[1,4096,256]{2,1,0:T(8,128)(2,1)S(1)}, bf16[1,4096,256]{2,1,0:T(8,128)(2,1)}, u32[]{:S(2)}) copy-start(bf16[1,4096,256]{2,1,0:T(8,128)(2,1)} %param.23) | copy-start | bytes 6291460
  73.9 11.4 %collective-permute-start.20 = (bf16[64,4096]{1,0:T(8,128)(2,1)S(1)}, bf16[64,4096]{1,0:T(8,128)(2,1)S(1)}, u32[]{:S(2)}, u32[]{:S(2)}) collective-permute-start(bf16[64,4096]{1,0:T(8,128)(2,1)S(1)} %get-tuple-element.146), channel_id=1, source_target_pairs={{0,1},{1,0},{2,3},{3,2},{4,5},{5,4},{6,7},{7,6},{8,9},{9,8},{10,11... | collective-permute-start | bytes 1572872 | tf_op jit(solution)/shard_map/ppermute | solution.py:162
  74.9 12.6 %collective-permute-start.25 = (bf16[128,4096]{1,0:T(8,128)(2,1)S(1)}, bf16[128,4096]{1,0:T(8,128)(2,1)S(1)}, u32[]{:S(2)}, u32[]{:S(2)}) collective-permute-start(bf16[128,4096]{1,0:T(8,128)(2,1)S(1)} %pad_maximum_fusion.2), channel_id=1, source_target_pairs={{0,1},{1,0},{2,3},{3,2},{4,5},{5,4},{6,7},{7,6},{8,9},{9,8},{10,11... | collective-permute-start | bytes 3145736 | tf_op jit(solution)/shard_map/ppermute | solution.py:162
  75.5 8.3 %collective-permute-start.26 = (bf16[32,4096]{1,0:T(8,128)(2,1)S(1)}, bf16[32,4096]{1,0:T(8,128)(2,1)S(1)}, u32[]{:S(2)}, u32[]{:S(2)}) collective-permute-start(bf16[32,4096]{1,0:T(8,128)(2,1)S(1)} %slice.140), channel_id=1, source_target_pairs={{0,4},{4,0},{1,5},{5,1},{2,6},{6,2},{3,7},{7,3},{8,12},{12,8},{9,1... | collective-permute-start | bytes 786440 | tf_op jit(solution)/shard_map/ppermute | solution.py:162
  76.9 8.0 %collective-permute-start.27 = (bf16[32,4096]{1,0:T(8,128)(2,1)S(1)}, bf16[32,4096]{1,0:T(8,128)(2,1)S(1)}, u32[]{:S(2)}, u32[]{:S(2)}) collective-permute-start(bf16[32,4096]{1,0:T(8,128)(2,1)S(1)} %slice.141), channel_id=1, source_target_pairs={{0,2},{2,0},{1,3},{3,1},{4,6},{6,4},{5,7},{7,5},{8,10},{10,8},{9,1... | collective-permute-start | bytes 786440 | tf_op jit(solution)/shard_map/ppermute | solution.py:162
  85.0 5.0 %collective-permute-start.28 = (bf16[64,4096]{1,0:T(8,128)(2,1)S(1)}, bf16[64,4096]{1,0:T(8,128)(2,1)S(1)}, u32[]{:S(2)}, u32[]{:S(2)}) collective-permute-start(bf16[64,4096]{1,0:T(8,128)(2,1)S(1)} %pad_maximum_fusion.4), channel_id=1, source_target_pairs={{0,1},{1,0},{2,3},{3,2},{4,5},{5,4},{6,7},{7,6},{8,9},{9,8},{10,11... | collective-permute-start | bytes 1572872 | tf_op jit(solution)/shard_map/ppermute | solution.py:162
  85.3 3.2 %copy-start.12 = (bf16[512,4096]{1,0:T(8,128)(2,1)}, bf16[512,4096]{1,0:T(8,128)(2,1)S(1)}, u32[]{:S(2)}) copy-start(bf16[512,4096]{1,0:T(8,128)(2,1)S(1)} %constant_dynamic-update-slice_fusion.2) | copy-start | bytes 12582916
  85.3 5.5 %copy-start.9 = (bf16[1,128,4096]{2,1,0:T(8,128)(2,1)S(1)}, bf16[1,128,4096]{2,1,0:T(8,128)(2,1)}, u32[]{:S(2)}) copy-start(bf16[1,128,4096]{2,1,0:T(8,128)(2,1)} %param.24) | copy-start | bytes 3145732
  95.7 22.6 %copy-start.4 = (bf16[512,4096]{1,0:T(8,128)(2,1)}, bf16[512,4096]{1,0:T(8,128)(2,1)S(1)}, u32[]{:S(2)}) copy-start(bf16[512,4096]{1,0:T(8,128)(2,1)S(1)} %multiply_convert_fusion) | copy-start | bytes 12582916
  95.7 5.0 %copy-start.13 = (bf16[512,4096]{1,0:T(8,128)(2,1)S(1)}, bf16[512,4096]{1,0:T(8,128)(2,1)}, u32[]{:S(2)}) copy-start(bf16[512,4096]{1,0:T(8,128)(2,1)} %copy-done.12) | copy-start | bytes 12582916
  100.2 7.5 %copy-start.10 = (f32[128,4096]{1,0:T(8,128)}, f32[128,4096]{1,0:T(8,128)S(1)}, u32[]{:S(2)}) copy-start(f32[128,4096]{1,0:T(8,128)S(1)} %convolution_multiply_fusion) | copy-start | bytes 6291460
  102.0 4.7 %copy-start.7 = (f32[4096,256]{1,0:T(8,128)}, f32[4096,256]{1,0:T(8,128)S(1)}, u32[]{:S(2)}) copy-start(f32[4096,256]{1,0:T(8,128)S(1)} %fusion.29) | copy-start | bytes 12582916
  103.3 13.4 %copy-start.5 = (bf16[512,4096]{1,0:T(8,128)(2,1)}, bf16[512,4096]{1,0:T(8,128)(2,1)S(1)}, u32[]{:S(2)}) copy-start(bf16[512,4096]{1,0:T(8,128)(2,1)S(1)} %convolution_convert_fusion) | copy-start | bytes 12582916
  103.3 2.1 copy-start.14
  104.2 121.6 %collective-permute-start.21 = (bf16[64,4096]{1,0:T(8,128)(2,1)}, bf16[64,4096]{1,0:T(8,128)(2,1)}, u32[]{:S(2)}, u32[]{:S(2)}) collective-permute-start(bf16[64,4096]{1,0:T(8,128)(2,1)} %get-tuple-element.120), channel_id=1, source_target_pairs={{0,1},{1,0},{2,3},{3,2},{4,5},{5,4},{6,7},{7,6},{8,9},{9,8},{10,11... | collective-permute-start | bytes 1572872 | tf_op jit(solution)/shard_map/ppermute | solution.py:162
  105.4 29.9 %collective-permute-start.34 = (bf16[2,1152,256]{2,1,0:T(8,128)(2,1)S(1)}, bf16[2,1152,256]{2,1,0:T(8,128)(2,1)S(1)}, u32[]{:S(2)}, u32[]{:S(2)}) collective-permute-start(bf16[2,1152,256]{2,1,0:T(8,128)(2,1)S(1)} %copy-done.14), channel_id=1, source_target_pairs={{0,8},{8,0},{1,9},{9,1},{2,10},{10,2},{3,11},{11,3},{4,12},{12,4},... | collective-permute-start | bytes 3538952 | tf_op jit(solution)/shard_map/ppermute | solution.py:162
  108.6 54.1 %collective-permute-start.29 = (bf16[2048,256]{1,0:T(8,128)(2,1)}, bf16[2048,256]{1,0:T(8,128)(2,1)}, u32[]{:S(2)}, u32[]{:S(2)}) collective-permute-start(bf16[2048,256]{1,0:T(8,128)(2,1)} %dynamic-slice_convert_fusion), channel_id=1, source_target_pairs={{0,64},{64,0},{1,65},{65,1},{2,66},{66,2},{3,67},{67,3},{4,68},{68... | collective-permute-start | bytes 3145736 | tf_op jit(solution)/shard_map/ppermute | solution.py:162
  112.1 1.9 collective-permute-start.32
  113.0 2.0 collective-permute-start.33
  114.0 2.7 %collective-permute-start.36 = (bf16[128,4096]{1,0:T(8,128)(2,1)S(1)}, bf16[128,4096]{1,0:T(8,128)(2,1)S(1)}, u32[]{:S(2)}, u32[]{:S(2)}) collective-permute-start(bf16[128,4096]{1,0:T(8,128)(2,1)S(1)} %slice.184), channel_id=1, source_target_pairs={{0,1},{1,0},{2,3},{3,2},{4,5},{5,4},{6,7},{7,6},{8,9},{9,8},{10,11... | collective-permute-start | bytes 3145736 | tf_op jit(solution)/shard_map/ppermute | solution.py:162
  115.1 3.2 %collective-permute-start.31 = (bf16[128,4096]{1,0:T(8,128)(2,1)S(1)}, bf16[128,4096]{1,0:T(8,128)(2,1)S(1)}, u32[]{:S(2)}, u32[]{:S(2)}) collective-permute-start(bf16[128,4096]{1,0:T(8,128)(2,1)S(1)} %slice.176), channel_id=1, source_target_pairs={{0,1},{1,0},{2,3},{3,2},{4,5},{5,4},{6,7},{7,6},{8,9},{9,8},{10,11... | collective-permute-start | bytes 3145736 | tf_op jit(solution)/shard_map/ppermute | solution.py:162
  116.6 46.0 %collective-permute-start.30 = (bf16[64,4096]{1,0:T(8,128)(2,1)}, bf16[64,4096]{1,0:T(8,128)(2,1)}, u32[]{:S(2)}, u32[]{:S(2)}) collective-permute-start(bf16[64,4096]{1,0:T(8,128)(2,1)} %dynamic-slice_convert_fusion.1), channel_id=1, source_target_pairs={{0,64},{64,0},{1,65},{65,1},{2,66},{66,2},{3,67},{67,3},{4,68},{68... | collective-permute-start | bytes 1572872 | tf_op jit(solution)/shard_map/ppermute | solution.py:162
  136.1 8.3 %collective-permute-start.39 = (bf16[32,4096]{1,0:T(8,128)(2,1)}, bf16[32,4096]{1,0:T(8,128)(2,1)}, u32[]{:S(2)}, u32[]{:S(2)}) collective-permute-start(bf16[32,4096]{1,0:T(8,128)(2,1)} %get-tuple-element.142), channel_id=1, source_target_pairs={{0,4},{4,0},{1,5},{5,1},{2,6},{6,2},{3,7},{7,3},{8,12},{12,8},{9,1... | collective-permute-start | bytes 786440 | tf_op jit(solution)/shard_map/ppermute | solution.py:162
  136.7 16.8 %collective-permute-start.37 = (bf16[32,4096]{1,0:T(8,128)(2,1)}, bf16[32,4096]{1,0:T(8,128)(2,1)}, u32[]{:S(2)}, u32[]{:S(2)}) collective-permute-start(bf16[32,4096]{1,0:T(8,128)(2,1)} %get-tuple-element.143), channel_id=1, source_target_pairs={{0,2},{2,0},{1,3},{3,1},{4,6},{6,4},{5,7},{7,5},{8,10},{10,8},{9,1... | collective-permute-start | bytes 786440 | tf_op jit(solution)/shard_map/ppermute | solution.py:162
  139.6 21.6 %copy-start.15 = (bf16[1,32,4096]{2,1,0:T(8,128)(2,1)S(1)}, bf16[1,32,4096]{2,1,0:T(8,128)(2,1)}, u32[]{:S(2)}) copy-start(bf16[1,32,4096]{2,1,0:T(8,128)(2,1)} %get-tuple-element.131) | copy-start | bytes 786436
  144.4 11.7 %collective-permute-start.38 = (bf16[32,4096]{1,0:T(8,128)(2,1)S(1)}, bf16[32,4096]{1,0:T(8,128)(2,1)S(1)}, u32[]{:S(2)}, u32[]{:S(2)}) collective-permute-start(bf16[32,4096]{1,0:T(8,128)(2,1)S(1)} %get-tuple-element.140), channel_id=1, source_target_pairs={{0,4},{4,0},{1,5},{5,1},{2,6},{6,2},{3,7},{7,3},{8,12},{12,8},{9,1... | collective-permute-start | bytes 786440 | tf_op jit(solution)/shard_map/ppermute | solution.py:162
  153.5 7.6 %collective-permute-start.35 = (bf16[32,4096]{1,0:T(8,128)(2,1)S(1)}, bf16[32,4096]{1,0:T(8,128)(2,1)S(1)}, u32[]{:S(2)}, u32[]{:S(2)}) collective-permute-start(bf16[32,4096]{1,0:T(8,128)(2,1)S(1)} %get-tuple-element.141), channel_id=1, source_target_pairs={{0,2},{2,0},{1,3},{3,1},{4,6},{6,4},{5,7},{7,5},{8,10},{10,8},{9,1... | collective-permute-start | bytes 786440 | tf_op jit(solution)/shard_map/ppermute | solution.py:162
  154.5 9.8 %copy-start.11 = (f32[128,4096]{1,0:T(8,128)S(1)}, f32[128,4096]{1,0:T(8,128)}, u32[]{:S(2)}) copy-start(f32[128,4096]{1,0:T(8,128)} %copy-done.10) | copy-start | bytes 6291460
  161.2 5.3 %copy-start.8 = (f32[4096,256]{1,0:T(8,128)S(1)}, f32[4096,256]{1,0:T(8,128)}, u32[]{:S(2)}) copy-start(f32[4096,256]{1,0:T(8,128)} %copy-done.7) | copy-start | bytes 12582916
  162.6 63.2 %collective-permute-start.40 = (bf16[2,64,4096]{2,1,0:T(8,128)(2,1)}, bf16[2,64,4096]{2,1,0:T(8,128)(2,1)S(1)}, u32[]{:S(2)}, u32[]{:S(2)}) collective-permute-start(bf16[2,64,4096]{2,1,0:T(8,128)(2,1)} %get-tuple-element.90), channel_id=1, source_target_pairs={{0,4},{4,0},{1,5},{5,1},{2,6},{6,2},{3,7},{7,3},{8,12},{12,8},{9,1... | collective-permute-start | bytes 3145736 | tf_op jit(solution)/shard_map/ppermute | solution.py:162
  163.3 62.5 %collective-permute-start.41 = (bf16[2,64,4096]{2,1,0:T(8,128)(2,1)}, bf16[2,64,4096]{2,1,0:T(8,128)(2,1)S(1)}, u32[]{:S(2)}, u32[]{:S(2)}) collective-permute-start(bf16[2,64,4096]{2,1,0:T(8,128)(2,1)} %get-tuple-element.91), channel_id=1, source_target_pairs={{0,2},{2,0},{1,3},{3,1},{4,6},{6,4},{5,7},{7,5},{8,10},{10,8},{9,1... | collective-permute-start | bytes 3145736 | tf_op jit(solution)/shard_map/ppermute | solution.py:162
  169.3 56.5 %collective-permute-start.10 = (bf16[2048,256]{1,0:T(8,128)(2,1)S(1)}, bf16[2048,256]{1,0:T(8,128)(2,1)}, u32[]{:S(2)}, u32[]{:S(2)}) collective-permute-start(bf16[2048,256]{1,0:T(8,128)(2,1)S(1)} %get-tuple-element.38), channel_id=1, source_target_pairs={{0,48},{1,49},{2,50},{3,51},{4,52},{5,53},{6,54},{7,55},{8,56},{9,... | collective-permute-start | bytes 3145736 | tf_op jit(solution)/shard_map/cond/branch_5_fun/ppermute | solution.py:215
  172.0 53.8 %collective-permute-start.11 = (bf16[64,4096]{1,0:T(8,128)(2,1)S(1)}, bf16[64,4096]{1,0:T(8,128)(2,1)}, u32[]{:S(2)}, u32[]{:S(2)}) collective-permute-start(bf16[64,4096]{1,0:T(8,128)(2,1)S(1)} %get-tuple-element.39), channel_id=1, source_target_pairs={{0,48},{1,49},{2,50},{3,51},{4,52},{5,53},{6,54},{7,55},{8,56},{9,... | collective-permute-start | bytes 1572872 | tf_op jit(solution)/shard_map/cond/branch_5_fun/ppermute | solution.py:215
  225.8 2.1 collective-permute-start.42
  225.8 10.1 %copy-start.16 = (f32[16,2]{0,1:T(2,128)S(1)}, f32[16,2]{0,1:T(2,128)}, u32[]{:S(2)}) copy-start(f32[16,2]{0,1:T(2,128)} %param.21) | copy-start | bytes 388
  225.8 10.1 %copy-start.2 = (f32[1,64,4096]{2,1,0:T(8,128)S(1)}, f32[1,64,4096]{2,1,0:T(8,128)}, u32[]{:S(2)}) copy-start(f32[1,64,4096]{2,1,0:T(8,128)} %param.27) | copy-start | bytes 3145732
  225.8 10.1 %copy-start.3 = (s32[3]{0:T(128)S(1)}, s32[3]{0:T(128)}, u32[]{:S(2)}) copy-start(s32[3]{0:T(128)} %pad_add_fusion.at) | copy-start | bytes 40
  231.0 22.4 %all-to-all-start.1 = ((bf16[8,16,4096]{2,1,0:T(8,128)(2,1)}), bf16[8,16,4096]{2,1,0:T(8,128)(2,1)S(1)}, u32[]{:S(2)}, u32[]{:S(2)}) async-start(bf16[8,16,4096]{2,1,0:T(8,128)(2,1)} %pad_maximum_fusion.3), calls=%async_computation.2 | async-start | bytes 2097152 | tf_op jit(solution)/shard_map/all_to_all | solution.py:341
  235.9 19.4 %copy-start.1 = (bf16[16,4096]{1,0:T(8,128)(2,1)S(1)}, bf16[16,4096]{1,0:T(8,128)(2,1)}, u32[]{:S(2)}) copy-start(bf16[16,4096]{1,0:T(8,128)(2,1)} %param.18) | copy-start | bytes 393220
Sparse Core Ops, SparseCore 0:
  35.4 53.7 reduce-scatter.1
  139.7 72.7 all-gather.1
